TPU v7x, 32 devices: a whole 2x2x4 slice. The times are simulated.
32 devices in a mesh: row: 4 (over y, core), col: 8 (over z, x).
Axes of the slice: x: 2, y: 2, z: 4, core: 2. Of those that a mesh axis runs over, the one named last changes fastest.
Arguments:
- reversed_rows: float32 [4, 4, 256, 2, 8, 256], P(None, 'row', None, None, 'col'), may hold values from -0.375 to 0.375
- state: float32 [4, 4, 256, 2, 8, 256], P(None, 'row', None, None, 'col'), may hold values from -6 to 6
- basis: float32 [4, 4, 256, 256], P(None, 'row'), may hold values from -1 to 2
- eigval: float32 [4, 4, 256], P(None, 'row'), may hold values from -4 to -0.5
Outputs:
- updated: float32 [4, 4, 256, 2, 8, 256], P(None, 'row', None, None, 'col')
All inputs are finite; a program needn't handle non-finite values.
Results may differ from a plain program's by a relative error of at most 0.00013.
Values sent between devices are 32-bit elements; how exact they have to be, the bound alone decides.
No kernel may reach another device: no remote copies, remote signals or barrier semaphores. Data moves between devices by JAX's collectives and lax.ppermute only.
A program may use at most 64 MiB of HBM per device.

v0:
```python
import jax
import jax.numpy as jnp
from jax import lax
from jax.sharding import PartitionSpec as P

BR = 4


def passed_along(shard, axis, by):
    size = lax.axis_size(axis)
    return lax.ppermute(shard, axis, [(i, (i + by) % size) for i in range(size)])


def from_partner(block, axis, bit):
    count = lax.axis_size(axis)
    route = []
    for low in range(count):
        high = low | 1 << bit
        if high != low and high < count:
            route += [(low, high), (high, low)]
    return lax.ppermute(block, axis, route)


def broadcast(block, axis, holder):
    block = jnp.where(lax.axis_index(axis) == holder, block, jnp.zeros_like(block))
    return lax.psum(block, axis)


def batched(einsum_form, first, second):
    return jnp.einsum(
        einsum_form,
        first,
        second,
        precision=lax.Precision.HIGHEST,
        preferred_element_type=jnp.float32,
    )


def shift_rows(pieces, offset):
    return passed_along(pieces, "row", offset)


def flip_rows(pieces):
    for bit_number in range(lax.axis_size("row").bit_length() - 1):
        pieces = from_partner((pieces[0], pieces[1]), "row", bit_number)
    return tuple((member[::-1] for member in pieces))


def next_rows(pieces):
    moved_data = shift_rows(pieces, 1)
    first_row = lax.axis_index("row") == 0
    return tuple(
        (
            jnp.where(
                first_row,
                jnp.concatenate([jnp.zeros_like(member[:1]), member[:-1]], axis=0),
                member,
            )
            for member in moved_data
        )
    )


def mirror_slots(slot_data, second_step):
    if second_step:
        moved_data = passed_along(slot_data, "col", -1)
        last_column = lax.axis_index("col") == lax.axis_size("col") - 1
        rolled = jnp.concatenate([moved_data[1:], jnp.zeros_like(moved_data[:1])], axis=0)
        slot_data = jnp.where(last_column, rolled, moved_data)
        slot_data = shift_rows(slot_data, -1)
    joint_bits = (lax.axis_size("row") * lax.axis_size("col")).bit_length() - 1
    for bit_number in range(joint_bits):
        slot_data = from_partner(slot_data, ("row", "col"), bit_number)
    return slot_data[::-1]


def take_slots(running, local_rows):
    return jnp.stack(
        [
            lax.dynamic_index_in_dim(
                running[:, :, column, :], local_rows[column], 0, keepdims=False
            )
            for column in range(running.shape[2])
        ]
    )


def solve_slots(right_side, row_basis, column_basis, row_values, column_values):
    inner_part = batched("sba,sbc->sac", row_basis, right_side)
    inner_part = batched("sac,scd->sad", inner_part, column_basis)
    inner_part = inner_part / (row_values[:, :, None] + column_values[:, None, :])
    outer_part = batched("sab,sbc->sac", row_basis, inner_part)
    return batched("sac,sdc->sad", outer_part, column_basis)


def local(reversed_rows, state, basis, eigval):
    row_count = lax.axis_size("row")
    col_count = lax.axis_size("col")
    row_pos = lax.axis_index("row")
    col_pos = lax.axis_index("col")
    local_cols = state.shape[3]
    block_width = state.shape[2]
    block_count = BR * row_count
    running = state.reshape(BR, block_width, local_cols, block_width)
    row_panel = reversed_rows.reshape(BR, block_width, local_cols, block_width)
    own_basis = basis.reshape(BR, block_width, block_width)
    own_values = eigval.reshape(BR, block_width)
    far_basis, far_values = flip_rows((own_basis, own_values))
    global_rows = jnp.arange(BR, dtype=jnp.int32) * row_count + row_pos
    global_cols = jnp.arange(local_cols, dtype=jnp.int32) * col_count + col_pos
    results = []
    pending = None
    for step_number in range(2):
        diagonal = block_count - 1 + step_number
        if step_number == 1:
            row_panel, far_basis, far_values = next_rows((row_panel, far_basis, far_values))
        slot_rows = diagonal - global_cols
        active = (
            (slot_rows >= 0)
            & (slot_rows < block_count)
            & (jnp.mod(slot_rows, row_count) == row_pos)
        )
        local_rows = jnp.clip(slot_rows // row_count, 0, BR - 1)
        is_upper = slot_rows <= global_cols
        slot_blocks = take_slots(running, local_rows)
        mirrored = mirror_slots(slot_blocks, step_number == 1)
        right_side = slot_blocks + jnp.swapaxes(mirrored, 1, 2)
        solution = solve_slots(
            right_side,
            own_basis[local_rows],
            far_basis[local_rows],
            own_values[local_rows],
            far_values[local_rows],
        )
        solution = jnp.where((active & is_upper)[:, None, None], solution, 0.0)
        returned = mirror_slots(solution, step_number == 1)
        solution = jnp.where(is_upper[:, None, None], solution, jnp.swapaxes(returned, 1, 2))
        solution = jnp.where(active[:, None, None], solution, 0.0)
        results.append((local_rows, active, solution))
        partners = diagonal - global_rows
        present = (partners >= 0) & (partners < block_count)
        received = []
        for local_index in range(BR):
            target = partners[local_index]
            block_piece = lax.dynamic_index_in_dim(
                solution, jnp.clip(target // col_count, 0, local_cols - 1), 0, keepdims=False
            )
            received.append(broadcast(block_piece, "col", jnp.mod(target, col_count)))
        received = jnp.where(present[:, None, None], jnp.stack(received), 0.0)
        reaches = (global_cols[None, :] > partners[:, None]) & present[:, None]
        changes = batched("rab,rbcd->racd", received, row_panel)
        running = running - jnp.where(reaches[:, None, :, None], changes, 0.0)
    for local_rows, active, solution in results:
        for column in range(local_cols):
            current = running[:, :, column, :]
            existing = lax.dynamic_index_in_dim(current, local_rows[column], 0, keepdims=False)
            chosen = jnp.where(active[column], solution[column], existing)
            current = lax.dynamic_update_index_in_dim(current, chosen, local_rows[column], 0)
            running = running.at[:, :, column, :].set(current)
    return running.reshape(state.shape)


def solution(mesh):
    placed = (
        P(None, "row", None, None, "col", None),
        P(None, "row", None, None, "col", None),
        P(None, "row", None, None),
        P(None, "row", None),
    )
    return jax.shard_map(
        local,
        mesh=mesh,
        in_specs=placed,
        out_specs=P(None, "row", None, None, "col", None),
        check_vma=False,
    )
```

profile of v0, /device:TPU:29, one launch (start us, length us, event | category | flops | bytes accessed | tf_op | source)
XLA Modules:
  0.0 556.1 jit_solution(13281320260411839543)
XLA Ops:
  9.6 1.8 copy.46
  11.4 1.5 fusion.56
  18.6 10.6 %collective-permute-done = f32[2,256,256]{1,2,0:T(8,128)S(1)} collective-permute-done((f32[2,256,256]{1,2,0:T(8,128)S(1)}, f32[2,256,256]{1,2,0:T(8,128)S(1)}, u32[]{:S(2)}, u32[]{:S(2)}) %collective-permute-start) | collective-permute-done | bytes 524320 | tf_op jit(solution)/shard_map/ppermute | solution.py:21
  29.4 11.7 %collective-permute-done.1 = f32[2,256,256]{1,2,0:T(8,128)S(1)} collective-permute-done((f32[2,256,256]{1,2,0:T(8,128)S(1)}, f32[2,256,256]{1,2,0:T(8,128)S(1)}, u32[]{:S(2)}, u32[]{:S(2)}) %collective-permute-start.1) | collective-permute-done | bytes 524320 | tf_op jit(solution)/shard_map/ppermute | solution.py:21
  41.4 25.6 %collective-permute-done.2 = f32[2,256,256]{1,2,0:T(8,128)S(1)} collective-permute-done((f32[2,256,256]{1,2,0:T(8,128)S(1)}, f32[2,256,256]{1,2,0:T(8,128)S(1)}, u32[]{:S(2)}, u32[]{:S(2)}) %collective-permute-start.2) | collective-permute-done | bytes 524320 | tf_op jit(solution)/shard_map/ppermute | solution.py:21
  67.5 1.7 collective-permute-done.3
  73.3 9.4 %collective-permute-done.8 = f32[4,256]{1,0:T(4,128)S(1)} collective-permute-done((f32[4,256]{1,0:T(4,128)S(1)}, f32[4,256]{1,0:T(4,128)S(1)}, u32[]{:S(2)}, u32[]{:S(2)}) %collective-permute-start.8) | collective-permute-done | bytes 4128 | tf_op jit(solution)/shard_map/ppermute | solution.py:21
  83.3 1.3 rev.19
  89.6 1.3 collective-permute-start.9
  90.9 11.0 %collective-permute-done.9 = f32[2,256,256]{1,2,0:T(8,128)S(1)} collective-permute-done((f32[2,256,256]{1,2,0:T(8,128)S(1)}, f32[2,256,256]{1,2,0:T(8,128)S(1)}, u32[]{:S(2)}, u32[]{:S(2)}) %collective-permute-start.9) | collective-permute-done | bytes 524320 | tf_op jit(solution)/shard_map/ppermute | solution.py:21
  101.9 11.3 %collective-permute-done.10 = f32[2,256,256]{1,2,0:T(8,128)S(1)} collective-permute-done((f32[2,256,256]{1,2,0:T(8,128)S(1)}, f32[2,256,256]{1,2,0:T(8,128)S(1)}, u32[]{:S(2)}, u32[]{:S(2)}) %collective-permute-start.10) | collective-permute-done | bytes 524320 | tf_op jit(solution)/shard_map/ppermute | solution.py:21
  113.2 26.0 %collective-permute-done.11 = f32[2,256,256]{1,2,0:T(8,128)S(1)} collective-permute-done((f32[2,256,256]{1,2,0:T(8,128)S(1)}, f32[2,256,256]{1,2,0:T(8,128)S(1)}, u32[]{:S(2)}, u32[]{:S(2)}) %collective-permute-start.11) | collective-permute-done | bytes 524320 | tf_op jit(solution)/shard_map/ppermute | solution.py:21
  139.7 1.5 collective-permute-done.12
  152.5 1.9 collective-permute-done.13
  158.9 2.4 copy.45
  162.8 71.0 %all-reduce.12.cloned.1.call-done = (f32[1,256,256]{2,1,0:T(8,128)}, f32[1,256,256]{2,1,0:T(8,128)}, f32[1,256,256]{2,1,0:T(8,128)}, f32[1,256,256]{2,1,0:T(8,128)}) async-done(((f32[1,256,256]{2,1,0:T(8,128)}, f32[1,256,256]{2,1,0:T(8,128)}, f32[1,256,256]{2,1,0:T(8,128)}, f32[1,256,256]{2,1,0:T(8,128)}), (f32[1,256,256]{2,1,0:T(8,128)}, f32[1,256,256]{2,1,0:T(8,128)}, f32[1,256,256]{2,1,0:T(8,128)}, ...) | async-done | bytes 1048592 | tf_op jit(solution)/shard_map/psum | solution.py:26
  233.8 4.6 select_subtract_fusion.1
  240.1 2.7 collective-permute-start.14
  242.8 10.8 %collective-permute-done.14 = f32[2,256,256]{2,1,0:T(8,128)S(1)} collective-permute-done((f32[2,256,256]{2,1,0:T(8,128)}, f32[2,256,256]{2,1,0:T(8,128)S(1)}, u32[]{:S(2)}, u32[]{:S(2)}) %collective-permute-start.14) | collective-permute-done | bytes 524320 | tf_op jit(solution)/shard_map/ppermute | solution.py:11
  254.5 1.8 copy.31
  258.6 1.7 collective-permute-start.15
  260.2 7.0 %collective-permute-done.15 = f32[2,256,256]{1,2,0:T(8,128)S(1)} collective-permute-done((f32[2,256,256]{1,2,0:T(8,128)S(1)}, f32[2,256,256]{1,2,0:T(8,128)S(1)}, u32[]{:S(2)}, u32[]{:S(2)}) %collective-permute-start.15) | collective-permute-done | bytes 524320 | tf_op jit(solution)/shard_map/ppermute | solution.py:11
  267.3 3.2 collective-permute-start.16
  270.5 12.2 %collective-permute-done.16 = f32[2,256,256]{1,2,0:T(8,128)S(1)} collective-permute-done((f32[2,256,256]{1,2,0:T(8,128)S(1)}, f32[2,256,256]{1,2,0:T(8,128)S(1)}, u32[]{:S(2)}, u32[]{:S(2)}) %collective-permute-start.16) | collective-permute-done | bytes 524320 | tf_op jit(solution)/shard_map/ppermute | solution.py:21
  282.7 13.0 %collective-permute-done.17 = f32[2,256,256]{1,2,0:T(8,128)S(1)} collective-permute-done((f32[2,256,256]{1,2,0:T(8,128)S(1)}, f32[2,256,256]{1,2,0:T(8,128)S(1)}, u32[]{:S(2)}, u32[]{:S(2)}) %collective-permute-start.17) | collective-permute-done | bytes 524320 | tf_op jit(solution)/shard_map/ppermute | solution.py:21
  295.9 1.5 collective-permute-start.21
  297.5 24.1 %collective-permute-done.18 = f32[2,256,256]{1,2,0:T(8,128)S(1)} collective-permute-done((f32[2,256,256]{1,2,0:T(8,128)S(1)}, f32[2,256,256]{1,2,0:T(8,128)S(1)}, u32[]{:S(2)}, u32[]{:S(2)}) %collective-permute-start.18) | collective-permute-done | bytes 524320 | tf_op jit(solution)/shard_map/ppermute | solution.py:21
  324.6 1.8 gather_fusion.4
  328.8 2.4 pad_select_fusion.1
  331.1 2.6 gather_fusion.5
  333.7 3.4 collective-permute-done.20
  337.2 1.9 rev.22
  339.0 2.2 fusion.25
  344.3 12.4 %collective-permute-done.23 = f32[2,256,256]{1,2,0:T(8,128)S(1)} collective-permute-done((f32[2,256,256]{1,2,0:T(8,128)}, f32[2,256,256]{1,2,0:T(8,128)S(1)}, u32[]{:S(2)}, u32[]{:S(2)}) %collective-permute-start.23) | collective-permute-done | bytes 524320 | tf_op jit(solution)/shard_map/ppermute | solution.py:11
  356.8 2.2 collective-permute-start.24
  359.0 7.7 %collective-permute-done.24 = f32[2,256,256]{1,2,0:T(8,128)S(1)} collective-permute-done((f32[2,256,256]{1,2,0:T(8,128)S(1)}, f32[2,256,256]{1,2,0:T(8,128)S(1)}, u32[]{:S(2)}, u32[]{:S(2)}) %collective-permute-start.24) | collective-permute-done | bytes 524320 | tf_op jit(solution)/shard_map/ppermute | solution.py:11
  366.7 4.2 collective-permute-start.25
  370.8 11.4 %collective-permute-done.25 = f32[2,256,256]{1,2,0:T(8,128)S(1)} collective-permute-done((f32[2,256,256]{1,2,0:T(8,128)S(1)}, f32[2,256,256]{1,2,0:T(8,128)S(1)}, u32[]{:S(2)}, u32[]{:S(2)}) %collective-permute-start.25) | collective-permute-done | bytes 524320 | tf_op jit(solution)/shard_map/ppermute | solution.py:21
  382.2 13.7 %collective-permute-done.26 = f32[2,256,256]{1,2,0:T(8,128)S(1)} collective-permute-done((f32[2,256,256]{1,2,0:T(8,128)S(1)}, f32[2,256,256]{1,2,0:T(8,128)S(1)}, u32[]{:S(2)}, u32[]{:S(2)}) %collective-permute-start.26) | collective-permute-done | bytes 524320 | tf_op jit(solution)/shard_map/ppermute | solution.py:21
  395.9 25.9 %collective-permute-done.27 = f32[2,256,256]{1,2,0:T(8,128)S(1)} collective-permute-done((f32[2,256,256]{1,2,0:T(8,128)S(1)}, f32[2,256,256]{1,2,0:T(8,128)S(1)}, u32[]{:S(2)}, u32[]{:S(2)}) %collective-permute-start.27) | collective-permute-done | bytes 524320 | tf_op jit(solution)/shard_map/ppermute | solution.py:21
  422.6 1.3 collective-permute-done.28
  435.2 23.4 %collective-permute-done.29 = f32[2,256,256]{1,2,0:T(8,128)} collective-permute-done((f32[2,256,256]{1,2,0:T(8,128)}, f32[2,256,256]{1,2,0:T(8,128)}, u32[]{:S(2)}, u32[]{:S(2)}) %collective-permute-start.29) | collective-permute-done | bytes 524320 | tf_op jit(solution)/shard_map/ppermute | solution.py:21
  458.6 1.3 fusion.24
  462.2 1.9 slice.264
  464.2 4.0 pad_select_fusion
  468.2 70.0 %all-reduce.10.cloned.1.call-done = (f32[1,256,256]{2,1,0:T(8,128)}, f32[1,256,256]{2,1,0:T(8,128)}, f32[1,256,256]{2,1,0:T(8,128)}, f32[1,256,256]{2,1,0:T(8,128)}) async-done(((f32[1,256,256]{2,1,0:T(8,128)}, f32[1,256,256]{2,1,0:T(8,128)}, f32[1,256,256]{2,1,0:T(8,128)}, f32[1,256,256]{2,1,0:T(8,128)}), (f32[1,256,256]{2,1,0:T(8,128)}, f32[1,256,256]{2,1,0:T(8,128)}, f32[1,256,256]{2,1,0:T(8,128)}, ...) | async-done | bytes 1048592 | tf_op jit(solution)/shard_map/psum | solution.py:26
  538.1 4.0 select_subtract_fusion
  545.7 3.5 copy.26
  (123 shorter events, 40.2 us)
Async XLA Ops:
  6.5 227.2 %all-reduce.12.cloned.1.call-start = ((), (), s32[]{:S(2)}) async-start(), calls=%async_computation.1 | async-start | bytes 2097152 | tf_op jit(solution)/shard_map/psum | solution.py:26
  12.9 4.8 copy-start.6
  12.9 56.5 %copy-start.7 = (f32[4,1,256]{2,1,0:T(1,128)S(1)}, f32[4,1,256]{2,1,0:T(1,128)}, u32[]{:S(2)}) copy-start(f32[4,1,256]{2,1,0:T(1,128)} %param.15) | copy-start | bytes 12292
  16.4 12.9 %collective-permute-start = (f32[2,256,256]{1,2,0:T(8,128)S(1)}, f32[2,256,256]{1,2,0:T(8,128)S(1)}, u32[]{:S(2)}, u32[]{:S(2)}) collective-permute-start(f32[2,256,256]{1,2,0:T(8,128)S(1)} %copy.17), channel_id=1, source_target_pairs={{0,1},{1,0},{2,3},{3,2},{4,5},{5,4},{6,7},{7,6},{8,9},{9,8},{10,11... | collective-permute-start | bytes 1572872 | tf_op jit(solution)/shard_map/ppermute | solution.py:21
  17.7 23.5 %collective-permute-start.5 = (f32[4,256,256]{2,1,0:T(8,128)S(1)}, f32[4,256,256]{2,1,0:T(8,128)}, u32[]{:S(2)}, u32[]{:S(2)}) collective-permute-start(f32[4,256,256]{2,1,0:T(8,128)S(1)} %bitcast.115), channel_id=1, source_target_pairs={{0,8},{8,0},{16,24},{24,16},{1,9},{9,1},{17,25},{25,17},{2,10},{10... | collective-permute-start | bytes 3145736 | tf_op jit(solution)/shard_map/ppermute | solution.py:21
  29.3 11.9 %collective-permute-start.1 = (f32[2,256,256]{1,2,0:T(8,128)S(1)}, f32[2,256,256]{1,2,0:T(8,128)S(1)}, u32[]{:S(2)}, u32[]{:S(2)}) collective-permute-start(f32[2,256,256]{1,2,0:T(8,128)S(1)} %collective-permute-done), channel_id=1, source_target_pairs={{0,2},{2,0},{1,3},{3,1},{4,6},{6,4},{5,7},{7,5},{8,10},{10,8},{9,1... | collective-permute-start | bytes 1572872 | tf_op jit(solution)/shard_map/ppermute | solution.py:21
  41.1 25.9 %collective-permute-start.2 = (f32[2,256,256]{1,2,0:T(8,128)S(1)}, f32[2,256,256]{1,2,0:T(8,128)S(1)}, u32[]{:S(2)}, u32[]{:S(2)}) collective-permute-start(f32[2,256,256]{1,2,0:T(8,128)S(1)} %collective-permute-done.1), channel_id=1, source_target_pairs={{0,4},{4,0},{1,5},{5,1},{2,6},{6,2},{3,7},{7,3},{8,12},{12,8},{9,1... | collective-permute-start | bytes 1572872 | tf_op jit(solution)/shard_map/ppermute | solution.py:21
  41.2 42.1 %collective-permute-start.6 = (f32[4,256,256]{2,1,0:T(8,128)}, f32[4,256,256]{2,1,0:T(8,128)}, u32[]{:S(2)}, u32[]{:S(2)}) collective-permute-start(f32[4,256,256]{2,1,0:T(8,128)} %collective-permute-done.5), channel_id=1, source_target_pairs={{0,16},{16,0},{8,24},{24,8},{1,17},{17,1},{9,25},{25,9},{2,18},{18... | collective-permute-start | bytes 3145736 | tf_op jit(solution)/shard_map/ppermute | solution.py:21
  67.0 2.2 collective-permute-start.3
  69.2 16.1 %collective-permute-start.4 = (f32[2,256,256]{1,2,0:T(8,128)}, f32[2,256,256]{1,2,0:T(8,128)}, u32[]{:S(2)}, u32[]{:S(2)}) collective-permute-start(f32[2,256,256]{1,2,0:T(8,128)} %collective-permute-done.3), channel_id=1, source_target_pairs={{0,16},{16,0},{1,17},{17,1},{2,18},{18,2},{3,19},{19,3},{4,20},{20... | collective-permute-start | bytes 1572872 | tf_op jit(solution)/shard_map/ppermute | solution.py:21
  69.4 1.5 collective-permute-start.7
  70.9 11.8 %collective-permute-start.8 = (f32[4,256]{1,0:T(4,128)S(1)}, f32[4,256]{1,0:T(4,128)S(1)}, u32[]{:S(2)}, u32[]{:S(2)}) collective-permute-start(f32[4,256]{1,0:T(4,128)S(1)} %collective-permute-done.7), channel_id=1, source_target_pairs={{0,16},{16,0},{8,24},{24,8},{1,17},{17,1},{9,25},{25,9},{2,18},{18... | collective-permute-start | bytes 12296 | tf_op jit(solution)/shard_map/ppermute | solution.py:21
  84.6 2.7 copy-start.1
  89.6 12.3 %collective-permute-start.9 = (f32[2,256,256]{1,2,0:T(8,128)S(1)}, f32[2,256,256]{1,2,0:T(8,128)S(1)}, u32[]{:S(2)}, u32[]{:S(2)}) collective-permute-start(f32[2,256,256]{1,2,0:T(8,128)S(1)} %copy.18), channel_id=1, source_target_pairs={{0,1},{1,0},{2,3},{3,2},{4,5},{5,4},{6,7},{7,6},{8,9},{9,8},{10,11... | collective-permute-start | bytes 1572872 | tf_op jit(solution)/shard_map/ppermute | solution.py:21
  101.9 11.3 %collective-permute-start.10 = (f32[2,256,256]{1,2,0:T(8,128)S(1)}, f32[2,256,256]{1,2,0:T(8,128)S(1)}, u32[]{:S(2)}, u32[]{:S(2)}) collective-permute-start(f32[2,256,256]{1,2,0:T(8,128)S(1)} %collective-permute-done.9), channel_id=1, source_target_pairs={{0,2},{2,0},{1,3},{3,1},{4,6},{6,4},{5,7},{7,5},{8,10},{10,8},{9,1... | collective-permute-start | bytes 1572872 | tf_op jit(solution)/shard_map/ppermute | solution.py:21
  113.2 26.0 %collective-permute-start.11 = (f32[2,256,256]{1,2,0:T(8,128)S(1)}, f32[2,256,256]{1,2,0:T(8,128)S(1)}, u32[]{:S(2)}, u32[]{:S(2)}) collective-permute-start(f32[2,256,256]{1,2,0:T(8,128)S(1)} %collective-permute-done.10), channel_id=1, source_target_pairs={{0,4},{4,0},{1,5},{5,1},{2,6},{6,2},{3,7},{7,3},{8,12},{12,8},{9,1... | collective-permute-start | bytes 1572872 | tf_op jit(solution)/shard_map/ppermute | solution.py:21
  139.2 2.0 collective-permute-start.12
  141.3 13.1 %collective-permute-start.13 = (f32[2,256,256]{1,2,0:T(8,128)S(1)}, f32[2,256,256]{1,2,0:T(8,128)S(1)}, u32[]{:S(2)}, u32[]{:S(2)}) collective-permute-start(f32[2,256,256]{1,2,0:T(8,128)S(1)} %collective-permute-done.12), channel_id=1, source_target_pairs={{0,16},{16,0},{1,17},{17,1},{2,18},{18,2},{3,19},{19,3},{4,20},{20... | collective-permute-start | bytes 1572872 | tf_op jit(solution)/shard_map/ppermute | solution.py:21
  154.5 4.4 copy-start.3
  155.6 382.5 %all-reduce.10.cloned.1.call-start = ((), (), s32[]{:S(2)}) async-start(), calls=%async_computation | async-start | bytes 2097152 | tf_op jit(solution)/shard_map/psum | solution.py:26
  238.6 0.7 copy-start.2
  240.1 13.5 %collective-permute-start.14 = (f32[2,256,256]{2,1,0:T(8,128)}, f32[2,256,256]{2,1,0:T(8,128)S(1)}, u32[]{:S(2)}, u32[]{:S(2)}) collective-permute-start(f32[2,256,256]{2,1,0:T(8,128)} %pad_maximum_fusion.1), channel_id=1, source_target_pairs={{0,7},{1,0},{2,1},{3,2},{4,3},{5,4},{6,5},{7,6},{8,15},{9,8},{10,9... | collective-permute-start | bytes 1572872 | tf_op jit(solution)/shard_map/ppermute | solution.py:11
  253.6 0.9 copy-start.5
  258.6 8.7 %collective-permute-start.15 = (f32[2,256,256]{1,2,0:T(8,128)S(1)}, f32[2,256,256]{1,2,0:T(8,128)S(1)}, u32[]{:S(2)}, u32[]{:S(2)}) collective-permute-start(f32[2,256,256]{1,2,0:T(8,128)S(1)} %pad_select_fusion.2), channel_id=1, source_target_pairs={{0,24},{8,0},{16,8},{24,16},{1,25},{9,1},{17,9},{25,17},{2,26},{10... | collective-permute-start | bytes 1572872 | tf_op jit(solution)/shard_map/ppermute | solution.py:11
  267.3 15.4 %collective-permute-start.16 = (f32[2,256,256]{1,2,0:T(8,128)S(1)}, f32[2,256,256]{1,2,0:T(8,128)S(1)}, u32[]{:S(2)}, u32[]{:S(2)}) collective-permute-start(f32[2,256,256]{1,2,0:T(8,128)S(1)} %collective-permute-done.15), channel_id=1, source_target_pairs={{0,1},{1,0},{2,3},{3,2},{4,5},{5,4},{6,7},{7,6},{8,9},{9,8},{10,11... | collective-permute-start | bytes 1572872 | tf_op jit(solution)/shard_map/ppermute | solution.py:21
  282.7 13.1 %collective-permute-start.17 = (f32[2,256,256]{1,2,0:T(8,128)S(1)}, f32[2,256,256]{1,2,0:T(8,128)S(1)}, u32[]{:S(2)}, u32[]{:S(2)}) collective-permute-start(f32[2,256,256]{1,2,0:T(8,128)S(1)} %collective-permute-done.16), channel_id=1, source_target_pairs={{0,2},{2,0},{1,3},{3,1},{4,6},{6,4},{5,7},{7,5},{8,10},{10,8},{9,1... | collective-permute-start | bytes 1572872 | tf_op jit(solution)/shard_map/ppermute | solution.py:21
  295.8 25.8 %collective-permute-start.18 = (f32[2,256,256]{1,2,0:T(8,128)S(1)}, f32[2,256,256]{1,2,0:T(8,128)S(1)}, u32[]{:S(2)}, u32[]{:S(2)}) collective-permute-start(f32[2,256,256]{1,2,0:T(8,128)S(1)} %collective-permute-done.17), channel_id=1, source_target_pairs={{0,4},{4,0},{1,5},{5,1},{2,6},{6,2},{3,7},{7,3},{8,12},{12,8},{9,1... | collective-permute-start | bytes 1572872 | tf_op jit(solution)/shard_map/ppermute | solution.py:21
  295.9 31.6 %collective-permute-start.21 = (f32[4,256,256]{2,1,0:T(8,128)}, f32[4,256,256]{2,1,0:T(8,128)}, u32[]{:S(2)}, u32[]{:S(2)}) collective-permute-start(f32[4,256,256]{2,1,0:T(8,128)} %copy-done.1), channel_id=1, source_target_pairs={{0,8},{8,16},{16,24},{24,0},{1,9},{9,17},{17,25},{25,1},{2,10},{10... | collective-permute-start | bytes 3145736 | tf_op jit(solution)/shard_map/ppermute | solution.py:11
  321.6 2.2 collective-permute-start.19
  322.1 4.9 collective-permute-start.22
  323.7 13.5 %collective-permute-start.20 = (f32[2,256,256]{1,2,0:T(8,128)}, f32[2,256,256]{1,2,0:T(8,128)}, u32[]{:S(2)}, u32[]{:S(2)}) collective-permute-start(f32[2,256,256]{1,2,0:T(8,128)} %collective-permute-done.19), channel_id=1, source_target_pairs={{0,16},{16,0},{1,17},{17,1},{2,18},{18,2},{3,19},{19,3},{4,20},{20... | collective-permute-start | bytes 1572872 | tf_op jit(solution)/shard_map/ppermute | solution.py:21
  339.0 2.2 copy-start.4
  343.3 115.3 %copy-start = (f32[2,256,256]{2,1,0:T(8,128)}, f32[2,256,256]{2,1,0:T(8,128)S(1)}, u32[]{:S(2)}) copy-start(f32[2,256,256]{2,1,0:T(8,128)S(1)} %convolution_select_fusion) | copy-start | bytes 1572868
  344.3 12.4 %collective-permute-start.23 = (f32[2,256,256]{1,2,0:T(8,128)}, f32[2,256,256]{1,2,0:T(8,128)S(1)}, u32[]{:S(2)}, u32[]{:S(2)}) collective-permute-start(f32[2,256,256]{1,2,0:T(8,128)} %copy.22), channel_id=1, source_target_pairs={{0,7},{1,0},{2,1},{3,2},{4,3},{5,4},{6,5},{7,6},{8,15},{9,8},{10,9... | collective-permute-start | bytes 1572872 | tf_op jit(solution)/shard_map/ppermute | solution.py:11
  356.8 9.8 %collective-permute-start.24 = (f32[2,256,256]{1,2,0:T(8,128)S(1)}, f32[2,256,256]{1,2,0:T(8,128)S(1)}, u32[]{:S(2)}, u32[]{:S(2)}) collective-permute-start(f32[2,256,256]{1,2,0:T(8,128)S(1)} %pad_select_fusion.3), channel_id=1, source_target_pairs={{0,24},{8,0},{16,8},{24,16},{1,25},{9,1},{17,9},{25,17},{2,26},{10... | collective-permute-start | bytes 1572872 | tf_op jit(solution)/shard_map/ppermute | solution.py:11
  366.7 15.5 %collective-permute-start.25 = (f32[2,256,256]{1,2,0:T(8,128)S(1)}, f32[2,256,256]{1,2,0:T(8,128)S(1)}, u32[]{:S(2)}, u32[]{:S(2)}) collective-permute-start(f32[2,256,256]{1,2,0:T(8,128)S(1)} %collective-permute-done.24), channel_id=1, source_target_pairs={{0,1},{1,0},{2,3},{3,2},{4,5},{5,4},{6,7},{7,6},{8,9},{9,8},{10,11... | collective-permute-start | bytes 1572872 | tf_op jit(solution)/shard_map/ppermute | solution.py:21
  382.2 13.7 %collective-permute-start.26 = (f32[2,256,256]{1,2,0:T(8,128)S(1)}, f32[2,256,256]{1,2,0:T(8,128)S(1)}, u32[]{:S(2)}, u32[]{:S(2)}) collective-permute-start(f32[2,256,256]{1,2,0:T(8,128)S(1)} %collective-permute-done.25), channel_id=1, source_target_pairs={{0,2},{2,0},{1,3},{3,1},{4,6},{6,4},{5,7},{7,5},{8,10},{10,8},{9,1... | collective-permute-start | bytes 1572872 | tf_op jit(solution)/shard_map/ppermute | solution.py:21
  395.9 25.9 %collective-permute-start.27 = (f32[2,256,256]{1,2,0:T(8,128)S(1)}, f32[2,256,256]{1,2,0:T(8,128)S(1)}, u32[]{:S(2)}, u32[]{:S(2)}) collective-permute-start(f32[2,256,256]{1,2,0:T(8,128)S(1)} %collective-permute-done.26), channel_id=1, source_target_pairs={{0,4},{4,0},{1,5},{5,1},{2,6},{6,2},{3,7},{7,3},{8,12},{12,8},{9,1... | collective-permute-start | bytes 1572872 | tf_op jit(solution)/shard_map/ppermute | solution.py:21
  421.8 2.2 collective-permute-start.28
  422.2 40.0 %collective-permute-start.30 = (f32[4,256,2,256]{3,2,1,0:T(2,128)}, f32[4,256,2,256]{3,2,1,0:T(2,128)}, u32[]{:S(2)}, u32[]{:S(2)}) collective-permute-start(f32[4,256,2,256]{3,2,1,0:T(2,128)} %bitcast.113), channel_id=1, source_target_pairs={{0,8},{8,16},{16,24},{24,0},{1,9},{9,17},{17,25},{25,1},{2,10},{10... | collective-permute-start | bytes 6291464 | tf_op jit(solution)/shard_map/ppermute | solution.py:11
  423.9 34.7 %collective-permute-start.29 = (f32[2,256,256]{1,2,0:T(8,128)}, f32[2,256,256]{1,2,0:T(8,128)}, u32[]{:S(2)}, u32[]{:S(2)}) collective-permute-start(f32[2,256,256]{1,2,0:T(8,128)} %collective-permute-done.28), channel_id=1, source_target_pairs={{0,16},{16,0},{1,17},{17,1},{2,18},{18,2},{3,19},{19,3},{4,20},{20... | collective-permute-start | bytes 1572872 | tf_op jit(solution)/shard_map/ppermute | solution.py:21
Sparse Core Ops, SparseCore 0:
  155.7 78.0 all-reduce.11
  461.1 77.0 all-reduce.9
where the time goes:
time: 562 us; the launch traced here: 556 us
  waiting for transfers between devices  420 us (75%)
  between operations  42.1 us (7%)
  local copies, waits for them, and re-layouts  37.2 us (7%)
  starting transfers between devices  26.7 us (5%)
  matrix products  15.9 us (3%)
  other arithmetic  14.7 us (3%)
    ppermute x24, waiting for transfers between devices, from_partner(): return lax.ppermute(block, axis, route)  241 us
    psum x2, waiting for transfers between devices, broadcast(): return lax.psum(block, axis)  141 us
    ppermute x7, waiting for transfers between devices, passed_along(): lax.ppermute(shard, axis, [(i, (i + by) % size) for i in range(size)])  38 us
    ppermute x24, starting transfers between devices, from_partner(): return lax.ppermute(block, axis, route)  17.2 us
    dot_general x10, matrix products, batched(): jnp.einsum(einsum_form, first, second, precision=lax.Precision.HIGHEST, p...  15.9 us
  transfers between devices with their start and end apart: 33, of which 27 were waited for; matrix products, arithmetic and copies ran while one was open for 5% of the time, Pallas kernels for 0%

commit v1 on v0

v1 whole, which is shorter than its diff:
```python
import numpy as np
import jax
import jax.numpy as jnp
from jax import lax
from jax.sharding import PartitionSpec as P

AXES = ("row", "col")
PRECISION = lax.Precision.HIGH


def product(first, second):
    return jnp.dot(first, second, precision=PRECISION, preferred_element_type=jnp.float32)


class Plan:
    def __init__(self, rows, cols, block_rows, block_cols):
        self.rows, self.cols = rows, cols
        self.count = block_rows * rows
        assert block_rows == 4 and block_cols == 2 and self.count == block_cols * cols
        self.line = 4
        self.stride = cols // self.line

    def table(self, function):
        values = [[function(r, c) for c in range(self.cols)] for r in range(self.rows)]
        return np.asarray(values)

    def own_mirror(self, r):
        return r == (-r) % self.rows

    def keys(self, r):
        return [p * self.rows + r for p in range(4)]

    def place(self, k, d):
        m = d - k
        return (k % self.rows, m % self.cols), k // self.rows, m // self.cols

    def solver_first(self, k):
        r, p = k % self.rows, k // self.rows
        owner = (self.count - 1 - k) % self.cols
        if p < 2:
            return owner
        return (owner + (-self.stride if r < self.rows // 2 else self.stride)) % self.cols

    def solver_second(self, k):
        r, p = k % self.rows, k // self.rows
        if self.own_mirror(r):
            if k == 0 or k > self.count - k:
                return None
            return (self.count - k) % self.cols
        return (self.solver_first(k) + 1) % self.cols

    def solving(self, d):
        found = {}
        for k in range(self.count):
            c = self.solver_first(k) if d < self.count else self.solver_second(k)
            if c is not None:
                assert (k % self.rows, c) not in found
                found[(k % self.rows, c)] = k
        return found


def solution(mesh):
    rows, cols = mesh.shape["row"], mesh.shape["col"]
    plan = Plan(rows, cols, 4, 2)
    count, line, stride = plan.count, plan.line, plan.stride
    first, second = plan.solving(count - 1), plan.solving(count)

    def lookup(function):
        return jnp.asarray(plan.table(function))[lax.axis_index("row"), lax.axis_index("col")]

    def send(value, moves):
        pairs = [(s[0] * cols + s[1], t[0] * cols + t[1]) for s, t in moves]
        assert len({s for s, _ in pairs}) == len(pairs) == len({t for _, t in pairs})
        return lax.ppermute(value, AXES, pairs)

    def spread(block, sources, residue):
        got = [block]
        for t in range(1, line):
            got.append(send(block, [((r, c), (r, (c + t * stride) % cols)) for r, c in sources]))
        on_line = lookup(lambda r, c: c % stride == residue[r])
        result = []
        for t in range(line):
            total = got[t]
            out = total
            for step in range(1, stride):
                moves = []
                for r, c in sources:
                    at = (c + t * stride) % cols
                    moves.append(((r, at), (r, at // stride * stride + (at + step) % stride)))
                arrived = send(total, moves)
                mine = lookup(lambda r, c, step=step: c % stride == (residue[r] + step) % stride)
                out = jnp.where(mine, arrived, out)
            result.append(out)
        return jnp.stack(result)

    def local(reversed_rows, state, basis, eigval):
        width = state.shape[2]
        running = state.reshape(4, width, 2, width)
        panel = reversed_rows.reshape(4, width, 2, width)
        own_basis = basis.reshape(4, width, width)
        own_values = eigval.reshape(4, width)

        def block(array, index):
            found = lax.dynamic_slice(array, (index // 2, 0, index % 2, 0), (1, width, 1, width))
            return found.reshape(width, width)

        def slot(k, d):
            _, p, q = plan.place(k, d)
            return 2 * p + q

        def eigen(index):
            vectors = lax.dynamic_index_in_dim(own_basis, index, 0, keepdims=False)
            values = lax.dynamic_index_in_dim(own_values, index, 0, keepdims=True)
            return vectors, values

        def packed(index):
            vectors, values = eigen(index)
            return jnp.concatenate([vectors, jnp.broadcast_to(values, (8, width))], axis=0)

        def unpacked(message):
            return message[:width], message[width : width + 1]

        def gather(d, solving, pick):
            hand, mirrored = [], ([], [])
            hand_slot, mirror_slot = {}, ({}, {})
            for device, k in solving.items():
                owner, p, q = plan.place(k, d)
                if owner != device:
                    hand.append((owner, device))
                    hand_slot[owner] = 2 * p + q
                owner, p, q = plan.place(d - k, d)
                if owner != device:
                    mirrored[p // 2].append((owner, device))
                    mirror_slot[p // 2][owner] = 2 * p + q
            handed = send(pick(lookup(lambda r, c: hand_slot.get((r, c), 0))), hand)
            own = pick(
                lookup(lambda r, c: slot(first_or(solving, (r, c), d), d) if is_own(solving, (r, c), d) else 0)
            )
            own = jnp.where(lookup(lambda r, c: is_own(solving, (r, c), d)), own, handed)
            parts = []
            for side in range(2):
                parts.append(
                    send(pick(lookup(lambda r, c: mirror_slot[side].get((r, c), 0))), mirrored[side])
                )
            mirror = parts[0] + parts[1]

            def at_home(r, c):
                k = solving.get((r, c))
                return k is not None and plan.place(d - k, d)[0] == (r, c)

            if any(at_home(r, c) for r in range(rows) for c in range(cols)):
                near = pick(lookup(lambda r, c: slot(d - solving[(r, c)], d) if at_home(r, c) else 0))
                mirror = jnp.where(lookup(at_home), near, mirror)
            return own, mirror

        def first_or(solving, device, d):
            return solving[device]

        def is_own(solving, device, d):
            k = solving.get(device)
            return k is not None and plan.place(k, d)[0] == device

        def solve(right_side, near, far):
            inner = product(near[0].T, right_side)
            inner = product(inner, far[0])
            inner = inner / (near[1].reshape(width, 1) + far[1].reshape(1, width))
            return product(product(near[0], inner), far[0].T)

        far = send(
            packed(
                lookup(
                    lambda r, c: (count - 1 - first[(rows - 1 - r, c)]) // rows
                    if (rows - 1 - r, c) in first
                    else 0
                )
            ),
            [((rows - 1 - r, c), (r, c)) for r, c in first],
        )
        own, mirror = gather(count - 1, first, lambda index: block(running, index))

        def both(index):
            return jnp.stack([block(running, index), block(panel, index)])

        own_second, mirror_second = gather(count, second, both)
        crossing = [device for device in second if not plan.own_mirror(device[0])]

        def far_slot(r, c):
            k = second.get(((-r) % rows, c))
            return 0 if k is None else (count - k) // rows

        far_second = send(packed(lookup(far_slot)), [(((-r) % rows, c), (r, c)) for r, c in crossing])
        within = lookup(lambda r, c: plan.own_mirror(r))
        near_far = packed(lookup(far_slot))
        far_second = jnp.where(within, near_far, far_second)

        moved = send(panel, [((r, c), ((r + 1) % rows, c)) for r in range(rows) for c in range(cols)])
        rolled = jnp.concatenate([jnp.zeros_like(moved[:1]), moved[:-1]], axis=0)
        next_panel = jnp.where(lax.axis_index("row") == 0, rolled, moved)

        near = eigen(lookup(lambda r, c: first.get((r, c), 0) // rows))
        solved_first = solve(own + mirror.T, near, unpacked(far))

        def first_device(k):
            return (k % rows, plan.solver_first(k))

        direct = [(first_device(k), device) for device, k in second.items()]
        left = send(solved_first, direct)
        cross = [
            (first_device(count - k), device)
            for device, k in second.items()
            if plan.own_mirror(device[0]) and 2 * k != count
        ]
        right = send(solved_first, cross)
        halfway = lookup(lambda r, c: second.get((r, c), 0) * 2 == count)
        right = jnp.where(halfway, left, right).T
        beside = send(
            solved_first,
            [(first_device(k - 1), device) for device, k in second.items() if not plan.own_mirror(device[0])],
        )
        right = jnp.where(within, right, beside)
        change = product(left, own_second[1])
        change_mirror = product(mirror_second[1].T, right)
        right_side = own_second[0] - change + mirror_second[0].T - change_mirror
        near = eigen(lookup(lambda r, c: second.get((r, c), 0) // rows))
        solved_second = solve(right_side, near, unpacked(far_second))

        residue = [plan.solver_first(r) % stride for r in range(rows)]
        line_first = spread(solved_first, list(first), residue)
        residue_second = [next(c for q, c in second if q == r) % stride for r in range(rows)]
        line_second = spread(solved_second, list(second), residue_second)

        def shift_from(c, source):
            return (c // stride - source // stride) % line

        col = lax.axis_index("col")
        first_blocks, second_blocks = [], []
        for p in range(4):
            index = lookup(lambda r, c: shift_from(c, plan.solver_first(p * rows + r)))
            first_blocks.append(lax.dynamic_index_in_dim(line_first, index, 0, keepdims=False))

            def second_index(r, c):
                k = p * rows + r
                at = plan.solver_second(k)
                if at is None:
                    at = plan.solver_second(count - k) if k > 0 else c
                return shift_from(c, at)

            found = lax.dynamic_index_in_dim(
                line_second, lookup(second_index), 0, keepdims=False
            )
            turned = lookup(lambda r, c: plan.solver_second(p * rows + r) is None)
            second_blocks.append(jnp.where(turned, found.T, found))

        ids = jnp.arange(4, dtype=jnp.int32) * rows + lax.axis_index("row")
        columns = jnp.arange(2, dtype=jnp.int32) * cols + col
        for step, (blocks, rows_of_a) in enumerate(
            ((first_blocks, panel), (second_blocks, next_panel))
        ):
            partners = count - 1 + step - ids
            reaches = (columns[None, :] > partners[:, None]) & (partners < count)[:, None]
            changes = jnp.einsum(
                "rab,rbcd->racd",
                jnp.stack(blocks),
                rows_of_a,
                precision=PRECISION,
                preferred_element_type=jnp.float32,
            )
            running = running - jnp.where(reaches[:, None, :, None], changes, 0.0)
        for step, blocks in enumerate((first_blocks, second_blocks)):
            partners = count - 1 + step - ids
            placed = (columns[None, :] == partners[:, None])[:, None, :, None]
            running = jnp.where(placed, jnp.stack(blocks)[:, :, None, :], running)
        return running.reshape(state.shape)

    placed = (
        P(None, "row", None, None, "col", None),
        P(None, "row", None, None, "col", None),
        P(None, "row", None, None),
        P(None, "row", None),
    )
    return jax.shard_map(
        local,
        mesh=mesh,
        in_specs=placed,
        out_specs=P(None, "row", None, None, "col", None),
        check_vma=False,
    )
```

time: 562 us -> 201 us (0.36)
  the two profiles are of different devices: /device:TPU:29 before, /device:TPU:0 now
where the time goes in v1:
time: 201 us; the launch traced here: 198 us
  local copies, waits for them, and re-layouts  64.8 us (32%)
  between operations  41.1 us (20%)
  starting transfers between devices  38 us (19%)
  waiting for transfers between devices  24.9 us (12%)
  other arithmetic  17.2 us (9%)
  matrix products  12.6 us (6%)
    ppermute x26, starting transfers between devices, send(): return lax.ppermute(value, AXES, pairs)  38 us
    dynamic_slice x28, local copies, waits for them, and re-layouts, lookup(): jnp.asarray(plan.table(function))  30.2 us
    ppermute x26, waiting for transfers between devices, send(): return lax.ppermute(value, AXES, pairs)  24.9 us
    dynamic_slice x8, local copies, waits for them, and re-layouts, block(): lax.dynamic_slice(array, (index // 2, 0, index % 2, 0), (1, width, 1, wid...  9.29 us
    dot_general x10, matrix products, product(): jnp.dot(first, second, precision=PRECISION, preferred_element_type=jnp.fl...  8.34 us
    unnamed x59, local copies, waits for them, and re-layouts  8.26 us
    transpose x4, local copies, waits for them, and re-layouts, local(): second_blocks.append(jnp.where(turned, found.T, found))  6.37 us
    another operation x10, other arithmetic, spread(): return jnp.stack(result)  5.08 us
  transfers between devices with their start and end apart: 26, of which 6 were waited for; matrix products, arithmetic and copies ran while one was open for 39% of the time, Pallas kernels for 0%

profile of v1, /device:TPU:0, one launch (start us, length us, event | category | flops | bytes accessed | tf_op | source)
XLA Modules:
  0.0 198.5 jit_solution(11764815091534620020)
XLA Ops:
  0.0 1.4 dynamic_slice.217
  5.1 1.3 dynamic_slice.253
  7.7 1.3 dynamic_slice.237
  15.4 1.4 collective-permute-start.10
  17.5 5.0 %collective-permute-start.4 = (f32[264,256]{1,0:T(8,128)}, f32[264,256]{1,0:T(8,128)}, u32[]{:S(2)}, u32[]{:S(2)}) collective-permute-start(f32[264,256]{1,0:T(8,128)} %pad_maximum_fusion.7), channel_id=1, source_target_pairs={{31,7},{22,14},{13,21},{4,28},{27,3},{18,10},{9,17},{0,24},{29,5},... | collective-permute-start | bytes 811016 | tf_op jit(solution)/shard_map/ppermute | solution.py:74
  49.8 2.1 %constant_dynamic-slice_fusion.20 = (f32[1,1,256,1,1,256]{5,4,3,2,1,0:T(1,128)}, f32[1,1,256,1,1,256]{5,4,3,2,1,0:T(1,128)S(1)}, f32[1,1,256,1,1,256]{5,4,3,2,1,...) fusion(f32[4,1,256,2,1,256]{5,4,3,2,1,0:T(1,128)S(1)} %copy-don, ...), kind=kLoop, calls=%fused_computation.111 | loop fusion | bytes 3670072 | tf_op jit(solution)/shard_map/dynamic_slice | solution.py:104
  52.8 1.5 collective-permute-start.1
  55.0 1.4 collective-permute-start.3
  57.1 1.4 collective-permute-start.2
  58.5 3.1 %constant_dynamic-slice_fusion.19 = (f32[1,1,256,1,1,256]{5,4,3,2,1,0:T(1,128)}, f32[1,1,256,1,1,256]{5,4,3,2,1,0:T(1,128)}, f32[1,1,256,1,1,256]{5,4,3,2,1,0:T(...) fusion(f32[4,1,256,2,1,256]{5,4,3,2,1,0:T(1,128)} %param.43, s32[]{:T(128)S(6)} %select_n.417, ...), kind=kLoop, calls=%fused_computation.110 | loop fusion | bytes 2621480 | tf_op jit(solution)/shard_map/dynamic_slice | solution.py:104
  69.7 1.3 dynamic_slice.269
  72.3 1.3 dynamic_slice.282
  79.6 1.3 dynamic_slice.263
  82.1 1.3 dynamic_slice.278
  85.6 2.7 %copy.103 = f32[4,1,256,2,1,256]{5,3,4,2,1,0:T(2,128)S(1)} copy(f32[4,1,256,2,1,256]{5,4,3,2,1,0:T(1,128)} %param.43) | data formatting | bytes 4194304
  94.9 1.8 copy.65
  96.6 1.7 copy.109
  98.3 1.8 copy.64
  104.9 1.5 collective-permute-start.6
  106.4 1.5 collective-permute-start.7
  107.9 1.4 collective-permute-start
  109.3 2.2 %fusion.21 = f32[256,256]{1,0:T(8,128)S(1)} fusion(f32[256,256]{0,1:T(8,128)} %collective-permute-done.1, f32[1,1,256,1,1,256]{2,5,0,1,3,4:T(8,128)} %copy.87, f32[256,256]{1,0:T(8,128)} %collective-permute-done.2, f32[256,256]{1,0:T(8,128)} %collective-permute-done.3, f32[4,1,256,256]{3,2,1,0:T(8,128)S(1)} %copy-done.9, s32[]{:T(128)S(6)} %select_n.425, ...), kind=kOutput, calls=%fused_computation.38 | convolution fusion | flops 100859904 | bytes 1572869 | tf_op jit(solution)/shard_map/dot_general | solution.py:12
  115.0 1.3 fusion.38
  118.0 1.3 collective-permute-start.5
  120.0 2.1 %maximum_select_fusion.1 = f32[2,256,256]{1,2,0:T(8,128)S(1)} fusion(f32[1,256,256]{1,2,0:T(8,128)} %bitcast.186, f32[1,256,256]{1,2,0:T(8,128)} %bitcast.187, f32[2,256,256]{1,2,0:T(8,128)} %collective-permute-done.6, f32[2,256,256]{1,2,0:T(8,128)} %collective-permute-done.7, pred[]{:T(512)} %bitcast.26), kind=kLoop, calls=%fused_computation.21 | loop fusion | flops 393216 | bytes 2097153 | tf_op jit(solution)/shard_map/jit(_where)/select_n | solution.py:153
  123.5 4.8 %collective-permute-done.5 = f32[256,256]{0,1:T(8,128)S(1)} collective-permute-done((f32[256,256]{0,1:T(8,128)}, f32[256,256]{0,1:T(8,128)S(1)}, u32[]{:S(2)}, u32[]{:S(2)}) %collective-permute-start.5) | collective-permute-done | bytes 262176 | tf_op jit(solution)/shard_map/ppermute | solution.py:74
  129.4 1.3 collective-permute-start.18
  131.4 1.7 fusion.12
  134.1 1.3 collective-permute-start.22
  135.7 5.5 %collective-permute-start.16 = (f32[256,256]{1,0:T(8,128)S(1)}, f32[256,256]{1,0:T(8,128)S(1)}, u32[]{:S(2)}, u32[]{:S(2)}) collective-permute-start(f32[256,256]{1,0:T(8,128)S(1)} %fusion.35), channel_id=1, source_target_pairs={{15,13},{22,20},{29,27},{4,2},{11,9},{18,16},{25,31},{0,6},{13,11}... | collective-permute-start | bytes 786440 | tf_op jit(solution)/shard_map/ppermute | solution.py:74
  141.2 6.0 %collective-permute-done.18 = f32[256,256]{1,0:T(8,128)S(1)} collective-permute-done((f32[256,256]{1,0:T(8,128)S(1)}, f32[256,256]{1,0:T(8,128)S(1)}, u32[]{:S(2)}, u32[]{:S(2)}) %collective-permute-start.18) | collective-permute-done | bytes 262176 | tf_op jit(solution)/shard_map/ppermute | solution.py:74
  147.1 1.3 collective-permute-start.20
  149.0 1.9 collective-permute-start.14
  150.9 5.9 %collective-permute-done.22 = f32[256,256]{1,0:T(8,128)S(1)} collective-permute-done((f32[256,256]{1,0:T(8,128)S(1)}, f32[256,256]{1,0:T(8,128)S(1)}, u32[]{:S(2)}, u32[]{:S(2)}) %collective-permute-start.22) | collective-permute-done | bytes 262176 | tf_op jit(solution)/shard_map/ppermute | solution.py:74
  156.9 1.3 collective-permute-start.24
  159.7 1.3 collective-permute-start.12
  161.6 5.4 %collective-permute-done.24 = f32[256,256]{1,0:T(8,128)S(1)} collective-permute-done((f32[256,256]{1,0:T(8,128)S(1)}, f32[256,256]{1,0:T(8,128)S(1)}, u32[]{:S(2)}, u32[]{:S(2)}) %collective-permute-start.24) | collective-permute-done | bytes 262176 | tf_op jit(solution)/shard_map/ppermute | solution.py:74
  167.0 1.6 collective-permute-start.11
  170.1 2.5 %fusion.6 = f32[4,256,2,256]{3,1,2,0:T(8,128)} fusion(f32[4,256,2,256]{3,2,1,0:T(2,128)S(1)} %bitcast.184, f32[1,256,256]{2,1,0:T(8,128)S(1)} %get-tuple-element.27, f32[1,256,256]{2,1,0:T(8,128)S(1)} %get-tuple-element.28, f32[1,256,256]{2,1,0:T(8,128)S(1)} %get-tuple-element.29, f32[1,256,256]{2,1,0:T(8,128)S(1)} %get-tuple-element.26), kind=kOutput, calls=%fused_computation.8 | convolution fusion | flops 806092800 | bytes 5242880 | tf_op jit(solution)/shard_map/rab,rbcd->racd/dot_general | solution.py:261
  172.6 1.3 collective-permute-start.15
  176.0 1.8 collective-permute-done.15
  180.2 1.8 copy.71
  182.0 1.8 copy.72
  183.8 1.8 copy.73
  185.6 3.2 %fusion.25 = (f32[1,256,256]{2,1,0:T(8,128)S(1)}, f32[1,256,256]{2,1,0:T(8,128)S(1)}, f32[1,256,256]{2,1,0:T(8,128)S(1)}) fusion(f32[256,256]{1,0:T(8,128)} %copy.71, f32[4,256,256]{2,1,0:T(8,128)S(1)} %pad_maximum_fusion, s32[]{:T(128)S(6)} %select_n.474, pred[]{:T(512)} %bitcast, f32[256,256]{1,0:T(8,128)} %copy.73, s32[]{:T(128)S(6)} %select_n.483, ...), kind=kLoop, calls=%fused_computation.50 | loop fusion | flops 196608 | bytes 2359311 | tf_op jit(solution)/shard_map/stack | solution.py:272
  189.1 1.9 slice.44
  193.3 1.8 fusion.3
  195.0 3.5 %copy.77 = f32[4,1,256,2,1,256]{5,4,3,2,1,0:T(1,128)} copy(f32[4,1,256,2,1,256]{5,2,3,0,4,1:T(8,128)S(1)} %fusion.3) | data formatting | bytes 4194304 | tf_op jit(solution)/shard_map/reshape | solution.py:273
  (153 shorter events, 52.6 us)
Async XLA Ops:
  0.0 49.8 %copy-start.1 = (f32[4,1,256,2,1,256]{5,4,3,2,1,0:T(1,128)S(1)}, f32[4,1,256,2,1,256]{5,4,3,2,1,0:T(1,128)}, u32[]{:S(2)}) copy-start(f32[4,1,256,2,1,256]{5,4,3,2,1,0:T(1,128)} %param.44) | copy-start | bytes 6291460
  15.4 98.2 %collective-permute-start.10 = (f32[264,256]{1,0:T(8,128)}, f32[264,256]{1,0:T(8,128)}, u32[]{:S(2)}, u32[]{:S(2)}) collective-permute-start(f32[264,256]{1,0:T(8,128)} %pad_maximum_fusion.8), channel_id=1, source_target_pairs={{31,15},{13,29},{27,11},{9,25},{29,13},{15,31},{25,9},{11,27}} | collective-permute-start | bytes 811016 | tf_op jit(solution)/shard_map/ppermute | solution.py:74
  17.5 94.0 %collective-permute-start.4 = (f32[264,256]{1,0:T(8,128)}, f32[264,256]{1,0:T(8,128)}, u32[]{:S(2)}, u32[]{:S(2)}) collective-permute-start(f32[264,256]{1,0:T(8,128)} %pad_maximum_fusion.7), channel_id=1, source_target_pairs={{31,7},{22,14},{13,21},{4,28},{27,3},{18,10},{9,17},{0,24},{29,5},... | collective-permute-start | bytes 811016 | tf_op jit(solution)/shard_map/ppermute | solution.py:74
  52.8 8.8 %copy-start.14 = (f32[1,1,256,1,1,256]{5,4,3,2,1,0:T(1,128)S(1)}, f32[1,1,256,1,1,256]{5,4,3,2,1,0:T(1,128)}, u32[]{:S(2)}) copy-start(f32[1,1,256,1,1,256]{5,4,3,2,1,0:T(1,128)} %get-tuple-element.7) | copy-start | bytes 786436
  52.8 52.1 %collective-permute-start.1 = (f32[256,256]{0,1:T(8,128)}, f32[256,256]{0,1:T(8,128)}, u32[]{:S(2)}, u32[]{:S(2)}) collective-permute-start(f32[256,256]{0,1:T(8,128)} %bitcast.88), channel_id=1, source_target_pairs={{7,5},{14,12},{21,23},{28,30},{3,1},{10,8},{17,19},{24,26}} | collective-permute-start | bytes 786440 | tf_op jit(solution)/shard_map/ppermute | solution.py:74
  55.0 51.3 %collective-permute-start.3 = (f32[256,256]{1,0:T(8,128)}, f32[256,256]{1,0:T(8,128)}, u32[]{:S(2)}, u32[]{:S(2)}) collective-permute-start(f32[256,256]{1,0:T(8,128)} %bitcast.177), channel_id=1, source_target_pairs={{24,7},{17,14},{10,21},{3,28},{28,3},{21,10},{14,17},{7,24}} | collective-permute-start | bytes 786440 | tf_op jit(solution)/shard_map/ppermute | solution.py:74
  57.1 50.7 %collective-permute-start.2 = (f32[256,256]{1,0:T(8,128)}, f32[256,256]{1,0:T(8,128)}, u32[]{:S(2)}, u32[]{:S(2)}) collective-permute-start(f32[256,256]{1,0:T(8,128)} %bitcast.178), channel_id=1, source_target_pairs={{24,5},{17,12},{10,23},{3,30},{28,1},{21,8},{14,19},{7,26}} | collective-permute-start | bytes 786440 | tf_op jit(solution)/shard_map/ppermute | solution.py:74
  85.6 2.8 %copy-start.25 = (pred[4,8]{1,0:T(4,128)(4,1)S(1)}, pred[4,8]{1,0:T(4,128)(4,1)}, u32[]{:S(2)}) copy-start(pred[4,8]{1,0:T(4,128)(4,1)} %constant.302.clone) | copy-start | bytes 100
  85.6 3.5 %copy-start.24 = (pred[4,8]{1,0:T(4,128)(4,1)S(1)}, pred[4,8]{1,0:T(4,128)(4,1)}, u32[]{:S(2)}) copy-start(pred[4,8]{1,0:T(4,128)(4,1)} %constant.296.clone) | copy-start | bytes 100
  85.6 4.1 %copy-start.23 = (pred[4,8]{1,0:T(4,128)(4,1)S(1)}, pred[4,8]{1,0:T(4,128)(4,1)}, u32[]{:S(2)}) copy-start(pred[4,8]{1,0:T(4,128)(4,1)} %constant.293.clone) | copy-start | bytes 100
  85.6 4.8 %copy-start.22 = (pred[4,8]{1,0:T(4,128)(4,1)S(1)}, pred[4,8]{1,0:T(4,128)(4,1)}, u32[]{:S(2)}) copy-start(pred[4,8]{1,0:T(4,128)(4,1)} %constant.292.clone) | copy-start | bytes 100
  85.6 5.3 %copy-start.21 = (pred[4,8]{1,0:T(4,128)(4,1)S(1)}, pred[4,8]{1,0:T(4,128)(4,1)}, u32[]{:S(2)}) copy-start(pred[4,8]{1,0:T(4,128)(4,1)} %constant.290.clone) | copy-start | bytes 100
  85.6 6.0 %copy-start.20 = (pred[4,8]{1,0:T(4,128)(4,1)S(1)}, pred[4,8]{1,0:T(4,128)(4,1)}, u32[]{:S(2)}) copy-start(pred[4,8]{1,0:T(4,128)(4,1)} %constant.288.clone) | copy-start | bytes 100
  85.6 6.6 %copy-start.19 = (pred[4,8]{1,0:T(4,128)(4,1)S(1)}, pred[4,8]{1,0:T(4,128)(4,1)}, u32[]{:S(2)}) copy-start(pred[4,8]{1,0:T(4,128)(4,1)} %constant.286.clone) | copy-start | bytes 100
  85.6 7.3 %copy-start.18 = (pred[4,8]{1,0:T(4,128)(4,1)S(1)}, pred[4,8]{1,0:T(4,128)(4,1)}, u32[]{:S(2)}) copy-start(pred[4,8]{1,0:T(4,128)(4,1)} %constant.282.clone) | copy-start | bytes 100
  85.6 7.9 %copy-start.17 = (pred[4,8]{1,0:T(4,128)(4,1)S(1)}, pred[4,8]{1,0:T(4,128)(4,1)}, u32[]{:S(2)}) copy-start(pred[4,8]{1,0:T(4,128)(4,1)} %constant.279.clone) | copy-start | bytes 100
  85.6 8.5 %copy-start.13 = (f32[1,1,256,1,1,256]{5,4,3,2,1,0:T(1,128)S(1)}, f32[1,1,256,1,1,256]{5,4,3,2,1,0:T(1,128)}, u32[]{:S(2)}) copy-start(f32[1,1,256,1,1,256]{5,4,3,2,1,0:T(1,128)} %get-tuple-element.12) | copy-start | bytes 786436
  88.4 20.9 %copy-start.9 = (f32[4,1,256,256]{3,2,1,0:T(8,128)S(1)}, f32[4,1,256,256]{3,2,1,0:T(8,128)}, u32[]{:S(2)}) copy-start(f32[4,1,256,256]{3,2,1,0:T(8,128)} %param.45) | copy-start | bytes 3145732
  104.9 13.1 %collective-permute-start.6 = (f32[2,256,256]{1,2,0:T(8,128)}, f32[2,256,256]{1,2,0:T(8,128)}, u32[]{:S(2)}, u32[]{:S(2)}) collective-permute-start(f32[2,256,256]{1,2,0:T(8,128)} %pad_maximum_fusion.5), channel_id=1, source_target_pairs={{25,13},{11,31},{29,9},{15,27}} | collective-permute-start | bytes 1572872 | tf_op jit(solution)/shard_map/ppermute | solution.py:74
  106.4 12.9 %collective-permute-start.7 = (f32[2,256,256]{1,2,0:T(8,128)}, f32[2,256,256]{1,2,0:T(8,128)}, u32[]{:S(2)}, u32[]{:S(2)}) collective-permute-start(f32[2,256,256]{1,2,0:T(8,128)} %pad_maximum_fusion.6), channel_id=1, source_target_pairs={{25,15},{18,22},{11,29},{29,11},{22,18},{15,25}} | collective-permute-start | bytes 1572872 | tf_op jit(solution)/shard_map/ppermute | solution.py:74
  107.9 14.2 %collective-permute-start = (f32[2,256,256]{2,1,0:T(8,128)}, f32[2,256,256]{2,1,0:T(8,128)}, u32[]{:S(2)}, u32[]{:S(2)}) collective-permute-start(f32[2,256,256]{2,1,0:T(8,128)} %pad_maximum_fusion.4), channel_id=1, source_target_pairs={{15,13},{29,31},{11,9},{25,27}} | collective-permute-start | bytes 1572872 | tf_op jit(solution)/shard_map/ppermute | solution.py:74
  111.5 77.5 %collective-permute-start.25 = (f32[4,256,2,256]{3,2,1,0:T(2,128)S(1)}, f32[4,256,2,256]{3,2,1,0:T(2,128)}, u32[]{:S(2)}, u32[]{:S(2)}) collective-permute-start(f32[4,256,2,256]{3,2,1,0:T(2,128)S(1)} %bitcast.183), channel_id=1, source_target_pairs={{0,8},{1,9},{2,10},{3,11},{4,12},{5,13},{6,14},{7,15},{8,16},{9,17... | collective-permute-start | bytes 6291464 | tf_op jit(solution)/shard_map/ppermute | solution.py:74
  117.2 5.6 %copy-start.15 = (f32[1,1,256,1,1,256]{5,2,4,3,1,0:T(8,128)S(1)}, f32[1,1,256,1,1,256]{5,2,4,3,1,0:T(8,128)}, u32[]{:S(2)}) copy-start(f32[1,1,256,1,1,256]{5,2,4,3,1,0:T(8,128)} %copy.108) | copy-start | bytes 786436
  117.2 5.6 %copy-start.16 = (f32[1,1,256,1,1,256]{5,2,4,3,1,0:T(8,128)S(1)}, f32[1,1,256,1,1,256]{5,2,4,3,1,0:T(8,128)}, u32[]{:S(2)}) copy-start(f32[1,1,256,1,1,256]{5,2,4,3,1,0:T(8,128)} %copy.109) | copy-start | bytes 786436
  117.2 12.2 %collective-permute-start.8 = (f32[256,256]{0,1:T(8,128)}, f32[256,256]{0,1:T(8,128)S(1)}, u32[]{:S(2)}, u32[]{:S(2)}) collective-permute-start(f32[256,256]{0,1:T(8,128)} %copy.63), channel_id=1, source_target_pairs={{19,22},{1,4},{23,18}} | collective-permute-start | bytes 786440 | tf_op jit(solution)/shard_map/ppermute | solution.py:74
  118.0 10.3 %collective-permute-start.5 = (f32[256,256]{0,1:T(8,128)}, f32[256,256]{0,1:T(8,128)S(1)}, u32[]{:S(2)}, u32[]{:S(2)}) collective-permute-start(f32[256,256]{0,1:T(8,128)} %copy.63), channel_id=1, source_target_pairs={{14,15},{21,22},{28,29},{3,4},{10,11},{17,18},{24,25},{5,0},{12,13... | collective-permute-start | bytes 786440 | tf_op jit(solution)/shard_map/ppermute | solution.py:74
  119.3 14.8 %collective-permute-start.21 = (f32[256,256]{1,0:T(8,128)S(1)}, f32[256,256]{1,0:T(8,128)S(1)}, u32[]{:S(2)}, u32[]{:S(2)}) collective-permute-start(f32[256,256]{1,0:T(8,128)S(1)} %fusion.38), channel_id=1, source_target_pairs={{7,3},{14,10},{21,17},{28,24},{3,7},{10,14},{17,21},{24,28},{5,1},... | collective-permute-start | bytes 786440 | tf_op jit(solution)/shard_map/ppermute | solution.py:74
  122.1 8.6 %collective-permute-start.9 = (f32[256,256]{1,0:T(8,128)S(1)}, f32[256,256]{1,0:T(8,128)S(1)}, u32[]{:S(2)}, u32[]{:S(2)}) collective-permute-start(f32[256,256]{1,0:T(8,128)S(1)} %fusion.38), channel_id=1, source_target_pairs={{7,15},{21,29},{3,11},{17,25},{5,13},{23,31},{1,9},{19,27}} | collective-permute-start | bytes 786440 | tf_op jit(solution)/shard_map/ppermute | solution.py:74
  123.5 10.0 %copy-start.11 = (f32[264,256]{1,0:T(8,128)S(1)}, f32[264,256]{1,0:T(8,128)}, u32[]{:S(2)}) copy-start(f32[264,256]{1,0:T(8,128)} %copy-done.10) | copy-start | bytes 811012
  123.5 10.0 %slice-start = ((f32[264,256]{1,0:T(8,128)}), f32[1,256]{1,0:T(1,128)S(1)}, s32[]{:S(2)}) async-start(f32[264,256]{1,0:T(8,128)} %copy-done.10), calls=%async_computation | async-start | bytes 2048 | tf_op jit(solution)/shard_map/slice | solution.py:121
  128.3 7.4 %collective-permute-start.19 = (f32[256,256]{1,0:T(8,128)S(1)}, f32[256,256]{1,0:T(8,128)S(1)}, u32[]{:S(2)}, u32[]{:S(2)}) collective-permute-start(f32[256,256]{1,0:T(8,128)S(1)} %fusion.38), channel_id=1, source_target_pairs={{7,1},{14,8},{21,23},{28,30},{3,5},{10,12},{17,19},{24,26},{5,7},{... | collective-permute-start | bytes 786440 | tf_op jit(solution)/shard_map/ppermute | solution.py:74
  129.4 17.7 %collective-permute-start.18 = (f32[256,256]{1,0:T(8,128)S(1)}, f32[256,256]{1,0:T(8,128)S(1)}, u32[]{:S(2)}, u32[]{:S(2)}) collective-permute-start(f32[256,256]{1,0:T(8,128)S(1)} %fusion.38), channel_id=1, source_target_pairs={{7,6},{14,15},{21,20},{28,29},{3,2},{10,11},{17,16},{24,25},{5,4},... | collective-permute-start | bytes 786440 | tf_op jit(solution)/shard_map/ppermute | solution.py:74
  130.7 18.3 %collective-permute-start.23 = (f32[256,256]{1,0:T(8,128)S(1)}, f32[256,256]{1,0:T(8,128)S(1)}, u32[]{:S(2)}, u32[]{:S(2)}) collective-permute-start(f32[256,256]{1,0:T(8,128)S(1)} %fusion.38), channel_id=1, source_target_pairs={{7,5},{14,12},{21,19},{28,26},{3,1},{10,8},{17,23},{24,30},{5,3},{... | collective-permute-start | bytes 786440 | tf_op jit(solution)/shard_map/ppermute | solution.py:74
  134.1 22.8 %collective-permute-start.22 = (f32[256,256]{1,0:T(8,128)S(1)}, f32[256,256]{1,0:T(8,128)S(1)}, u32[]{:S(2)}, u32[]{:S(2)}) collective-permute-start(f32[256,256]{1,0:T(8,128)S(1)} %collective-permute-done.21), channel_id=1, source_target_pairs={{3,2},{10,11},{17,16},{24,25},{7,6},{14,15},{21,20},{28,29},{1,0},... | collective-permute-start | bytes 786440 | tf_op jit(solution)/shard_map/ppermute | solution.py:74
  135.7 33.6 %collective-permute-start.16 = (f32[256,256]{1,0:T(8,128)S(1)}, f32[256,256]{1,0:T(8,128)S(1)}, u32[]{:S(2)}, u32[]{:S(2)}) collective-permute-start(f32[256,256]{1,0:T(8,128)S(1)} %fusion.35), channel_id=1, source_target_pairs={{15,13},{22,20},{29,27},{4,2},{11,9},{18,16},{25,31},{0,6},{13,11}... | collective-permute-start | bytes 786440 | tf_op jit(solution)/shard_map/ppermute | solution.py:74
  147.1 12.5 %collective-permute-start.20 = (f32[256,256]{1,0:T(8,128)S(1)}, f32[256,256]{1,0:T(8,128)S(1)}, u32[]{:S(2)}, u32[]{:S(2)}) collective-permute-start(f32[256,256]{1,0:T(8,128)S(1)} %collective-permute-done.19), channel_id=1, source_target_pairs={{1,0},{8,9},{23,22},{30,31},{5,4},{12,13},{19,18},{26,27},{7,6},{1... | collective-permute-start | bytes 786440 | tf_op jit(solution)/shard_map/ppermute | solution.py:74
  149.0 23.6 %collective-permute-start.14 = (f32[256,256]{1,0:T(8,128)S(1)}, f32[256,256]{1,0:T(8,128)S(1)}, u32[]{:S(2)}, u32[]{:S(2)}) collective-permute-start(f32[256,256]{1,0:T(8,128)S(1)} %fusion.35), channel_id=1, source_target_pairs={{15,11},{22,18},{29,25},{4,0},{11,15},{18,22},{25,29},{0,4},{13,9}... | collective-permute-start | bytes 786440 | tf_op jit(solution)/shard_map/ppermute | solution.py:74
  156.9 10.1 %collective-permute-start.24 = (f32[256,256]{1,0:T(8,128)S(1)}, f32[256,256]{1,0:T(8,128)S(1)}, u32[]{:S(2)}, u32[]{:S(2)}) collective-permute-start(f32[256,256]{1,0:T(8,128)S(1)} %collective-permute-done.23), channel_id=1, source_target_pairs={{5,4},{12,13},{19,18},{26,27},{1,0},{8,9},{23,22},{30,31},{3,2},{1... | collective-permute-start | bytes 786440 | tf_op jit(solution)/shard_map/ppermute | solution.py:74
  159.7 14.3 %collective-permute-start.12 = (f32[256,256]{1,0:T(8,128)S(1)}, f32[256,256]{1,0:T(8,128)S(1)}, u32[]{:S(2)}, u32[]{:S(2)}) collective-permute-start(f32[256,256]{1,0:T(8,128)S(1)} %fusion.35), channel_id=1, source_target_pairs={{15,9},{22,16},{29,31},{4,6},{11,13},{18,20},{25,27},{0,2},{13,15}... | collective-permute-start | bytes 786440 | tf_op jit(solution)/shard_map/ppermute | solution.py:74
  167.0 7.7 %collective-permute-start.11 = (f32[256,256]{1,0:T(8,128)S(1)}, f32[256,256]{1,0:T(8,128)S(1)}, u32[]{:S(2)}, u32[]{:S(2)}) collective-permute-start(f32[256,256]{1,0:T(8,128)S(1)} %fusion.35), channel_id=1, source_target_pairs={{15,14},{22,23},{29,28},{4,5},{11,10},{18,19},{25,24},{0,1},{13,12... | collective-permute-start | bytes 786440 | tf_op jit(solution)/shard_map/ppermute | solution.py:74
  169.3 6.0 %collective-permute-start.17 = (f32[256,256]{1,0:T(8,128)S(1)}, f32[256,256]{1,0:T(8,128)S(1)}, u32[]{:S(2)}, u32[]{:S(2)}) collective-permute-start(f32[256,256]{1,0:T(8,128)S(1)} %collective-permute-done.16), channel_id=1, source_target_pairs={{13,12},{20,21},{27,26},{2,3},{9,8},{16,17},{31,30},{6,7},{11,10},... | collective-permute-start | bytes 786440 | tf_op jit(solution)/shard_map/ppermute | solution.py:74
  170.1 2.5 %copy-start.3 = (f32[1,256,256]{2,1,0:T(8,128)}, f32[1,256,256]{2,1,0:T(8,128)S(1)}, u32[]{:S(2)}) copy-start(f32[1,256,256]{2,1,0:T(8,128)S(1)} %get-tuple-element.27) | copy-start | bytes 786436
  172.6 5.2 %collective-permute-start.15 = (f32[256,256]{1,0:T(8,128)S(1)}, f32[256,256]{1,0:T(8,128)S(1)}, u32[]{:S(2)}, u32[]{:S(2)}) collective-permute-start(f32[256,256]{1,0:T(8,128)S(1)} %collective-permute-done.14), channel_id=1, source_target_pairs={{11,10},{18,19},{25,24},{0,1},{15,14},{22,23},{29,28},{4,5},{9,8},... | collective-permute-start | bytes 786440 | tf_op jit(solution)/shard_map/ppermute | solution.py:74
  173.9 4.5 %collective-permute-start.13 = (f32[256,256]{1,0:T(8,128)S(1)}, f32[256,256]{1,0:T(8,128)S(1)}, u32[]{:S(2)}, u32[]{:S(2)}) collective-permute-start(f32[256,256]{1,0:T(8,128)S(1)} %collective-permute-done.12), channel_id=1, source_target_pairs={{9,8},{16,17},{31,30},{6,7},{13,12},{20,21},{27,26},{2,3},{15,14},... | collective-permute-start | bytes 786440 | tf_op jit(solution)/shard_map/ppermute | solution.py:74
  185.6 3.2 %copy-start.4 = (f32[1,256,256]{2,1,0:T(8,128)S(1)}, f32[1,256,256]{2,1,0:T(8,128)}, u32[]{:S(2)}) copy-start(f32[1,256,256]{2,1,0:T(8,128)} %copy-done.3) | copy-start | bytes 786436
  185.6 3.3 %copy-start.6 = (f32[1,256,256]{2,1,0:T(8,128)S(1)}, f32[1,256,256]{2,1,0:T(8,128)}, u32[]{:S(2)}) copy-start(f32[1,256,256]{2,1,0:T(8,128)} %copy-done.5) | copy-start | bytes 786436
  185.6 3.3 %copy-start.8 = (f32[1,256,256]{2,1,0:T(8,128)S(1)}, f32[1,256,256]{2,1,0:T(8,128)}, u32[]{:S(2)}) copy-start(f32[1,256,256]{2,1,0:T(8,128)} %copy-done.7) | copy-start | bytes 786436
  185.6 3.3 %copy-start.12 = (f32[1,256,256]{2,1,0:T(8,128)S(1)}, f32[1,256,256]{2,1,0:T(8,128)}, u32[]{:S(2)}) copy-start(f32[1,256,256]{2,1,0:T(8,128)} %get-tuple-element.23) | copy-start | bytes 786436
  (5 other events, 9.6 us)

commit v2 on v0

v2 whole, which is shorter than its diff:
```python
import numpy as np
import jax
import jax.numpy as jnp
from jax import lax
from jax.experimental import pallas as pl
from jax.experimental.pallas import tpu as pltpu
from jax.sharding import PartitionSpec as P

AXES = ("row", "col")
LANES = 128
LIMIT = 40 * 1024 * 1024


def product(first, second, dims=((1,), (0,))):
    return lax.dot_general(
        first,
        second,
        (dims, ((), ())),
        precision=lax.Precision.HIGHEST,
        preferred_element_type=jnp.float32,
    )


class Plan:
    def __init__(self, rows, cols, block_rows, block_cols):
        self.rows, self.cols = rows, cols
        self.count = block_rows * rows
        assert block_rows == 4 and block_cols == 2 and self.count == block_cols * cols
        self.line = 4
        self.stride = cols // self.line
        self.devices = [(r, c) for r in range(rows) for c in range(cols)]
        self.first = self.solving(self.solver_first)
        self.second = self.solving(self.solver_second)

    def own_mirror(self, r):
        return r == (-r) % self.rows

    def place(self, k, d):
        m = d - k
        return (k % self.rows, m % self.cols), 2 * (k // self.rows) + m // self.cols

    def turn(self, r):
        return -1 if self.own_mirror(r) else 1

    def step(self, r, c, by):
        return c // self.stride * self.stride + (c + by * self.turn(r)) % self.stride

    def shift(self, c, by):
        return (c + by * self.stride) % self.cols

    def solver_first(self, k):
        r, p = k % self.rows, k // self.rows
        owner = (self.count - 1 - k) % self.cols
        if p < 2:
            return owner
        return self.shift(owner, -1 if r < self.rows // 2 else 1)

    def solver_second(self, k):
        r = k % self.rows
        if self.own_mirror(r) and (k == 0 or 2 * k > self.count):
            return None
        return self.step(r, self.solver_first(k), 1)

    def solving(self, solver):
        found = {}
        for k in range(self.count):
            c = solver(k)
            if c is not None:
                assert (k % self.rows, c) not in found
                found[(k % self.rows, c)] = k
        return found

    def wants(self, k, d, c):
        return d - k < self.count and self.cols + c >= d - k

    def uses(self, k, d, device):
        r, c = device
        if k % self.rows == r and self.wants(k, d, c):
            return True
        return d == self.count and (d - k) % self.rows == r and k % self.rows == r and self.wants(d - k, d, c)


class Table:
    def __init__(self, plan):
        self.plan, self.columns, self.names = plan, [], {}

    def add(self, name, function):
        self.names[name] = len(self.columns)
        self.columns.append([int(function(device)) for device in plan_devices(self.plan)])

    def array(self):
        return np.asarray(self.columns, np.int32).T.reshape(-1)

    def reader(self, ref):
        device = lax.axis_index("row") * self.plan.cols + lax.axis_index("col")
        return lambda name: ref[device * len(self.columns) + self.names[name]]


def plan_devices(plan):
    return plan.devices


def solution(mesh):
    rows, cols = mesh.shape["row"], mesh.shape["col"]
    plan = Plan(rows, cols, 4, 2)
    count, line, stride = plan.count, plan.line, plan.stride
    first, second = plan.first, plan.second
    table = Table(plan)

    def checked(moves):
        assert len({s for s, _ in moves}) == len(moves) == len({t for _, t in moves})
        return moves

    def send(value, moves):
        pairs = [(s[0] * cols + s[1], t[0] * cols + t[1]) for s, t in checked(moves)]
        return lax.ppermute(value, AXES, pairs)

    def operand_moves(name, d, solving):
        hand, mirror = [], ([], [])
        slots = {"hand": {}, "mirror0": {}, "mirror1": {}}
        for device, k in solving.items():
            owner, slot = plan.place(k, d)
            if owner != device:
                hand.append((owner, device))
                slots["hand"][owner] = slot
            owner, slot = plan.place(d - k, d)
            assert owner != device
            mirror[slot // 4].append((owner, device))
            slots["mirror%d" % (slot // 4)][owner] = slot
        for part, found in slots.items():
            table.add(name + part, lambda device: found.get(device, 0))
        local = lambda device: device in solving and plan.place(solving[device], d)[0] == device
        table.add(name + "local", local)
        table.add(name + "own", lambda device: plan.place(solving[device], d)[1] if local(device) else 0)
        table.add(name + "near", lambda device: solving.get(device, 0) // rows)
        table.add(name + "solves", lambda device: device in solving)
        return checked(hand), checked(mirror[0]), checked(mirror[1])

    hand_first, mirror_first0, mirror_first1 = operand_moves("first_", count - 1, first)
    hand_second, mirror_second0, mirror_second1 = operand_moves("second_", count, second)

    far_first = [((rows - 1 - r, c), (r, c)) for r, c in first]
    table.add(
        "first_far",
        lambda device: (count - 1 - first.get((rows - 1 - device[0], device[1]), 0)) // rows,
    )
    far_second = [((-r % rows, c), (r, c)) for r, c in second if not plan.own_mirror(r)]

    def far_slot(device):
        k = second.get((-device[0] % rows, device[1]), 1)
        return (count - k) // rows

    table.add("second_far", far_slot)
    table.add("within", lambda device: plan.own_mirror(device[0]))
    table.add("halfway", lambda device: 2 * second.get(device, 0) == count)

    def at_first(k):
        return (k % rows, plan.solver_first(k))

    cross = [
        (at_first(count - k), device)
        for device, k in second.items()
        if plan.own_mirror(device[0]) and 2 * k != count
    ]
    beside = [(at_first(k - 1), device) for device, k in second.items() if not plan.own_mirror(device[0])]

    def spread_moves(d, solving):
        shifts = []
        steps = {}
        for by in range(1, line):
            moves = []
            for (r, c), k in solving.items():
                at = plan.shift(c, by)
                group = [(r, plan.step(r, at, step)) for step in range(stride)]
                if any(plan.uses(k, d, device) for device in group):
                    moves.append(((r, c), (r, at)))
            shifts.append(moves)
        for by in range(line):
            for step in range(1, stride):
                moves = []
                for (r, c), k in solving.items():
                    at = plan.shift(c, by)
                    target = (r, plan.step(r, at, step))
                    direct = d < count and by == 0 and second.get(target) in (k, count - k)
                    if plan.uses(k, d, target) or direct or (d < count and by == 0 and step == 1):
                        moves.append(((r, at), target))
                steps[by, step] = moves
        return shifts, steps

    shifts_first, steps_first = spread_moves(count - 1, first)
    shifts_second, steps_second = spread_moves(count, second)

    for p in range(4):

        def index_first(device, p=p):
            return (device[1] // stride - plan.solver_first(p * rows + device[0]) // stride) % line

        table.add("first_index%d" % p, index_first)

        def turned(device, p=p):
            k = p * rows + device[0]
            return k > 0 and plan.solver_second(k) is None

        def index_second(device, p=p):
            k = p * rows + device[0]
            if k == 0:
                return 0
            at = plan.solver_second(count - k if turned(device, p) else k)
            return (device[1] // stride - at // stride) % line

        table.add("second_turned%d" % p, turned)
        table.add("second_index%d" % p, index_second)

    def reached(device, p, q):
        k = p * rows + device[0]
        return 0 < k and q * cols + device[1] > count - k

    common = [(p, q) for p in range(4) for q in range(2) if reached((rows // 2, cols // 2), p, q)]
    seldom = [
        (p, q)
        for p in range(4)
        for q in range(2)
        if (p, q) not in common and any(reached(device, p, q) for device in plan.devices)
    ]

    def panel_moves(slots):
        return [
            ((((r - 1) % rows), c), (r, c))
            for r, c in plan.devices
            if any(reached((r, c), p, q) for p, q in slots)
        ]

    def source_row(p):
        name = "panel%d" % p
        if name not in table.names:
            table.add(name, lambda device: p - 1 if device[0] == rows - 1 and p > 0 else p)
        return name

    for p in range(4):
        source_row(p)
    constants = table.array()

    def local(reversed_rows, state, basis, eigval):
        width = state.shape[2]
        halves = width // LANES
        stripe = 2 * halves
        running = state.reshape(4 * width * stripe, LANES)
        panel = reversed_rows.reshape(4 * width * stripe, LANES)
        own_basis = basis.reshape(4, width, width)
        own_values = eigval.reshape(4, width)
        numbers = jnp.asarray(constants)
        block_shape = jax.ShapeDtypeStruct((width, width), jnp.float32)
        pair_shape = jax.ShapeDtypeStruct((2 * width, width), jnp.float32)
        eigen_shape = jax.ShapeDtypeStruct((width + 8, width), jnp.float32)

        def where_at(slot, half):
            start = slot // 2 * (width * stripe) + slot % 2 * halves + half
            return pl.ds(start, width, stride=stripe)

        def read(ref, slot):
            parts = [ref[where_at(slot, half), :] for half in range(halves)]
            return jnp.concatenate(parts, axis=1) if halves > 1 else parts[0]

        def write(ref, slot, value):
            for half in range(halves):
                ref[where_at(slot, half), :] = value[:, half * LANES : (half + 1) * LANES]

        def call(body, outputs, *operands, flops=0):
            whole = pl.BlockSpec(memory_space=pltpu.VMEM)
            moved = sum(4 * int(np.prod(o.shape)) for o in (*operands, *outputs))
            return pl.pallas_call(
                body,
                out_shape=outputs,
                in_specs=[pl.BlockSpec(memory_space=pltpu.SMEM)] + [whole] * len(operands),
                out_specs=[whole] * len(outputs),
                compiler_params=pltpu.CompilerParams(vmem_limit_bytes=LIMIT),
                cost_estimate=pl.CostEstimate(flops=flops, bytes_accessed=moved, transcendentals=0),
            )(numbers, *operands)

        def put_eigen(target, basis_ref, values_ref, index):
            target[:width, :] = basis_ref[index]
            target[width:, :] = jnp.broadcast_to(values_ref[pl.ds(index, 1), :], (8, width))

        def pack_first(numbers_ref, state_ref, basis_ref, values_ref, mirror0, mirror1, hand, far, own):
            at = table.reader(numbers_ref)
            mirror0[...] = read(state_ref, at("first_mirror0"))
            mirror1[...] = read(state_ref, at("first_mirror1"))
            hand[...] = read(state_ref, at("first_hand"))
            put_eigen(far, basis_ref, values_ref, at("first_far"))
            value = read(state_ref, at("first_own"))
            own[...] = jnp.where(at("first_local") == 1, value, 0.0)

        def pack_second(
            numbers_ref, state_ref, panel_ref, basis_ref, values_ref,
            mirror0, mirror1, hand, far, own, often, rarely,
        ):
            at = table.reader(numbers_ref)
            for target, name in ((mirror0, "mirror0"), (mirror1, "mirror1"), (hand, "hand"), (own, "own")):
                slot = at("second_" + name)
                pair = (read(state_ref, slot), read(panel_ref, slot))
                for index, value in enumerate(pair):
                    if name == "own":
                        value = jnp.where(at("second_local") == 1, value, 0.0)
                    target[index * width : (index + 1) * width, :] = value
            put_eigen(far, basis_ref, values_ref, at("second_far"))
            for target, slots in ((often, common), (rarely, seldom)):
                for index, (p, q) in enumerate(slots):
                    slot = 2 * at("panel%d" % p) + q
                    target[index * width : (index + 1) * width, :] = read(panel_ref, slot)

        def column(values):
            return jnp.broadcast_to(values, (width, width)).T

        def solve(right_side, near, near_values, far, far_values):
            inner = product(near.T, right_side)
            inner = product(inner, far)
            inner = inner / (column(near_values) + far_values)
            return product(product(near, inner), far, ((1,), (1,)))

        def solve_first(
            numbers_ref, own, hand, mirror0, mirror1, far, basis_ref, values_ref, out
        ):
            at = table.reader(numbers_ref)
            right_side = own[...] + hand[...] + (mirror0[...] + mirror1[...]).T
            index = at("first_near")
            found = solve(
                right_side,
                basis_ref[index],
                values_ref[pl.ds(index, 1), :],
                far[:width, :],
                far[width : width + 1, :],
            )
            out[...] = jnp.where(at("first_solves") == 1, found, 0.0)

        def solve_second(
            numbers_ref, own, hand, mirror0, mirror1, far, left, cross_ref, beside_ref,
            basis_ref, values_ref, out,
        ):
            at = table.reader(numbers_ref)
            upper, lower = slice(0, width), slice(width, 2 * width)
            halfway = jnp.where(at("halfway") == 1, left[...], 0.0)
            right = (cross_ref[...] + halfway).T + beside_ref[...]
            own_side = own[upper, :] + hand[upper, :]
            own_side = own_side - product(left[...], own[lower, :] + hand[lower, :])
            across = (mirror0[lower, :] + mirror1[lower, :]).T
            mirror_side = (mirror0[upper, :] + mirror1[upper, :]).T - product(across, right)
            index = at("second_near")
            within = at("within") == 1
            far_index = at("second_far")
            far_basis = jnp.where(within, basis_ref[far_index], far[:width, :])
            far_values = jnp.where(within, values_ref[pl.ds(far_index, 1), :], far[width : width + 1, :])
            found = solve(
                own_side + mirror_side,
                basis_ref[index],
                values_ref[pl.ds(index, 1), :],
                far_basis,
                far_values,
            )
            out[...] = jnp.where(at("second_solves") == 1, found, 0.0)

        def update(d, name, slots_of):
            def body(numbers_ref, running_ref, *refs):
                at = table.reader(numbers_ref)
                arrived, sources, out, blocks = refs[: line * stride], refs[line * stride : -2], refs[-2], refs[-1]
                for by in range(line):
                    total = arrived[by * stride][...]
                    for step in range(1, stride):
                        total = total + arrived[by * stride + step][...]
                    blocks[by] = total
                row, col = lax.axis_index("row"), lax.axis_index("col")
                for p in range(4):
                    partner = d - (p * rows + row)
                    index = at("%s_index%d" % (name, p))
                    for q in range(2):
                        here = q * cols + col
                        slot = 2 * p + q
                        rest = read(running_ref, slot)
                        write(out, slot, rest)
                        rows_of_a = slots_of(sources, p, q)

                        if rows_of_a is not None:

                            @pl.when((here > partner) & (partner < count))
                            def _():
                                taken = blocks[index]
                                if name == "second":
                                    taken = jnp.where(at("second_turned%d" % p) == 1, taken.T, taken)
                                write(out, slot, rest - product(taken, rows_of_a()))

                        @pl.when(here == partner)
                        def _():
                            taken = blocks[index]
                            if name == "second":
                                taken = jnp.where(at("second_turned%d" % p) == 1, taken.T, taken)
                            write(out, slot, taken)

            def run(running, arrived, sources):
                whole = pl.BlockSpec(memory_space=pltpu.VMEM)
                operands = (running, *arrived, *sources)
                return pl.pallas_call(
                    body,
                    out_shape=jax.ShapeDtypeStruct(running.shape, jnp.float32),
                    in_specs=[pl.BlockSpec(memory_space=pltpu.SMEM)] + [whole] * len(operands),
                    out_specs=whole,
                    scratch_shapes=[pltpu.VMEM((line, width, width), jnp.float32)],
                    compiler_params=pltpu.CompilerParams(vmem_limit_bytes=LIMIT),
                    cost_estimate=pl.CostEstimate(
                        flops=16 * width**3 * 6, bytes_accessed=8 * running.size, transcendentals=0
                    ),
                )(numbers, *operands)

            return run

        def own_panel(sources, p, q):
            return lambda: read(sources[0], 2 * p + q)

        def next_panel(sources, p, q):
            for ref, slots in zip(sources, (common, seldom)):
                if (p, q) in slots:
                    index = slots.index((p, q))
                    return lambda: ref[index * width : (index + 1) * width, :]
            return None

        def forward(blocks, steps):
            arrived = []
            for by in range(line):
                arrived.append(blocks[by])
                for step in range(1, stride):
                    arrived.append(send(blocks[by], steps[by, step]))
            return arrived

        solve_flops = 4 * 2 * 6 * width**3

        mirror0, mirror1, hand, far, own = call(
            pack_first,
            [block_shape] * 3 + [eigen_shape, block_shape],
            running, own_basis, own_values,
        )
        mirror0 = send(mirror0, mirror_first0)
        mirror1 = send(mirror1, mirror_first1)
        hand = send(hand, hand_first)
        far = send(far, far_first)

        later = call(
            pack_second,
            [pair_shape] * 3
            + [eigen_shape, pair_shape]
            + [
                jax.ShapeDtypeStruct((len(slots) * width, width), jnp.float32)
                for slots in (common, seldom)
            ],
            running, panel, own_basis, own_values,
        )
        later_mirror0 = send(later[0], mirror_second0)
        later_mirror1 = send(later[1], mirror_second1)
        later_hand = send(later[2], hand_second)
        later_far = send(later[3], far_second)
        later_own = later[4]
        often = send(later[5], panel_moves(common))
        rarely = send(later[6], panel_moves(seldom))

        (solved,) = call(
            solve_first, [block_shape], own, hand, mirror0, mirror1, far, own_basis, own_values,
            flops=solve_flops,
        )
        left = send(solved, steps_first[0, 1])
        next_to = send(solved, beside)
        crossed = send(solved, cross)
        blocks = [solved] + [send(solved, moves) for moves in shifts_first]

        (solved_next,) = call(
            solve_second, [block_shape],
            later_own, later_hand, later_mirror0, later_mirror1, later_far,
            left, crossed, next_to, own_basis, own_values,
            flops=solve_flops + solve_flops // 2,
        )
        arrived = [blocks[0], left] + [send(blocks[0], steps_first[0, s]) for s in range(2, stride)]
        arrived += forward(blocks, steps_first)[stride:]
        running = update(count - 1, "first", own_panel)(running, arrived, [panel])

        blocks = [solved_next] + [send(solved_next, moves) for moves in shifts_second]
        arrived = forward(blocks, steps_second)
        running = update(count, "second", next_panel)(running, arrived, [often, rarely])
        return running.reshape(state.shape)

    placed = (
        P(None, "row", None, None, "col", None),
        P(None, "row", None, None, "col", None),
        P(None, "row", None, None),
        P(None, "row", None),
    )
    return jax.shard_map(
        local,
        mesh=mesh,
        in_specs=placed,
        out_specs=P(None, "row", None, None, "col", None),
        check_vma=False,
    )
```

time: 562 us -> 85.4 us (0.15)
  waiting for transfers between devices: 420 us -> 24 us
  between operations: 42.1 us -> 0.41 us
  local copies, waits for them, and re-layouts: 37.2 us -> 4.22 us
  Pallas kernels: 0 us -> 16.2 us
  matrix products: 15.9 us -> 0 us
  other arithmetic: 14.7 us -> 0 us
  starting transfers between devices: 26.7 us -> 39.9 us
    ppermute x31 -> x26, waiting for transfers between devices: 279 us -> 24 us  [send(): return lax.ppermute(value, AXES, pairs)]
    psum x2 -> x0, waiting for transfers between devices: 141 us -> none  [broadcast(): return lax.psum(block, axis)]
    pallas_call x0 -> x6, Pallas kernels: none -> 16.2 us  [the longest x2 8.48 us: run(): pl.pallas_call(body, out_shape=jax.ShapeDtypeStruct(running.shape, jnp.fl...]
    dot_general x10 -> x0, matrix products: 15.9 us -> none  [batched(): jnp.einsum(einsum_form, first, second, precision=lax.Precision.HIGHEST, p...]
    ppermute x31 -> x26, starting transfers between devices: 26.7 us -> 39.9 us  [send(): return lax.ppermute(value, AXES, pairs)]
    select_n x11 -> x0, other arithmetic: 11 us -> none  [the longest x3 6.38 us: next_rows(): jnp.where(first_row, jnp.concatenate([jnp.zeros_like(member[:1]), member[...]
    slice x16 -> x0, local copies, waits for them, and re-layouts: 9.81 us -> none  [the longest x2 3.13 us: next_rows(): member[:-1]]
    gather x8 -> x0, local copies, waits for them, and re-layouts: 7.8 us -> none  [the longest x2 3.17 us: local(): far_basis[local_rows]]
  transfers between devices with their start and end apart: 33 -> 26, of which waited for: 27 -> 9; matrix products, arithmetic and copies ran while one was open for 5% -> 0% of each run, Pallas kernels for 0% -> 12%
where the time goes in v2:
time: 85.4 us; the launch traced here: 84.8 us
  starting transfers between devices  39.9 us (47%)
  waiting for transfers between devices  24 us (28%)
  Pallas kernels  16.2 us (19%)
  local copies, waits for them, and re-layouts  4.22 us (5%)
    ppermute x26, starting transfers between devices, send(): return lax.ppermute(value, AXES, pairs)  39.9 us
    ppermute x26, waiting for transfers between devices, send(): return lax.ppermute(value, AXES, pairs)  24 us
    pallas_call x2, Pallas kernels, run(): pl.pallas_call(body, out_shape=jax.ShapeDtypeStruct(running.shape, jnp.fl...  8.48 us
    pallas_call x4, Pallas kernels, call(): pl.pallas_call(body, out_shape=outputs, in_specs=[pl.BlockSpec(memory_spa...  7.77 us
    unnamed x13, local copies, waits for them, and re-layouts  4.22 us
  transfers between devices with their start and end apart: 26, of which 9 were waited for; matrix products, arithmetic and copies ran while one was open for 0% of the time, Pallas kernels for 12%

profile of v2, /device:TPU:29, one launch (start us, length us, event | category | flops | bytes accessed | tf_op | source)
XLA Modules:
  0.0 84.8 jit_solution(9830501790597394459)
XLA Ops:
  0.0 0.7 copy.9
  0.7 1.6 %copy-done = f32[4,1,256,2,1,256]{5,4,3,2,1,0:T(1,128)S(1)} copy-done((f32[4,1,256,2,1,256]{5,4,3,2,1,0:T(1,128)S(1)}, f32[4,1,256,2,1,256]{5,4,3,2,1,0:T(1,128)}, u32[]{:S(2)}) %copy-start) | copy-done | bytes 2097176
  2.3 1.2 %copy-done.2 = f32[4,1,256,256]{3,2,1,0:T(8,128)S(1)} copy-done((f32[4,1,256,256]{3,2,1,0:T(8,128)S(1)}, f32[4,1,256,256]{3,2,1,0:T(8,128)}, u32[]{:S(2)}) %copy-start.2) | copy-done | bytes 1048600
  3.5 0.7 copy-done.5
  4.2 0.7 shard_map.55
  5.0 1.3 %collective-permute-start = (f32[256,256]{1,0:T(8,128)S(1)}, f32[256,256]{1,0:T(8,128)S(1)}, u32[]{:S(2)}, u32[]{:S(2)}) collective-permute-start(f32[256,256]{1,0:T(8,128)S(1)} %get-tuple-element.18), channel_id=1, source_target_pairs={{7,5},{14,12},{21,23},{28,30},{3,1},{10,8},{17,19},{24,26}} | collective-permute-start | bytes 786440 | tf_op jit(solution)/shard_map/ppermute | solution.py:116
  6.3 1.3 %collective-permute-start.1 = (f32[256,256]{1,0:T(8,128)S(1)}, f32[256,256]{1,0:T(8,128)S(1)}, u32[]{:S(2)}, u32[]{:S(2)}) collective-permute-start(f32[256,256]{1,0:T(8,128)S(1)} %get-tuple-element.19), channel_id=1, source_target_pairs={{24,5},{17,12},{10,23},{3,30},{28,1},{21,8},{14,19},{7,26}} | collective-permute-start | bytes 786440 | tf_op jit(solution)/shard_map/ppermute | solution.py:116
  7.6 0.7 collective-permute-start.2
  8.2 0.0 copy-start.3
  8.3 1.0 %shard_map.58 = (f32[512,256]{1,0:T(8,128)S(1)}, f32[512,256]{1,0:T(8,128)S(1)}, f32[512,256]{1,0:T(8,128)S(1)}, f32[264,256]{1,0:T(8,128)S(1)}, f32[512,256]{1,...) custom-call(s32[1088]{0:T(1024)S(1)} %copy-done.5, f32[4096,128]{1,0:T(8,128)S(1)} %bitcast.8, ...), custom_call_target="tpu_custom_call" | custom-call | bytes 9187328 | tf_op jit(solution)/shard_map/pallas_call | solution.py:271
  9.2 0.7 collective-permute-start.11
  9.9 1.3 %collective-permute-start.3 = (f32[264,256]{1,0:T(8,128)S(1)}, f32[264,256]{1,0:T(8,128)S(1)}, u32[]{:S(2)}, u32[]{:S(2)}) collective-permute-start(f32[264,256]{1,0:T(8,128)S(1)} %get-tuple-element.21), channel_id=1, source_target_pairs={{31,7},{22,14},{13,21},{4,28},{27,3},{18,10},{9,17},{0,24},{29,5},... | collective-permute-start | bytes 811016 | tf_op jit(solution)/shard_map/ppermute | solution.py:116
  11.2 0.8 collective-permute-done.hand
  12.1 0.7 collective-permute-start.14
  12.7 4.0 %collective-permute-done.1.mirror0 = f32[256,256]{1,0:T(8,128)S(1)} collective-permute-done((f32[256,256]{1,0:T(8,128)S(1)}, f32[256,256]{1,0:T(8,128)S(1)}, u32[]{:S(2)}, u32[]{:S(2)}) %collective-permute-start.1) | collective-permute-done | bytes 262176 | tf_op jit(solution)/shard_map/ppermute | solution.py:116
  16.7 0.7 collective-permute-start.12
  17.4 0.7 collective-permute-start.13
  18.1 1.4 %collective-permute-done.3.far = f32[264,256]{1,0:T(8,128)S(1)} collective-permute-done((f32[264,256]{1,0:T(8,128)S(1)}, f32[264,256]{1,0:T(8,128)S(1)}, u32[]{:S(2)}, u32[]{:S(2)}) %collective-permute-start.3) | collective-permute-done | bytes 270368 | tf_op jit(solution)/shard_map/ppermute | solution.py:116
  19.5 2.7 %shard_map.56.refs_0_ = f32[256,256]{1,0:T(8,128)S(1)} custom-call(s32[1088]{0:T(1024)S(1)} %copy-done.5, f32[256,256]{1,0:T(8,128)S(1)} %get-tuple-element.17.own, f32[256,256]{1,0:T(8,128)S(1)} %collective-permute-done.hand, f32[256,256]{1,0:T(8,128)S(1)} %collective-permute-done.1.mirror0, f32[256,256]{1,0:T(8,128)S(1)} %collective-permute-done.2.mirror1, ...), custom_call_target="tpu_custom_call" | custom-call | flops 805306368 | bytes 2633728 | tf_op jit(solution)/shard_map/pallas_call | solution.py:271
  22.3 0.7 collective-permute-start.16
  23.0 0.0 collective-permute-done.14.far
  23.0 0.7 collective-permute-start.15
  23.7 7.0 %collective-permute-start.9 = (f32[256,256]{1,0:T(8,128)S(1)}, f32[256,256]{1,0:T(8,128)S(1)}, u32[]{:S(2)}, u32[]{:S(2)}) collective-permute-start(f32[256,256]{1,0:T(8,128)S(1)} %shard_map.56.refs_0_), channel_id=1, source_target_pairs={{17,23},{24,30},{5,3},{12,10},{23,21},{30,28},{1,7},{8,14},{19,17}... | collective-permute-start | bytes 786440 | tf_op jit(solution)/shard_map/ppermute | solution.py:116
  30.6 1.3 %collective-permute-start.25 = (f32[512,256]{1,0:T(8,128)S(1)}, f32[512,256]{1,0:T(8,128)S(1)}, u32[]{:S(2)}, u32[]{:S(2)}) collective-permute-start(f32[512,256]{1,0:T(8,128)S(1)} %get-tuple-element.28), channel_id=1, source_target_pairs={{15,23},{22,30},{23,31}} | collective-permute-start | bytes 1572872 | tf_op jit(solution)/shard_map/ppermute | solution.py:116
  31.9 5.1 %collective-permute-start.7 = (f32[256,256]{1,0:T(8,128)S(1)}, f32[256,256]{1,0:T(8,128)S(1)}, u32[]{:S(2)}, u32[]{:S(2)}) collective-permute-start(f32[256,256]{1,0:T(8,128)S(1)} %shard_map.56.refs_0_), channel_id=1, source_target_pairs={{3,7},{10,14},{17,21},{24,28},{5,1},{12,8},{23,19},{30,26},{1,5},{... | collective-permute-start | bytes 786440 | tf_op jit(solution)/shard_map/ppermute | solution.py:116
  37.1 1.9 %collective-permute-start.5 = (f32[256,256]{1,0:T(8,128)S(1)}, f32[256,256]{1,0:T(8,128)S(1)}, u32[]{:S(2)}, u32[]{:S(2)}) collective-permute-start(f32[256,256]{1,0:T(8,128)S(1)} %shard_map.56.refs_0_), channel_id=1, source_target_pairs={{21,23},{28,30},{3,5},{10,12},{17,19},{24,26},{5,7},{12,14},{23,17... | collective-permute-start | bytes 786440 | tf_op jit(solution)/shard_map/ppermute | solution.py:116
  39.0 0.1 collective-permute-start.24
  39.1 3.8 %collective-permute-start.4 = (f32[256,256]{1,0:T(8,128)S(1)}, f32[256,256]{1,0:T(8,128)S(1)}, u32[]{:S(2)}, u32[]{:S(2)}) collective-permute-start(f32[256,256]{1,0:T(8,128)S(1)} %shard_map.56.refs_0_), channel_id=1, source_target_pairs={{7,6},{14,15},{21,20},{28,29},{3,2},{10,11},{17,16},{24,25},{5,4},... | collective-permute-start | bytes 786440 | tf_op jit(solution)/shard_map/ppermute | solution.py:116
  42.9 0.7 collective-permute-done.7.refs_4_
  43.6 1.3 %collective-permute-start.10 = (f32[256,256]{1,0:T(8,128)S(1)}, f32[256,256]{1,0:T(8,128)S(1)}, u32[]{:S(2)}, u32[]{:S(2)}) collective-permute-start(f32[256,256]{1,0:T(8,128)S(1)} %collective-permute-done.9.refs_6_), channel_id=1, source_target_pairs={{23,22},{30,31},{3,2},{10,11},{21,20},{28,29},{7,6},{14,15},{17,16... | collective-permute-start | bytes 786440 | tf_op jit(solution)/shard_map/ppermute | solution.py:116
  44.9 1.7 %collective-permute-done.5.refs_2_ = f32[256,256]{1,0:T(8,128)S(1)} collective-permute-done((f32[256,256]{1,0:T(8,128)S(1)}, f32[256,256]{1,0:T(8,128)S(1)}, u32[]{:S(2)}, u32[]{:S(2)}) %collective-permute-start.5) | collective-permute-done | bytes 262176 | tf_op jit(solution)/shard_map/ppermute | solution.py:116
  46.6 1.3 %collective-permute-start.8 = (f32[256,256]{1,0:T(8,128)S(1)}, f32[256,256]{1,0:T(8,128)S(1)}, u32[]{:S(2)}, u32[]{:S(2)}) collective-permute-start(f32[256,256]{1,0:T(8,128)S(1)} %collective-permute-done.7.refs_4_), channel_id=1, source_target_pairs={{7,6},{14,15},{21,20},{28,29},{1,0},{8,9},{19,18},{26,27},{5,4},{1... | collective-permute-start | bytes 786440 | tf_op jit(solution)/shard_map/ppermute | solution.py:116
  47.9 2.4 %collective-permute-start.6 = (f32[256,256]{1,0:T(8,128)S(1)}, f32[256,256]{1,0:T(8,128)S(1)}, u32[]{:S(2)}, u32[]{:S(2)}) collective-permute-start(f32[256,256]{1,0:T(8,128)S(1)} %collective-permute-done.5.refs_2_), channel_id=1, source_target_pairs={{23,22},{30,31},{5,4},{12,13},{19,18},{26,27},{7,6},{14,15},{17,16... | collective-permute-start | bytes 786440 | tf_op jit(solution)/shard_map/ppermute | solution.py:116
  50.3 0.0 copy-start.1
  50.3 3.4 %shard_map.59.refs_0_ = f32[256,256]{1,0:T(8,128)S(1)} custom-call(s32[1088]{0:T(1024)S(1)} %copy-done.5, f32[512,256]{1,0:T(8,128)S(1)} %get-tuple-element.22.own, f32[512,256]{1,0:T(8,128)S(1)} %collective-permute-done.11.hand, f32[512,256]{1,0:T(8,128)S(1)} %collective-permute-done.12.mirror0, f32[512,256]{1,0:T(8,128)S(1)} %collective-permute-done.13.mirror1, ...), custom_call_target="tpu_custom_call" | custom-call | flops 1207959552 | bytes 4468736 | tf_op jit(solution)/shard_map/pallas_call | solution.py:271
  53.7 0.7 collective-permute-start.22
  54.4 0.7 collective-permute-start.20
  55.1 0.7 collective-permute-start.18
  55.7 1.3 %collective-permute-start.17 = (f32[256,256]{1,0:T(8,128)S(1)}, f32[256,256]{1,0:T(8,128)S(1)}, u32[]{:S(2)}, u32[]{:S(2)}) collective-permute-start(f32[256,256]{1,0:T(8,128)S(1)} %shard_map.59.refs_0_), channel_id=1, source_target_pairs={{20,21},{2,3},{16,17},{4,5},{13,12},{31,30},{9,8},{27,26}} | collective-permute-start | bytes 786440 | tf_op jit(solution)/shard_map/ppermute | solution.py:116
  57.1 1.3 %collective-permute-start.23 = (f32[256,256]{1,0:T(8,128)S(1)}, f32[256,256]{1,0:T(8,128)S(1)}, u32[]{:S(2)}, u32[]{:S(2)}) collective-permute-start(f32[256,256]{1,0:T(8,128)S(1)} %collective-permute-done.22.refs_6_), channel_id=1, source_target_pairs={{18,19},{0,1},{22,23},{31,30},{2,3},{11,10},{29,28},{15,14},{25,24}} | collective-permute-start | bytes 786440 | tf_op jit(solution)/shard_map/ppermute | solution.py:116
  58.4 1.3 %collective-permute-start.21 = (f32[256,256]{1,0:T(8,128)S(1)}, f32[256,256]{1,0:T(8,128)S(1)}, u32[]{:S(2)}, u32[]{:S(2)}) collective-permute-start(f32[256,256]{1,0:T(8,128)S(1)} %collective-permute-done.20.refs_4_), channel_id=1, source_target_pairs={{16,17},{6,7},{15,14},{20,21},{29,28},{0,1},{9,8},{27,26},{13,12},... | collective-permute-start | bytes 786440 | tf_op jit(solution)/shard_map/ppermute | solution.py:116
  59.7 1.3 %collective-permute-start.19 = (f32[256,256]{1,0:T(8,128)S(1)}, f32[256,256]{1,0:T(8,128)S(1)}, u32[]{:S(2)}, u32[]{:S(2)}) collective-permute-start(f32[256,256]{1,0:T(8,128)S(1)} %collective-permute-done.18.refs_2_), channel_id=1, source_target_pairs={{22,23},{31,30},{4,5},{13,12},{18,19},{27,26},{6,7},{15,14},{25,24... | collective-permute-start | bytes 786440 | tf_op jit(solution)/shard_map/ppermute | solution.py:116
  61.0 3.4 %shard_map.57.running_ref = f32[4096,128]{1,0:T(8,128)S(1)} custom-call(s32[1088]{0:T(1024)S(1)} %copy-done.5, f32[4096,128]{1,0:T(8,128)S(1)} %bitcast.9, f32[256,256]{1,0:T(8,128)S(1)} %shard_map.56.refs_0_, f32[256,256]{1,0:T(8,128)S(1)} %collective-permute-done.4.refs_1_.left, f32[256,256]{1,0:T(8,128)S(1)} %collective-permute-done.5.refs_2_, ...), custom_call_target="tpu_custom_call" | custom-call | flops 1610612736 | bytes 4194304 | tf_op jit(solution)/shard_map/pallas_call | solution.py:400
  64.4 6.9 %collective-permute-done.17.refs_1_ = f32[256,256]{1,0:T(8,128)S(1)} collective-permute-done((f32[256,256]{1,0:T(8,128)S(1)}, f32[256,256]{1,0:T(8,128)S(1)}, u32[]{:S(2)}, u32[]{:S(2)}) %collective-permute-start.17) | collective-permute-done | bytes 262176 | tf_op jit(solution)/shard_map/ppermute | solution.py:116
  71.3 2.8 %collective-permute-done.23.refs_7_ = f32[256,256]{1,0:T(8,128)S(1)} collective-permute-done((f32[256,256]{1,0:T(8,128)S(1)}, f32[256,256]{1,0:T(8,128)S(1)}, u32[]{:S(2)}, u32[]{:S(2)}) %collective-permute-start.23) | collective-permute-done | bytes 262176 | tf_op jit(solution)/shard_map/ppermute | solution.py:116
  74.1 2.8 %collective-permute-done.21.refs_5_ = f32[256,256]{1,0:T(8,128)S(1)} collective-permute-done((f32[256,256]{1,0:T(8,128)S(1)}, f32[256,256]{1,0:T(8,128)S(1)}, u32[]{:S(2)}, u32[]{:S(2)}) %collective-permute-start.21) | collective-permute-done | bytes 262176 | tf_op jit(solution)/shard_map/ppermute | solution.py:116
  76.9 2.8 %collective-permute-done.19.refs_3_ = f32[256,256]{1,0:T(8,128)S(1)} collective-permute-done((f32[256,256]{1,0:T(8,128)S(1)}, f32[256,256]{1,0:T(8,128)S(1)}, u32[]{:S(2)}, u32[]{:S(2)}) %collective-permute-start.19) | collective-permute-done | bytes 262176 | tf_op jit(solution)/shard_map/ppermute | solution.py:116
  79.7 5.0 %shard_map.60 = f32[4096,128]{1,0:T(8,128)} custom-call(s32[1088]{0:T(1024)S(1)} %copy-done.5, f32[4096,128]{1,0:T(8,128)S(1)} %shard_map.57.running_ref, f32[256,256]{1,0:T(8,128)S(1)} %shard_map.59.refs_0_, f32[256,256]{1,0:T(8,128)S(1)} %collective-permute-done.17.refs_1_, f32[256,256]{1,0:T(8,128)S(1)} %collective-permute-done.18.refs_2_, ...), custom_call_target="tpu_custom_call" | custom-call | flops 1610612736 | bytes 4194304 | tf_op jit(solution)/shard_map/pallas_call | solution.py:400
  (23 shorter events, 0.1 us)
Async XLA Ops:
  0.7 1.6 %copy-start = (f32[4,1,256,2,1,256]{5,4,3,2,1,0:T(1,128)S(1)}, f32[4,1,256,2,1,256]{5,4,3,2,1,0:T(1,128)}, u32[]{:S(2)}) copy-start(f32[4,1,256,2,1,256]{5,4,3,2,1,0:T(1,128)} %param.6) | copy-start | bytes 6291460
  2.3 1.2 %copy-start.2 = (f32[4,1,256,256]{3,2,1,0:T(8,128)S(1)}, f32[4,1,256,256]{3,2,1,0:T(8,128)}, u32[]{:S(2)}) copy-start(f32[4,1,256,256]{3,2,1,0:T(8,128)} %param.7) | copy-start | bytes 3145732
  3.5 0.7 copy-start.5
  4.2 4.0 %copy-start.4 = (f32[4,1,256,2,1,256]{5,4,3,2,1,0:T(1,128)S(1)}, f32[4,1,256,2,1,256]{5,4,3,2,1,0:T(1,128)}, u32[]{:S(2)}) copy-start(f32[4,1,256,2,1,256]{5,4,3,2,1,0:T(1,128)} %param.5) | copy-start | bytes 6291460
  5.0 7.1 %collective-permute-start = (f32[256,256]{1,0:T(8,128)S(1)}, f32[256,256]{1,0:T(8,128)S(1)}, u32[]{:S(2)}, u32[]{:S(2)}) collective-permute-start(f32[256,256]{1,0:T(8,128)S(1)} %get-tuple-element.18), channel_id=1, source_target_pairs={{7,5},{14,12},{21,23},{28,30},{3,1},{10,8},{17,19},{24,26}} | collective-permute-start | bytes 786440 | tf_op jit(solution)/shard_map/ppermute | solution.py:116
  6.3 10.5 %collective-permute-start.1 = (f32[256,256]{1,0:T(8,128)S(1)}, f32[256,256]{1,0:T(8,128)S(1)}, u32[]{:S(2)}, u32[]{:S(2)}) collective-permute-start(f32[256,256]{1,0:T(8,128)S(1)} %get-tuple-element.19), channel_id=1, source_target_pairs={{24,5},{17,12},{10,23},{3,30},{28,1},{21,8},{14,19},{7,26}} | collective-permute-start | bytes 786440 | tf_op jit(solution)/shard_map/ppermute | solution.py:116
  7.6 9.9 %collective-permute-start.2 = (f32[256,256]{1,0:T(8,128)S(1)}, f32[256,256]{1,0:T(8,128)S(1)}, u32[]{:S(2)}, u32[]{:S(2)}) collective-permute-start(f32[256,256]{1,0:T(8,128)S(1)} %get-tuple-element.20), channel_id=1, source_target_pairs={{24,7},{17,14},{10,21},{3,28},{28,3},{21,10},{14,17},{7,24}} | collective-permute-start | bytes 786440 | tf_op jit(solution)/shard_map/ppermute | solution.py:116
  8.2 11.3 %copy-start.3 = (f32[4,1,256,256]{3,2,1,0:T(8,128)S(1)}, f32[4,1,256,256]{3,2,1,0:T(8,128)}, u32[]{:S(2)}) copy-start(f32[4,1,256,256]{3,2,1,0:T(8,128)} %param.7) | copy-start | bytes 3145732
  9.2 14.4 %collective-permute-start.11 = (f32[512,256]{1,0:T(8,128)S(1)}, f32[512,256]{1,0:T(8,128)S(1)}, u32[]{:S(2)}, u32[]{:S(2)}) collective-permute-start(f32[512,256]{1,0:T(8,128)S(1)} %get-tuple-element.23), channel_id=1, source_target_pairs={{22,20},{4,2},{18,16},{0,4},{15,13},{29,31},{11,9},{25,27}} | collective-permute-start | bytes 1572872 | tf_op jit(solution)/shard_map/ppermute | solution.py:116
  9.9 9.6 %collective-permute-start.3 = (f32[264,256]{1,0:T(8,128)S(1)}, f32[264,256]{1,0:T(8,128)S(1)}, u32[]{:S(2)}, u32[]{:S(2)}) collective-permute-start(f32[264,256]{1,0:T(8,128)S(1)} %get-tuple-element.21), channel_id=1, source_target_pairs={{31,7},{22,14},{13,21},{4,28},{27,3},{18,10},{9,17},{0,24},{29,5},... | collective-permute-start | bytes 811016 | tf_op jit(solution)/shard_map/ppermute | solution.py:116
  12.1 10.9 %collective-permute-start.14 = (f32[264,256]{1,0:T(8,128)S(1)}, f32[264,256]{1,0:T(8,128)S(1)}, u32[]{:S(2)}, u32[]{:S(2)}) collective-permute-start(f32[264,256]{1,0:T(8,128)S(1)} %get-tuple-element.26), channel_id=1, source_target_pairs={{31,15},{13,29},{27,11},{9,25},{29,13},{15,31},{25,9},{11,27}} | collective-permute-start | bytes 811016 | tf_op jit(solution)/shard_map/ppermute | solution.py:116
  16.7 13.9 %collective-permute-start.12 = (f32[512,256]{1,0:T(8,128)S(1)}, f32[512,256]{1,0:T(8,128)S(1)}, u32[]{:S(2)}, u32[]{:S(2)}) collective-permute-start(f32[512,256]{1,0:T(8,128)S(1)} %get-tuple-element.24), channel_id=1, source_target_pairs={{25,13},{11,31},{29,9},{15,27}} | collective-permute-start | bytes 1572872 | tf_op jit(solution)/shard_map/ppermute | solution.py:116
  17.4 14.5 %collective-permute-start.13 = (f32[512,256]{1,0:T(8,128)S(1)}, f32[512,256]{1,0:T(8,128)S(1)}, u32[]{:S(2)}, u32[]{:S(2)}) collective-permute-start(f32[512,256]{1,0:T(8,128)S(1)} %get-tuple-element.25), channel_id=1, source_target_pairs={{25,15},{18,20},{11,29},{4,2},{29,11},{22,16},{15,25},{0,4}} | collective-permute-start | bytes 1572872 | tf_op jit(solution)/shard_map/ppermute | solution.py:116
  22.3 14.8 %collective-permute-start.16 = (f32[256,256]{1,0:T(8,128)S(1)}, f32[256,256]{1,0:T(8,128)S(1)}, u32[]{:S(2)}, u32[]{:S(2)}) collective-permute-start(f32[256,256]{1,0:T(8,128)S(1)} %shard_map.56.refs_0_), channel_id=1, source_target_pairs={{7,15},{21,29},{3,11},{17,25},{5,13},{23,31},{1,9},{19,27}} | collective-permute-start | bytes 786440 | tf_op jit(solution)/shard_map/ppermute | solution.py:116
  23.0 16.0 %collective-permute-start.15 = (f32[256,256]{1,0:T(8,128)S(1)}, f32[256,256]{1,0:T(8,128)S(1)}, u32[]{:S(2)}, u32[]{:S(2)}) collective-permute-start(f32[256,256]{1,0:T(8,128)S(1)} %shard_map.56.refs_0_), channel_id=1, source_target_pairs={{19,20},{1,2},{23,16}} | collective-permute-start | bytes 786440 | tf_op jit(solution)/shard_map/ppermute | solution.py:116
  23.7 15.4 %collective-permute-start.9 = (f32[256,256]{1,0:T(8,128)S(1)}, f32[256,256]{1,0:T(8,128)S(1)}, u32[]{:S(2)}, u32[]{:S(2)}) collective-permute-start(f32[256,256]{1,0:T(8,128)S(1)} %shard_map.56.refs_0_), channel_id=1, source_target_pairs={{17,23},{24,30},{5,3},{12,10},{23,21},{30,28},{1,7},{8,14},{19,17}... | collective-permute-start | bytes 786440 | tf_op jit(solution)/shard_map/ppermute | solution.py:116
  30.6 23.0 %collective-permute-start.25 = (f32[512,256]{1,0:T(8,128)S(1)}, f32[512,256]{1,0:T(8,128)S(1)}, u32[]{:S(2)}, u32[]{:S(2)}) collective-permute-start(f32[512,256]{1,0:T(8,128)S(1)} %get-tuple-element.28), channel_id=1, source_target_pairs={{15,23},{22,30},{23,31}} | collective-permute-start | bytes 1572872 | tf_op jit(solution)/shard_map/ppermute | solution.py:116
  31.9 11.7 %collective-permute-start.7 = (f32[256,256]{1,0:T(8,128)S(1)}, f32[256,256]{1,0:T(8,128)S(1)}, u32[]{:S(2)}, u32[]{:S(2)}) collective-permute-start(f32[256,256]{1,0:T(8,128)S(1)} %shard_map.56.refs_0_), channel_id=1, source_target_pairs={{3,7},{10,14},{17,21},{24,28},{5,1},{12,8},{23,19},{30,26},{1,5},{... | collective-permute-start | bytes 786440 | tf_op jit(solution)/shard_map/ppermute | solution.py:116
  37.1 9.5 %collective-permute-start.5 = (f32[256,256]{1,0:T(8,128)S(1)}, f32[256,256]{1,0:T(8,128)S(1)}, u32[]{:S(2)}, u32[]{:S(2)}) collective-permute-start(f32[256,256]{1,0:T(8,128)S(1)} %shard_map.56.refs_0_), channel_id=1, source_target_pairs={{21,23},{28,30},{3,5},{10,12},{17,19},{24,26},{5,7},{12,14},{23,17... | collective-permute-start | bytes 786440 | tf_op jit(solution)/shard_map/ppermute | solution.py:116
  39.0 32.3 %collective-permute-start.24 = (f32[1024,256]{1,0:T(8,128)S(1)}, f32[1024,256]{1,0:T(8,128)S(1)}, u32[]{:S(2)}, u32[]{:S(2)}) collective-permute-start(f32[1024,256]{1,0:T(8,128)S(1)} %get-tuple-element.27), channel_id=1, source_target_pairs={{24,0},{25,1},{26,2},{27,3},{28,4},{29,5},{30,6},{31,7},{0,8},{1,9... | collective-permute-start | bytes 3145736 | tf_op jit(solution)/shard_map/ppermute | solution.py:116
  39.1 8.8 %collective-permute-start.4 = (f32[256,256]{1,0:T(8,128)S(1)}, f32[256,256]{1,0:T(8,128)S(1)}, u32[]{:S(2)}, u32[]{:S(2)}) collective-permute-start(f32[256,256]{1,0:T(8,128)S(1)} %shard_map.56.refs_0_), channel_id=1, source_target_pairs={{7,6},{14,15},{21,20},{28,29},{3,2},{10,11},{17,16},{24,25},{5,4},... | collective-permute-start | bytes 786440 | tf_op jit(solution)/shard_map/ppermute | solution.py:116
  43.6 10.7 %collective-permute-start.10 = (f32[256,256]{1,0:T(8,128)S(1)}, f32[256,256]{1,0:T(8,128)S(1)}, u32[]{:S(2)}, u32[]{:S(2)}) collective-permute-start(f32[256,256]{1,0:T(8,128)S(1)} %collective-permute-done.9.refs_6_), channel_id=1, source_target_pairs={{23,22},{30,31},{3,2},{10,11},{21,20},{28,29},{7,6},{14,15},{17,16... | collective-permute-start | bytes 786440 | tf_op jit(solution)/shard_map/ppermute | solution.py:116
  46.6 8.4 %collective-permute-start.8 = (f32[256,256]{1,0:T(8,128)S(1)}, f32[256,256]{1,0:T(8,128)S(1)}, u32[]{:S(2)}, u32[]{:S(2)}) collective-permute-start(f32[256,256]{1,0:T(8,128)S(1)} %collective-permute-done.7.refs_4_), channel_id=1, source_target_pairs={{7,6},{14,15},{21,20},{28,29},{1,0},{8,9},{19,18},{26,27},{5,4},{1... | collective-permute-start | bytes 786440 | tf_op jit(solution)/shard_map/ppermute | solution.py:116
  47.9 7.8 %collective-permute-start.6 = (f32[256,256]{1,0:T(8,128)S(1)}, f32[256,256]{1,0:T(8,128)S(1)}, u32[]{:S(2)}, u32[]{:S(2)}) collective-permute-start(f32[256,256]{1,0:T(8,128)S(1)} %collective-permute-done.5.refs_2_), channel_id=1, source_target_pairs={{23,22},{30,31},{5,4},{12,13},{19,18},{26,27},{7,6},{14,15},{17,16... | collective-permute-start | bytes 786440 | tf_op jit(solution)/shard_map/ppermute | solution.py:116
  50.3 10.7 %copy-start.1 = (f32[4,1,256,2,1,256]{5,4,3,2,1,0:T(1,128)S(1)}, f32[4,1,256,2,1,256]{5,4,3,2,1,0:T(1,128)}, u32[]{:S(2)}) copy-start(f32[4,1,256,2,1,256]{5,4,3,2,1,0:T(1,128)} %param.6) | copy-start | bytes 6291460
  53.7 3.4 %collective-permute-start.22 = (f32[256,256]{1,0:T(8,128)S(1)}, f32[256,256]{1,0:T(8,128)S(1)}, u32[]{:S(2)}, u32[]{:S(2)}) collective-permute-start(f32[256,256]{1,0:T(8,128)S(1)} %shard_map.59.refs_0_), channel_id=1, source_target_pairs={{20,18},{2,0},{16,22},{25,31},{4,2},{13,11},{31,29},{9,15},{27,25}} | collective-permute-start | bytes 786440 | tf_op jit(solution)/shard_map/ppermute | solution.py:116
  54.4 4.0 %collective-permute-start.20 = (f32[256,256]{1,0:T(8,128)S(1)}, f32[256,256]{1,0:T(8,128)S(1)}, u32[]{:S(2)}, u32[]{:S(2)}) collective-permute-start(f32[256,256]{1,0:T(8,128)S(1)} %shard_map.59.refs_0_), channel_id=1, source_target_pairs={{20,16},{2,6},{11,15},{16,20},{25,29},{4,0},{13,9},{31,27},{9,13},... | collective-permute-start | bytes 786440 | tf_op jit(solution)/shard_map/ppermute | solution.py:116
  55.1 4.6 %collective-permute-start.18 = (f32[256,256]{1,0:T(8,128)S(1)}, f32[256,256]{1,0:T(8,128)S(1)}, u32[]{:S(2)}, u32[]{:S(2)}) collective-permute-start(f32[256,256]{1,0:T(8,128)S(1)} %shard_map.59.refs_0_), channel_id=1, source_target_pairs={{20,22},{29,31},{2,4},{11,13},{16,18},{25,27},{4,6},{13,15},{31,25... | collective-permute-start | bytes 786440 | tf_op jit(solution)/shard_map/ppermute | solution.py:116
  55.7 15.6 %collective-permute-start.17 = (f32[256,256]{1,0:T(8,128)S(1)}, f32[256,256]{1,0:T(8,128)S(1)}, u32[]{:S(2)}, u32[]{:S(2)}) collective-permute-start(f32[256,256]{1,0:T(8,128)S(1)} %shard_map.59.refs_0_), channel_id=1, source_target_pairs={{20,21},{2,3},{16,17},{4,5},{13,12},{31,30},{9,8},{27,26}} | collective-permute-start | bytes 786440 | tf_op jit(solution)/shard_map/ppermute | solution.py:116
  57.1 17.1 %collective-permute-start.23 = (f32[256,256]{1,0:T(8,128)S(1)}, f32[256,256]{1,0:T(8,128)S(1)}, u32[]{:S(2)}, u32[]{:S(2)}) collective-permute-start(f32[256,256]{1,0:T(8,128)S(1)} %collective-permute-done.22.refs_6_), channel_id=1, source_target_pairs={{18,19},{0,1},{22,23},{31,30},{2,3},{11,10},{29,28},{15,14},{25,24}} | collective-permute-start | bytes 786440 | tf_op jit(solution)/shard_map/ppermute | solution.py:116
  58.4 18.6 %collective-permute-start.21 = (f32[256,256]{1,0:T(8,128)S(1)}, f32[256,256]{1,0:T(8,128)S(1)}, u32[]{:S(2)}, u32[]{:S(2)}) collective-permute-start(f32[256,256]{1,0:T(8,128)S(1)} %collective-permute-done.20.refs_4_), channel_id=1, source_target_pairs={{16,17},{6,7},{15,14},{20,21},{29,28},{0,1},{9,8},{27,26},{13,12},... | collective-permute-start | bytes 786440 | tf_op jit(solution)/shard_map/ppermute | solution.py:116
  59.7 20.1 %collective-permute-start.19 = (f32[256,256]{1,0:T(8,128)S(1)}, f32[256,256]{1,0:T(8,128)S(1)}, u32[]{:S(2)}, u32[]{:S(2)}) collective-permute-start(f32[256,256]{1,0:T(8,128)S(1)} %collective-permute-done.18.refs_2_), channel_id=1, source_target_pairs={{22,23},{31,30},{4,5},{13,12},{18,19},{27,26},{6,7},{15,14},{25,24... | collective-permute-start | bytes 786440 | tf_op jit(solution)/shard_map/ppermute | solution.py:116

commit v3 on v0

v3 whole, which is shorter than its diff:
```python
import numpy as np
import jax
import jax.numpy as jnp
from jax import lax
from jax.experimental import pallas as pl
from jax.experimental.pallas import tpu as pltpu
from jax.sharding import PartitionSpec as P

AXES = ("row", "col")
LANES = 128
LIMIT = 40 * 1024 * 1024
GATE_SECOND = "none"
GATE_SPREAD = "next"
GATE_PANEL = "next"


def product(first, second, dims=((1,), (0,))):
    return lax.dot_general(
        first,
        second,
        (dims, ((), ())),
        precision=lax.Precision.HIGHEST,
        preferred_element_type=jnp.float32,
    )


class Plan:
    line = 4

    def __init__(self, rows, cols, block_rows, block_cols):
        self.rows, self.cols = rows, cols
        self.count = block_rows * rows
        assert block_rows == 4 and block_cols == 2 and self.count == block_cols * cols
        self.stride = cols // self.line

    def within(self, r):
        return r % (self.rows // 2) == 0

    def sign(self, r):
        return 1 - 2 * ((2 * r) // self.rows)

    def solver(self, r, p):
        order = 2 * (p % 2) + p // 2
        return (self.cols - 1 - r - self.sign(r) * order * self.stride) % self.cols

    def solves(self, r, c):
        return c % self.stride == (self.cols - 1 - r) % self.stride

    def local_row(self, r, c):
        order = (self.sign(r) * (self.cols - 1 - r - c)) % self.cols // self.stride
        return 2 * (order % 2) + order // 2

    def local_at(self, d, c, q):
        return (d - q * self.cols - c) // self.rows

    def shift(self, c, by):
        return (c + by * self.stride) % self.cols

    def step(self, c, by):
        return c // self.stride * self.stride + (c + by) % self.stride


def solution(mesh):
    rows, cols = mesh.shape["row"], mesh.shape["col"]
    plan = Plan(rows, cols, 4, 2)
    count, line, stride = plan.count, plan.line, plan.stride
    devices = [(r, c) for r in range(rows) for c in range(cols)]
    first = {(r, c): plan.local_row(r, c) * rows + r for r, c in devices if plan.solves(r, c)}
    assert sorted(first.values()) == list(range(count))
    assert all(plan.solver(r, k // rows) == c for (r, c), k in first.items())
    second = {
        device: k
        for device, k in first.items()
        if not (plan.within(device[0]) and (k == 0 or 2 * k > count))
    }

    def send(value, moves):
        assert len({s for s, _ in moves}) == len(moves) == len({t for _, t in moves})
        return lax.ppermute(value, AXES, [(s[0] * cols + s[1], t[0] * cols + t[1]) for s, t in moves])

    def after(value, *others):
        return lax.optimization_barrier((value, *others))[0] if others else value

    def operand_moves(d, solving):
        hand, mirror = ([], []), ([], [])
        for device, k in solving.items():
            for moves, i in ((hand, k), (mirror, d - k)):
                owner = (i % rows, (d - i) % cols)
                assert plan.local_at(d, owner[1], (d - i) // cols) == i // rows
                if owner != device:
                    moves[(d - i) // cols].append((owner, device))
                else:
                    assert moves is hand and d < count and i // rows < 2
        return hand, mirror

    hand_first, mirror_first = operand_moves(count - 1, first)
    assert not hand_first[1]
    hand_second, mirror_second = operand_moves(count, second)
    far_first = [((rows - 1 - r, c), (r, c)) for r, c in first]
    far_second = [((-r % rows, c), (r, c)) for r, c in second if not plan.within(r)]

    def solver_of(k):
        return (k % rows, plan.solver(k % rows, k // rows))

    beside = [(solver_of(k - 1), device) for device, k in second.items() if not plan.within(device[0])]
    for (r, c), k in second.items():
        if plan.within(r) and 2 * k != count:
            assert solver_of(count - k) == (r, plan.shift(c, -1))

    def wants(k, d, c):
        return d - k < count and cols + c >= d - k

    def uses(k, d, device):
        r, c = device
        return wants(k, d, c) or (d == count and plan.within(r) and wants(d - k, d, c))

    def spread_moves(d, solving):
        shifts, steps = [], {}
        for by in range(1, line):
            moves = []
            for (r, c), k in solving.items():
                at = plan.shift(c, by)
                group = [(r, plan.step(at, step)) for step in range(stride)]
                direct = d < count and by == 1 and second.get((r, at)) == count - k
                if direct or any(uses(k, d, device) for device in group):
                    moves.append(((r, c), (r, at)))
            shifts.append(moves)
        for by in range(line):
            for step in range(1, stride):
                moves = []
                for (r, c), k in solving.items():
                    at = plan.shift(c, by)
                    target = (r, plan.step(at, step))
                    if uses(k, d, target):
                        moves.append(((r, at), target))
                steps[by, step] = moves
        return shifts, steps

    shifts_first, steps_first = spread_moves(count - 1, first)
    shifts_second, steps_second = spread_moves(count, second)

    def reached(device, p, q):
        k = p * rows + device[0]
        return 0 < k and q * cols + device[1] > count - k

    slots = [(p, q) for p in range(4) for q in range(2)]
    common = [s for s in slots if reached((rows // 2, cols // 2), *s)]
    seldom = [s for s in slots if s not in common and any(reached(device, *s) for device in devices)]

    def panel_moves(chosen):
        return [
            (((r - 1) % rows, c), (r, c)) for r, c in devices if any(reached((r, c), *s) for s in chosen)
        ]

    def local(reversed_rows, state, basis, eigval):
        width = state.shape[2]
        halves = width // LANES
        stripe = 2 * halves
        slab = width * stripe
        running = state.reshape(4 * slab, LANES)
        panel = reversed_rows.reshape(4 * slab, LANES)
        own_basis = basis.reshape(4, width, width)
        own_values = eigval.reshape(4 * halves, LANES)
        block_shape = jax.ShapeDtypeStruct((width, width), jnp.float32)
        pair_shape = jax.ShapeDtypeStruct((2 * width, width), jnp.float32)
        eigen_shape = jax.ShapeDtypeStruct((width + 8, width), jnp.float32)
        vmem = pl.BlockSpec(memory_space=pltpu.VMEM)
        hbm = pl.BlockSpec(memory_space=pltpu.HBM)

        def where_at(p, q, half):
            return pl.ds(p * slab + q * halves + half, width, stride=stripe)

        def joined(parts):
            return jnp.concatenate(parts, axis=1) if halves > 1 else parts[0]

        def read(ref, p, q):
            return joined([ref[where_at(p, q, half), :] for half in range(halves)])

        def write(ref, p, q, value):
            for half in range(halves):
                ref[where_at(p, q, half), :] = value[:, half * LANES : (half + 1) * LANES]

        def values_at(ref, p):
            return joined([ref[pl.ds(p * halves + half, 1), :] for half in range(halves)])

        def here():
            return lax.axis_index("row"), lax.axis_index("col")

        def call(body, outputs, operands, specs=None, scratch=(), flops=0):
            moved = sum(4 * int(np.prod(o.shape)) for o in (*operands, *outputs))
            return pl.pallas_call(
                body,
                out_shape=outputs,
                in_specs=specs or [vmem] * len(operands),
                out_specs=[vmem] * len(outputs),
                scratch_shapes=scratch,
                compiler_params=pltpu.CompilerParams(vmem_limit_bytes=LIMIT),
                cost_estimate=pl.CostEstimate(flops=flops, bytes_accessed=moved, transcendentals=0),
            )(*operands)

        def local_at(d, c, q):
            return jnp.clip(plan.local_at(d, c, q), 0, 3)

        def pack_first(state_ref, basis_ref, values_ref, upper, lower, far, slabs, values, sems):
            r, c = here()
            index = 3 - plan.local_row(rows - 1 - r, c)
            places = [local_at(count - 1, c, q) for q in range(2)]
            copies = [
                pltpu.make_async_copy(
                    state_ref.at[pl.ds(pl.multiple_of(places[q] * slab, slab), slab)], slabs.at[q], sems.at[q]
                )
                for q in (1, 0)
            ]
            copies.append(pltpu.make_async_copy(basis_ref.at[index], far.at[pl.ds(0, width)], sems.at[2]))
            copies.append(pltpu.make_async_copy(values_ref, values, sems.at[3]))
            for copy in copies:
                copy.start()
            copies[0].wait()
            upper[...] = read(slabs.at[1], 0, 1)
            copies[1].wait()
            lower[...] = read(slabs.at[0], 0, 0)
            copies[3].wait()
            far[width:, :] = jnp.broadcast_to(values_at(values, index), (8, width))
            copies[2].wait()

        def pack_second(state_ref, panel_ref, basis_ref, values_ref, upper, lower, far, often, rarely):
            r, c = here()
            for target, q in ((upper, 1), (lower, 0)):
                p = local_at(count, c, q)
                target[:width, :] = read(state_ref, p, q)
                target[width:, :] = read(panel_ref, p, q)
            opposite = lax.rem(rows - r, rows)
            k = plan.local_row(opposite, c) * rows + opposite
            index = jnp.clip((count - k) // rows, 0, 3)
            far[:width, :] = basis_ref[index]
            far[width:, :] = jnp.broadcast_to(values_at(values_ref, index), (8, width))
            last = (r == rows - 1).astype(jnp.int32)
            for target, chosen in ((often, common), (rarely, seldom)):
                for index, (p, q) in enumerate(chosen):
                    source = jnp.maximum(p - last, 0)
                    target[index * width : (index + 1) * width, :] = read(panel_ref, source, q)

        def column(values):
            return jnp.broadcast_to(values, (width, width)).T

        def solve(right_side, near, near_values, far, far_values):
            inner = product(near.T, right_side)
            inner = product(inner, far)
            inner = inner / (column(near_values) + far_values)
            return product(product(near, inner), far, ((1,), (1,)))

        def solve_first(upper, hand, mirror0, mirror1, far, basis_ref, values_ref, out):
            r, c = here()
            p = plan.local_row(r, c)
            solves = plan.solves(r, c)
            own = jnp.where(solves & (p < 2), upper[...], 0.0) + hand[...]
            right_side = own + (mirror0[...] + mirror1[...]).T
            found = solve(
                right_side,
                basis_ref[p],
                values_at(values_ref, p),
                far[:width, :],
                far[width : width + 1, :],
            )
            out[...] = jnp.where(solves, found, 0.0)

        def solve_second(
            hand0, hand1, mirror0, mirror1, far, left, shifted, beside_ref, basis_ref, values_ref, out
        ):
            r, c = here()
            p = plan.local_row(r, c)
            k = p * rows + r
            within = plan.within(r)
            halfway = 2 * k == count
            top, bottom = slice(0, width), slice(width, 2 * width)
            turned = jnp.where(halfway, left[...], shifted[...]).T
            right = jnp.where(within, turned, beside_ref[...])
            own_side = hand0[top, :] + hand1[top, :]
            own_side = own_side - product(left[...], hand0[bottom, :] + hand1[bottom, :])
            across = (mirror0[bottom, :] + mirror1[bottom, :]).T
            mirror_side = (mirror0[top, :] + mirror1[top, :]).T - product(across, right)
            far_index = jnp.clip((count - k) // rows, 0, 3)
            far_basis = jnp.where(within, basis_ref[far_index], far[:width, :])
            far_values = jnp.where(within, values_at(values_ref, far_index), far[width : width + 1, :])
            found = solve(
                own_side + mirror_side, basis_ref[p], values_at(values_ref, p), far_basis, far_values
            )
            idle = within & ((k == 0) | (2 * k > count))
            out[...] = jnp.where(plan.solves(r, c) & jnp.logical_not(idle), found, 0.0)

        def update(d, running, arrived, sources, rows_of_a):
            def body(running_ref, *refs):
                r, c = here()
                parts, given = refs[: len(arrived)], refs[len(arrived) : -2]
                out, blocks = refs[-2], refs[-1]
                for by in range(line):
                    total = parts[by * stride][...]
                    for step in range(1, stride):
                        total = total + parts[by * stride + step][...]
                    blocks[by] = total
                for p in range(4):
                    k = p * rows + r
                    partner = d - k
                    turned = plan.within(r) & (2 * k > count)
                    if d < count:
                        turned = jnp.bool_(False)
                    solved_row = jnp.where(turned, jnp.clip(partner // rows, 0, 3), p)
                    index = (c // stride - plan.solver(r, solved_row) // stride) % line

                    def block():
                        found = blocks[index]
                        return found if d < count else jnp.where(turned, found.T, found)

                    for q in range(2):
                        at = q * cols + c
                        old = read(running_ref, p, q)
                        write(out, p, q, old)
                        a_block = rows_of_a(given, p, q)
                        if a_block is not None:

                            @pl.when((at > partner) & (partner < count))
                            def _():
                                write(out, p, q, old - product(block(), a_block()))

                        @pl.when(at == partner)
                        def _():
                            write(out, p, q, block())

            return call(
                body,
                [jax.ShapeDtypeStruct(running.shape, jnp.float32)],
                (running, *arrived, *sources),
                scratch=[pltpu.VMEM((line, width, width), jnp.float32)],
                flops=16 * width**3 * 6,
            )[0]

        def own_rows(given, p, q):
            return lambda: read(given[0], p, q)

        def next_rows(given, p, q):
            for ref, chosen in zip(given, (common, seldom)):
                if (p, q) in chosen:
                    at = chosen.index((p, q)) * width
                    return lambda: ref[at : at + width, :]
            return None

        def forwarded(blocks, steps):
            arrived = []
            for by in range(line):
                arrived.append(blocks[by])
                for step in range(1, stride):
                    arrived.append(send(blocks[by], steps[by, step]))
            return arrived

        solve_flops = 4 * 2 * 6 * width**3

        upper, lower, far = call(
            pack_first,
            [block_shape, block_shape, eigen_shape],
            (running, own_basis, own_values),
            specs=[hbm, hbm, hbm],
            scratch=[
                pltpu.VMEM((2, slab, LANES), jnp.float32),
                pltpu.VMEM((4 * halves, LANES), jnp.float32),
                pltpu.SemaphoreType.DMA((4,)),
            ],
        )
        mirror1 = send(upper, mirror_first[1])
        mirror0 = send(lower, mirror_first[0])
        far = send(far, far_first)
        hand = send(lower, hand_first[0])

        gates = {"none": (), "hand": (hand,), "far": (far,), "all": (hand, far, mirror0, mirror1)}[GATE_SECOND]
        later = call(
            pack_second,
            [pair_shape, pair_shape, eigen_shape]
            + [jax.ShapeDtypeStruct((len(s) * width, width), jnp.float32) for s in (common, seldom)],
            (after(running, *gates), panel, own_basis, own_values),
        )
        hands = [send(later[1], hand_second[0]), send(later[0], hand_second[1])]
        mirrors = [send(later[1], mirror_second[0]), send(later[0], mirror_second[1])]
        far_later = send(later[2], far_second)

        (solved,) = call(
            solve_first,
            [block_shape],
            (upper, hand, mirror0, mirror1, far, own_basis, own_values),
            flops=solve_flops,
        )

        next_to = send(solved, beside)
        shifted = send(solved, shifts_first[0])
        (solved_next,) = call(
            solve_second,
            [block_shape],
            (*hands, *mirrors, far_later, solved, shifted, next_to, own_basis, own_values),
            flops=solve_flops + solve_flops // 2,
        )
        options = {"none": (), "beside": (next_to,), "both": (next_to, shifted), "next": (solved_next,)}
        held = after(solved, *options[GATE_SPREAD])
        blocks = [held, shifted, send(held, shifts_first[1]), send(held, shifts_first[2])]
        often = send(after(later[3], *options[GATE_PANEL]), panel_moves(common))
        rarely = send(after(later[4], *options[GATE_PANEL]), panel_moves(seldom))
        arrived = forwarded(blocks, steps_first)
        running = update(count - 1, running, arrived, [panel], own_rows)

        blocks = [solved_next] + [send(solved_next, moves) for moves in shifts_second]
        arrived = forwarded(blocks, steps_second)
        running = update(count, running, arrived, [often, rarely], next_rows)
        return running.reshape(state.shape)

    placed = (
        P(None, "row", None, None, "col", None),
        P(None, "row", None, None, "col", None),
        P(None, "row", None, None),
        P(None, "row", None),
    )
    return jax.shard_map(
        local,
        mesh=mesh,
        in_specs=placed,
        out_specs=P(None, "row", None, None, "col", None),
        check_vma=False,
    )
```

time: 562 us -> 89.5 us (0.16)
  waiting for transfers between devices: 420 us -> 16 us
  between operations: 42.1 us -> 0.41 us
  local copies, waits for them, and re-layouts: 37.2 us -> 3.52 us
  starting transfers between devices: 26.7 us -> 55.7 us
  matrix products: 15.9 us -> 0 us
  other arithmetic: 14.7 us -> 0 us
  Pallas kernels: 0 us -> 12.4 us
    ppermute x31 -> x26, waiting for transfers between devices: 279 us -> 16 us  [send(): lax.ppermute(value, AXES, [(s[0] * cols + s[1], t[0] * cols + t[1]) for s...]
    psum x2 -> x0, waiting for transfers between devices: 141 us -> none  [broadcast(): return lax.psum(block, axis)]
    ppermute x31 -> x26, starting transfers between devices: 26.7 us -> 55.7 us  [send(): lax.ppermute(value, AXES, [(s[0] * cols + s[1], t[0] * cols + t[1]) for s...]
    dot_general x10 -> x0, matrix products: 15.9 us -> none  [batched(): jnp.einsum(einsum_form, first, second, precision=lax.Precision.HIGHEST, p...]
    pallas_call x0 -> x6, Pallas kernels: none -> 12.4 us  [call(): pl.pallas_call(body, out_shape=outputs, in_specs=specs or [vmem] * len(op...]
    select_n x11 -> x0, other arithmetic: 11 us -> none  [the longest x3 6.38 us: next_rows(): jnp.where(first_row, jnp.concatenate([jnp.zeros_like(member[:1]), member[...]
    slice x16 -> x0, local copies, waits for them, and re-layouts: 9.81 us -> none  [the longest x2 3.13 us: next_rows(): member[:-1]]
    gather x8 -> x0, local copies, waits for them, and re-layouts: 7.8 us -> none  [the longest x2 3.17 us: local(): far_basis[local_rows]]
  transfers between devices with their start and end apart: 33 -> 26, of which waited for: 27 -> 8; matrix products, arithmetic and copies ran while one was open for 5% -> 0% of each run, Pallas kernels for 0% -> 6%
where the time goes in v3:
time: 89.5 us; the launch traced here: 88.1 us
  starting transfers between devices  55.7 us (62%)
  waiting for transfers between devices  16 us (18%)
  Pallas kernels  12.4 us (14%)
  local copies, waits for them, and re-layouts  3.52 us (4%)
    ppermute x26, starting transfers between devices, send(): lax.ppermute(value, AXES, [(s[0] * cols + s[1], t[0] * cols + t[1]) for s...  55.7 us
    ppermute x26, waiting for transfers between devices, send(): lax.ppermute(value, AXES, [(s[0] * cols + s[1], t[0] * cols + t[1]) for s...  16 us
    pallas_call x6, Pallas kernels, call(): pl.pallas_call(body, out_shape=outputs, in_specs=specs or [vmem] * len(op...  12.4 us
    unnamed x14, local copies, waits for them, and re-layouts  3.52 us
  transfers between devices with their start and end apart: 26, of which 8 were waited for; matrix products, arithmetic and copies ran while one was open for 0% of the time, Pallas kernels for 6%

profile of v3, /device:TPU:29, one launch (start us, length us, event | category | flops | bytes accessed | tf_op | source)
XLA Modules:
  0.0 88.1 jit_solution(7244124282497745969)
XLA Ops:
  0.0 1.6 %copy-done = f32[4,1,256,2,1,256]{5,4,3,2,1,0:T(1,128)S(1)} copy-done((f32[4,1,256,2,1,256]{5,4,3,2,1,0:T(1,128)S(1)}, f32[4,1,256,2,1,256]{5,4,3,2,1,0:T(1,128)}, u32[]{:S(2)}) %copy-start) | copy-done | bytes 2097176
  1.6 1.2 %copy-done.3 = f32[4,1,256,256]{3,2,1,0:T(8,128)S(1)} copy-done((f32[4,1,256,256]{3,2,1,0:T(8,128)S(1)}, f32[4,1,256,256]{3,2,1,0:T(8,128)}, u32[]{:S(2)}) %copy-start.3) | copy-done | bytes 1048600
  2.8 0.7 copy-done.5
  3.5 0.2 shard_map.46
  3.7 1.4 %collective-permute-start.2 = (f32[256,256]{1,0:T(8,128)S(1)}, f32[256,256]{1,0:T(8,128)S(1)}, u32[]{:S(2)}, u32[]{:S(2)}) collective-permute-start(f32[256,256]{1,0:T(8,128)S(1)} %get-tuple-element.16.upper), channel_id=1, source_target_pairs={{28,1},{24,5},{21,8},{17,12},{14,19},{10,23},{7,26},{3,30}} | collective-permute-start | bytes 786440 | tf_op jit(solution)/shard_map/ppermute | solution.py:79
  5.1 1.3 %collective-permute-start.3 = (f32[264,256]{1,0:T(8,128)S(1)}, f32[264,256]{1,0:T(8,128)S(1)}, u32[]{:S(2)}, u32[]{:S(2)}) collective-permute-start(f32[264,256]{1,0:T(8,128)S(1)} %get-tuple-element.18), channel_id=1, source_target_pairs={{25,1},{27,3},{29,5},{31,7},{16,8},{18,10},{20,12},{22,14},{9,17},... | collective-permute-start | bytes 811016 | tf_op jit(solution)/shard_map/ppermute | solution.py:79
  6.4 0.7 collective-permute-start.1
  7.1 1.3 %collective-permute-start = (f32[256,256]{1,0:T(8,128)S(1)}, f32[256,256]{1,0:T(8,128)S(1)}, u32[]{:S(2)}, u32[]{:S(2)}) collective-permute-start(f32[256,256]{1,0:T(8,128)S(1)} %get-tuple-element.17), channel_id=1, source_target_pairs={{3,1},{7,5},{10,8},{14,12},{17,19},{21,23},{24,26},{28,30}} | collective-permute-start | bytes 786440 | tf_op jit(solution)/shard_map/ppermute | solution.py:79
  8.4 0.0 copy-start.4
  8.4 0.2 shard_map.48
  8.7 0.0 copy-start.6
  8.7 0.8 collective-permute-start.6
  9.5 4.8 %collective-permute-done.2.mirror1 = f32[256,256]{1,0:T(8,128)S(1)} collective-permute-done((f32[256,256]{1,0:T(8,128)S(1)}, f32[256,256]{1,0:T(8,128)S(1)}, u32[]{:S(2)}, u32[]{:S(2)}) %collective-permute-start.2) | collective-permute-done | bytes 262176 | tf_op jit(solution)/shard_map/ppermute | solution.py:79
  14.3 4.1 %collective-permute-start.8 = (f32[264,256]{1,0:T(8,128)S(1)}, f32[264,256]{1,0:T(8,128)S(1)}, u32[]{:S(2)}, u32[]{:S(2)}) collective-permute-start(f32[264,256]{1,0:T(8,128)S(1)} %get-tuple-element.21), channel_id=1, source_target_pairs={{24,8},{26,10},{28,12},{30,14},{8,24},{10,26},{12,28},{14,30}} | collective-permute-start | bytes 811016 | tf_op jit(solution)/shard_map/ppermute | solution.py:79
  18.4 0.0 collective-permute-done.1.mirror0
  18.5 1.3 %collective-permute-start.4 = (f32[512,256]{1,0:T(8,128)S(1)}, f32[512,256]{1,0:T(8,128)S(1)}, u32[]{:S(2)}, u32[]{:S(2)}) collective-permute-start(f32[512,256]{1,0:T(8,128)S(1)} %get-tuple-element.19), channel_id=1, source_target_pairs={{11,8},{15,12},{25,26},{29,30}} | collective-permute-start | bytes 1572872 | tf_op jit(solution)/shard_map/ppermute | solution.py:79
  19.8 1.1 %collective-permute-done.hand = f32[256,256]{1,0:T(8,128)S(1)} collective-permute-done((f32[256,256]{1,0:T(8,128)S(1)}, f32[256,256]{1,0:T(8,128)S(1)}, u32[]{:S(2)}, u32[]{:S(2)}) %collective-permute-start) | collective-permute-done | bytes 262176 | tf_op jit(solution)/shard_map/ppermute | solution.py:79
  20.9 1.3 %collective-permute-start.7 = (f32[512,256]{1,0:T(8,128)S(1)}, f32[512,256]{1,0:T(8,128)S(1)}, u32[]{:S(2)}, u32[]{:S(2)}) collective-permute-start(f32[512,256]{1,0:T(8,128)S(1)} %get-tuple-element.20), channel_id=1, source_target_pairs={{0,5},{29,8},{25,12},{15,26},{11,30}} | collective-permute-start | bytes 1572872 | tf_op jit(solution)/shard_map/ppermute | solution.py:79
  22.2 0.7 collective-permute-start.5
  22.9 2.1 %shard_map.47.left.refs_0_ = f32[256,256]{1,0:T(8,128)S(1)} custom-call(f32[256,256]{1,0:T(8,128)S(1)} %get-tuple-element.16.upper, f32[256,256]{1,0:T(8,128)S(1)} %collective-permute-done.hand, f32[256,256]{1,0:T(8,128)S(1)} %collective-permute-done.1.mirror0, f32[256,256]{1,0:T(8,128)S(1)} %collective-permute-done.2.mirror1, ...), custom_call_target="tpu_custom_call" | custom-call | flops 805306368 | bytes 2633728 | tf_op jit(solution)/shard_map/pallas_call | solution.py:191
  25.0 0.0 copy-start.1
  25.0 1.4 %collective-permute-start.10 = (f32[256,256]{1,0:T(8,128)S(1)}, f32[256,256]{1,0:T(8,128)S(1)}, u32[]{:S(2)}, u32[]{:S(2)}) collective-permute-start(f32[256,256]{1,0:T(8,128)S(1)} %shard_map.47.left.refs_0_), channel_id=1, source_target_pairs={{1,8},{3,10},{5,12},{7,14},{17,24},{19,26},{21,28},{23,30}} | collective-permute-start | bytes 786440 | tf_op jit(solution)/shard_map/ppermute | solution.py:79
  26.5 0.0 collective-permute-done.6.mirror0
  26.5 7.3 %collective-permute-start.9 = (f32[256,256]{1,0:T(8,128)S(1)}, f32[256,256]{1,0:T(8,128)S(1)}, u32[]{:S(2)}, u32[]{:S(2)}) collective-permute-start(f32[256,256]{1,0:T(8,128)S(1)} %shard_map.47.left.refs_0_), channel_id=1, source_target_pairs={{1,3},{3,5},{5,7},{8,10},{10,12},{12,14},{17,19},{19,21},{21,23},{... | collective-permute-start | bytes 786440 | tf_op jit(solution)/shard_map/ppermute | solution.py:79
  33.8 0.2 collective-permute-done.4.hand0
  34.0 2.7 %collective-permute-done.10.beside_ref = f32[256,256]{1,0:T(8,128)S(1)} collective-permute-done((f32[256,256]{1,0:T(8,128)S(1)}, f32[256,256]{1,0:T(8,128)S(1)}, u32[]{:S(2)}, u32[]{:S(2)}) %collective-permute-start.10) | collective-permute-done | bytes 262176 | tf_op jit(solution)/shard_map/ppermute | solution.py:79
  36.7 0.4 collective-permute-done.9.shifted.refs_2_
  37.1 2.7 %shard_map.49.refs_0_ = f32[256,256]{1,0:T(8,128)S(1)} custom-call(f32[512,256]{1,0:T(8,128)S(1)} %collective-permute-done.4.hand0, f32[512,256]{1,0:T(8,128)S(1)} %collective-permute-done.5.hand1, f32[512,256]{1,0:T(8,128)S(1)} %collective-permute-done.6.mirror0, f32[512,256]{1,0:T(8,128)S(1)} %collective-permute-done.7.mirror1, ...), custom_call_target="tpu_custom_call" | custom-call | flops 1207959552 | bytes 4468736 | tf_op jit(solution)/shard_map/pallas_call | solution.py:191
  39.8 1.3 %collective-permute-start.12 = (f32[256,256]{1,0:T(8,128)S(1)}, f32[256,256]{1,0:T(8,128)S(1)}, u32[]{:S(2)}, u32[]{:S(2)}) collective-permute-start(f32[256,256]{1,0:T(8,128)S(1)} %collective-permute-done.9.shifted.refs_2_), channel_id=1, source_target_pairs={{3,2},{5,4},{7,6},{10,11},{12,13},{14,15},{19,18},{21,20},{23,22},... | collective-permute-start | bytes 786440 | tf_op jit(solution)/shard_map/ppermute | solution.py:79
  41.2 7.4 %collective-permute-start.15 = (f32[256,256]{1,0:T(8,128)S(1)}, f32[256,256]{1,0:T(8,128)S(1)}, u32[]{:S(2)}, u32[]{:S(2)}) collective-permute-start(f32[256,256]{1,0:T(8,128)S(1)} %shard_map.47.left.refs_0_), channel_id=1, source_target_pairs={{1,7},{5,3},{8,14},{12,10},{17,23},{19,17},{23,21},{24,30},{26,24}... | collective-permute-start | bytes 786440 | tf_op jit(solution)/shard_map/ppermute | solution.py:79
  48.6 2.5 %collective-permute-start.13 = (f32[256,256]{1,0:T(8,128)S(1)}, f32[256,256]{1,0:T(8,128)S(1)}, u32[]{:S(2)}, u32[]{:S(2)}) collective-permute-start(f32[256,256]{1,0:T(8,128)S(1)} %shard_map.47.left.refs_0_), channel_id=1, source_target_pairs={{1,5},{3,7},{5,1},{8,12},{10,14},{12,8},{17,21},{19,23},{23,19},{2... | collective-permute-start | bytes 786440 | tf_op jit(solution)/shard_map/ppermute | solution.py:79
  51.1 0.1 collective-permute-start.24
  51.1 1.3 %collective-permute-start.11 = (f32[256,256]{1,0:T(8,128)S(1)}, f32[256,256]{1,0:T(8,128)S(1)}, u32[]{:S(2)}, u32[]{:S(2)}) collective-permute-start(f32[256,256]{1,0:T(8,128)S(1)} %shard_map.47.left.refs_0_), channel_id=1, source_target_pairs={{1,0},{5,4},{8,9},{10,11},{12,13},{14,15},{19,18},{23,22},{24,25},... | collective-permute-start | bytes 786440 | tf_op jit(solution)/shard_map/ppermute | solution.py:79
  52.4 5.0 %collective-permute-start.22 = (f32[256,256]{1,0:T(8,128)S(1)}, f32[256,256]{1,0:T(8,128)S(1)}, u32[]{:S(2)}, u32[]{:S(2)}) collective-permute-start(f32[256,256]{1,0:T(8,128)S(1)} %shard_map.49.refs_0_), channel_id=1, source_target_pairs={{3,1},{5,3},{8,14},{12,10},{17,23},{21,19},{24,30},{26,24},{30,28}} | collective-permute-start | bytes 786440 | tf_op jit(solution)/shard_map/ppermute | solution.py:79
  57.5 4.5 %collective-permute-start.20 = (f32[256,256]{1,0:T(8,128)S(1)}, f32[256,256]{1,0:T(8,128)S(1)}, u32[]{:S(2)}, u32[]{:S(2)}) collective-permute-start(f32[256,256]{1,0:T(8,128)S(1)} %shard_map.49.refs_0_), channel_id=1, source_target_pairs={{3,7},{5,1},{8,12},{10,14},{12,8},{17,21},{21,17},{24,28},{26,30},... | collective-permute-start | bytes 786440 | tf_op jit(solution)/shard_map/ppermute | solution.py:79
  62.0 1.9 %collective-permute-start.18 = (f32[256,256]{1,0:T(8,128)S(1)}, f32[256,256]{1,0:T(8,128)S(1)}, u32[]{:S(2)}, u32[]{:S(2)}) collective-permute-start(f32[256,256]{1,0:T(8,128)S(1)} %shard_map.49.refs_0_), channel_id=1, source_target_pairs={{3,5},{5,7},{8,10},{10,12},{12,14},{17,19},{21,23},{24,26},{26,28}... | collective-permute-start | bytes 786440 | tf_op jit(solution)/shard_map/ppermute | solution.py:79
  63.9 1.3 %collective-permute-start.17 = (f32[256,256]{1,0:T(8,128)S(1)}, f32[256,256]{1,0:T(8,128)S(1)}, u32[]{:S(2)}, u32[]{:S(2)}) collective-permute-start(f32[256,256]{1,0:T(8,128)S(1)} %shard_map.49.refs_0_), channel_id=1, source_target_pairs={{3,2},{5,4},{8,9},{10,11},{12,13},{14,15},{17,16},{21,20},{24,25},... | collective-permute-start | bytes 786440 | tf_op jit(solution)/shard_map/ppermute | solution.py:79
  65.3 1.3 %collective-permute-start.16 = (f32[256,256]{1,0:T(8,128)S(1)}, f32[256,256]{1,0:T(8,128)S(1)}, u32[]{:S(2)}, u32[]{:S(2)}) collective-permute-start(f32[256,256]{1,0:T(8,128)S(1)} %collective-permute-done.15.refs_6_), channel_id=1, source_target_pairs={{7,6},{3,2},{14,15},{10,11},{23,22},{17,16},{21,20},{30,31},{24,25... | collective-permute-start | bytes 786440 | tf_op jit(solution)/shard_map/ppermute | solution.py:79
  66.6 2.7 %collective-permute-done.20.refs_4_ = f32[256,256]{1,0:T(8,128)S(1)} collective-permute-done((f32[256,256]{1,0:T(8,128)S(1)}, f32[256,256]{1,0:T(8,128)S(1)}, u32[]{:S(2)}, u32[]{:S(2)}) %collective-permute-start.20) | collective-permute-done | bytes 262176 | tf_op jit(solution)/shard_map/ppermute | solution.py:79
  69.2 1.3 %collective-permute-start.14 = (f32[256,256]{1,0:T(8,128)S(1)}, f32[256,256]{1,0:T(8,128)S(1)}, u32[]{:S(2)}, u32[]{:S(2)}) collective-permute-start(f32[256,256]{1,0:T(8,128)S(1)} %collective-permute-done.13.refs_4_), channel_id=1, source_target_pairs={{5,4},{7,6},{1,0},{12,13},{14,15},{8,9},{21,20},{23,22},{19,18},{2... | collective-permute-start | bytes 786440 | tf_op jit(solution)/shard_map/ppermute | solution.py:79
  70.5 1.6 %collective-permute-done.18.refs_2_ = f32[256,256]{1,0:T(8,128)S(1)} collective-permute-done((f32[256,256]{1,0:T(8,128)S(1)}, f32[256,256]{1,0:T(8,128)S(1)}, u32[]{:S(2)}, u32[]{:S(2)}) %collective-permute-start.18) | collective-permute-done | bytes 262176 | tf_op jit(solution)/shard_map/ppermute | solution.py:79
  72.1 1.3 %collective-permute-start.25 = (f32[512,256]{1,0:T(8,128)S(1)}, f32[512,256]{1,0:T(8,128)S(1)}, u32[]{:S(2)}, u32[]{:S(2)}) collective-permute-start(f32[512,256]{1,0:T(8,128)S(1)} %get-tuple-element.26), channel_id=1, source_target_pairs={{15,23},{22,30},{23,31}} | collective-permute-start | bytes 1572872 | tf_op jit(solution)/shard_map/ppermute | solution.py:79
  73.4 1.3 %collective-permute-start.23 = (f32[256,256]{1,0:T(8,128)S(1)}, f32[256,256]{1,0:T(8,128)S(1)}, u32[]{:S(2)}, u32[]{:S(2)}) collective-permute-start(f32[256,256]{1,0:T(8,128)S(1)} %collective-permute-done.22.refs_6_), channel_id=1, source_target_pairs={{1,0},{3,2},{14,15},{10,11},{23,22},{19,18},{30,31},{24,25},{28,29}} | collective-permute-start | bytes 786440 | tf_op jit(solution)/shard_map/ppermute | solution.py:79
  74.7 1.3 %collective-permute-start.21 = (f32[256,256]{1,0:T(8,128)S(1)}, f32[256,256]{1,0:T(8,128)S(1)}, u32[]{:S(2)}, u32[]{:S(2)}) collective-permute-start(f32[256,256]{1,0:T(8,128)S(1)} %collective-permute-done.20.refs_4_), channel_id=1, source_target_pairs={{7,6},{1,0},{12,13},{14,15},{8,9},{21,20},{17,16},{28,29},{30,31},... | collective-permute-start | bytes 786440 | tf_op jit(solution)/shard_map/ppermute | solution.py:79
  76.1 2.2 %collective-permute-start.19 = (f32[256,256]{1,0:T(8,128)S(1)}, f32[256,256]{1,0:T(8,128)S(1)}, u32[]{:S(2)}, u32[]{:S(2)}) collective-permute-start(f32[256,256]{1,0:T(8,128)S(1)} %collective-permute-done.18.refs_2_), channel_id=1, source_target_pairs={{5,4},{7,6},{10,11},{12,13},{14,15},{19,18},{23,22},{26,27},{28,29... | collective-permute-start | bytes 786440 | tf_op jit(solution)/shard_map/ppermute | solution.py:79
  78.3 2.8 %shard_map.50.running_ref = f32[4096,128]{1,0:T(8,128)S(1)} custom-call(f32[4096,128]{1,0:T(8,128)S(1)} %bitcast.7, f32[256,256]{1,0:T(8,128)S(1)} %shard_map.47.left.refs_0_, f32[256,256]{1,0:T(8,128)S(1)} %collective-permute-done.11.refs_1_, f32[256,256]{1,0:T(8,128)S(1)} %collective-permute-done.9.shifted.refs_2_, ...), custom_call_target="tpu_custom_call" | custom-call | flops 1610612736 | bytes 8388608 | tf_op jit(solution)/shard_map/pallas_call | solution.py:191
  81.1 2.5 %collective-permute-done.19.refs_3_ = f32[256,256]{1,0:T(8,128)S(1)} collective-permute-done((f32[256,256]{1,0:T(8,128)S(1)}, f32[256,256]{1,0:T(8,128)S(1)}, u32[]{:S(2)}, u32[]{:S(2)}) %collective-permute-start.19) | collective-permute-done | bytes 262176 | tf_op jit(solution)/shard_map/ppermute | solution.py:79
  83.6 4.4 %shard_map.51 = f32[4096,128]{1,0:T(8,128)} custom-call(f32[4096,128]{1,0:T(8,128)S(1)} %shard_map.50.running_ref, f32[256,256]{1,0:T(8,128)S(1)} %shard_map.49.refs_0_, f32[256,256]{1,0:T(8,128)S(1)} %collective-permute-done.17.refs_1_, f32[256,256]{1,0:T(8,128)S(1)} %collective-permute-done.18.refs_2_, f32[256,256]{1,0:T(8,128)S(1)} %collective-permute-done.19.refs_3_, ...), custom_call_target="tpu_custom_call" | custom-call | flops 1610612736 | bytes 7864320 | tf_op jit(solution)/shard_map/pallas_call | solution.py:191
  (24 shorter events, 0.1 us)
Async XLA Ops:
  0.0 1.6 %copy-start = (f32[4,1,256,2,1,256]{5,4,3,2,1,0:T(1,128)S(1)}, f32[4,1,256,2,1,256]{5,4,3,2,1,0:T(1,128)}, u32[]{:S(2)}) copy-start(f32[4,1,256,2,1,256]{5,4,3,2,1,0:T(1,128)} %param.5) | copy-start | bytes 6291460
  1.6 1.2 %copy-start.3 = (f32[4,1,256,256]{3,2,1,0:T(8,128)S(1)}, f32[4,1,256,256]{3,2,1,0:T(8,128)}, u32[]{:S(2)}) copy-start(f32[4,1,256,256]{3,2,1,0:T(8,128)} %param.6) | copy-start | bytes 3145732
  2.8 0.7 copy-start.5
  3.5 4.9 %copy-start.2 = (f32[4,1,256,2,1,256]{5,4,3,2,1,0:T(1,128)S(1)}, f32[4,1,256,2,1,256]{5,4,3,2,1,0:T(1,128)}, u32[]{:S(2)}) copy-start(f32[4,1,256,2,1,256]{5,4,3,2,1,0:T(1,128)} %param.4) | copy-start | bytes 6291460
  3.7 10.6 %collective-permute-start.2 = (f32[256,256]{1,0:T(8,128)S(1)}, f32[256,256]{1,0:T(8,128)S(1)}, u32[]{:S(2)}, u32[]{:S(2)}) collective-permute-start(f32[256,256]{1,0:T(8,128)S(1)} %get-tuple-element.16.upper), channel_id=1, source_target_pairs={{28,1},{24,5},{21,8},{17,12},{14,19},{10,23},{7,26},{3,30}} | collective-permute-start | bytes 786440 | tf_op jit(solution)/shard_map/ppermute | solution.py:79
  5.1 17.1 %collective-permute-start.3 = (f32[264,256]{1,0:T(8,128)S(1)}, f32[264,256]{1,0:T(8,128)S(1)}, u32[]{:S(2)}, u32[]{:S(2)}) collective-permute-start(f32[264,256]{1,0:T(8,128)S(1)} %get-tuple-element.18), channel_id=1, source_target_pairs={{25,1},{27,3},{29,5},{31,7},{16,8},{18,10},{20,12},{22,14},{9,17},... | collective-permute-start | bytes 811016 | tf_op jit(solution)/shard_map/ppermute | solution.py:79
  6.4 12.0 %collective-permute-start.1 = (f32[256,256]{1,0:T(8,128)S(1)}, f32[256,256]{1,0:T(8,128)S(1)}, u32[]{:S(2)}, u32[]{:S(2)}) collective-permute-start(f32[256,256]{1,0:T(8,128)S(1)} %get-tuple-element.17), channel_id=1, source_target_pairs={{28,3},{24,7},{21,10},{17,14},{14,17},{10,21},{7,24},{3,28}} | collective-permute-start | bytes 786440 | tf_op jit(solution)/shard_map/ppermute | solution.py:79
  7.1 13.8 %collective-permute-start = (f32[256,256]{1,0:T(8,128)S(1)}, f32[256,256]{1,0:T(8,128)S(1)}, u32[]{:S(2)}, u32[]{:S(2)}) collective-permute-start(f32[256,256]{1,0:T(8,128)S(1)} %get-tuple-element.17), channel_id=1, source_target_pairs={{3,1},{7,5},{10,8},{14,12},{17,19},{21,23},{24,26},{28,30}} | collective-permute-start | bytes 786440 | tf_op jit(solution)/shard_map/ppermute | solution.py:79
  8.4 14.5 %copy-start.4 = (f32[4,1,256,256]{3,2,1,0:T(8,128)S(1)}, f32[4,1,256,256]{3,2,1,0:T(8,128)}, u32[]{:S(2)}) copy-start(f32[4,1,256,256]{3,2,1,0:T(8,128)} %param.6) | copy-start | bytes 3145732
  8.7 28.5 %copy-start.6 = (f32[4,1,256]{2,1,0:T(1,128)S(1)}, f32[4,1,256]{2,1,0:T(1,128)}, u32[]{:S(2)}) copy-start(f32[4,1,256]{2,1,0:T(1,128)} %param.7) | copy-start | bytes 12292
  8.7 17.8 %collective-permute-start.6 = (f32[512,256]{1,0:T(8,128)S(1)}, f32[512,256]{1,0:T(8,128)S(1)}, u32[]{:S(2)}, u32[]{:S(2)}) collective-permute-start(f32[512,256]{1,0:T(8,128)S(1)} %get-tuple-element.19), channel_id=1, source_target_pairs={{4,3},{29,10},{25,14},{22,17},{18,21},{15,24},{11,28}} | collective-permute-start | bytes 1572872 | tf_op jit(solution)/shard_map/ppermute | solution.py:79
  14.3 10.7 %collective-permute-start.8 = (f32[264,256]{1,0:T(8,128)S(1)}, f32[264,256]{1,0:T(8,128)S(1)}, u32[]{:S(2)}, u32[]{:S(2)}) collective-permute-start(f32[264,256]{1,0:T(8,128)S(1)} %get-tuple-element.21), channel_id=1, source_target_pairs={{24,8},{26,10},{28,12},{30,14},{8,24},{10,26},{12,28},{14,30}} | collective-permute-start | bytes 811016 | tf_op jit(solution)/shard_map/ppermute | solution.py:79
  18.5 15.6 %collective-permute-start.4 = (f32[512,256]{1,0:T(8,128)S(1)}, f32[512,256]{1,0:T(8,128)S(1)}, u32[]{:S(2)}, u32[]{:S(2)}) collective-permute-start(f32[512,256]{1,0:T(8,128)S(1)} %get-tuple-element.19), channel_id=1, source_target_pairs={{11,8},{15,12},{25,26},{29,30}} | collective-permute-start | bytes 1572872 | tf_op jit(solution)/shard_map/ppermute | solution.py:79
  20.9 13.1 %collective-permute-start.7 = (f32[512,256]{1,0:T(8,128)S(1)}, f32[512,256]{1,0:T(8,128)S(1)}, u32[]{:S(2)}, u32[]{:S(2)}) collective-permute-start(f32[512,256]{1,0:T(8,128)S(1)} %get-tuple-element.20), channel_id=1, source_target_pairs={{0,5},{29,8},{25,12},{15,26},{11,30}} | collective-permute-start | bytes 1572872 | tf_op jit(solution)/shard_map/ppermute | solution.py:79
  22.2 11.8 %collective-permute-start.5 = (f32[512,256]{1,0:T(8,128)S(1)}, f32[512,256]{1,0:T(8,128)S(1)}, u32[]{:S(2)}, u32[]{:S(2)}) collective-permute-start(f32[512,256]{1,0:T(8,128)S(1)} %get-tuple-element.20), channel_id=1, source_target_pairs={{4,3},{0,5},{11,10},{15,14},{18,17},{22,21},{25,24},{29,28}} | collective-permute-start | bytes 1572872 | tf_op jit(solution)/shard_map/ppermute | solution.py:79
  25.0 53.2 %copy-start.1 = (f32[4,1,256,2,1,256]{5,4,3,2,1,0:T(1,128)S(1)}, f32[4,1,256,2,1,256]{5,4,3,2,1,0:T(1,128)}, u32[]{:S(2)}) copy-start(f32[4,1,256,2,1,256]{5,4,3,2,1,0:T(1,128)} %param.5) | copy-start | bytes 6291460
  25.0 11.7 %collective-permute-start.10 = (f32[256,256]{1,0:T(8,128)S(1)}, f32[256,256]{1,0:T(8,128)S(1)}, u32[]{:S(2)}, u32[]{:S(2)}) collective-permute-start(f32[256,256]{1,0:T(8,128)S(1)} %shard_map.47.left.refs_0_), channel_id=1, source_target_pairs={{1,8},{3,10},{5,12},{7,14},{17,24},{19,26},{21,28},{23,30}} | collective-permute-start | bytes 786440 | tf_op jit(solution)/shard_map/ppermute | solution.py:79
  26.5 10.7 %collective-permute-start.9 = (f32[256,256]{1,0:T(8,128)S(1)}, f32[256,256]{1,0:T(8,128)S(1)}, u32[]{:S(2)}, u32[]{:S(2)}) collective-permute-start(f32[256,256]{1,0:T(8,128)S(1)} %shard_map.47.left.refs_0_), channel_id=1, source_target_pairs={{1,3},{3,5},{5,7},{8,10},{10,12},{12,14},{17,19},{19,21},{21,23},{... | collective-permute-start | bytes 786440 | tf_op jit(solution)/shard_map/ppermute | solution.py:79
  39.8 12.6 %collective-permute-start.12 = (f32[256,256]{1,0:T(8,128)S(1)}, f32[256,256]{1,0:T(8,128)S(1)}, u32[]{:S(2)}, u32[]{:S(2)}) collective-permute-start(f32[256,256]{1,0:T(8,128)S(1)} %collective-permute-done.9.shifted.refs_2_), channel_id=1, source_target_pairs={{3,2},{5,4},{7,6},{10,11},{12,13},{14,15},{19,18},{21,20},{23,22},... | collective-permute-start | bytes 786440 | tf_op jit(solution)/shard_map/ppermute | solution.py:79
  41.2 16.3 %collective-permute-start.15 = (f32[256,256]{1,0:T(8,128)S(1)}, f32[256,256]{1,0:T(8,128)S(1)}, u32[]{:S(2)}, u32[]{:S(2)}) collective-permute-start(f32[256,256]{1,0:T(8,128)S(1)} %shard_map.47.left.refs_0_), channel_id=1, source_target_pairs={{1,7},{5,3},{8,14},{12,10},{17,23},{19,17},{23,21},{24,30},{26,24}... | collective-permute-start | bytes 786440 | tf_op jit(solution)/shard_map/ppermute | solution.py:79
  48.6 13.4 %collective-permute-start.13 = (f32[256,256]{1,0:T(8,128)S(1)}, f32[256,256]{1,0:T(8,128)S(1)}, u32[]{:S(2)}, u32[]{:S(2)}) collective-permute-start(f32[256,256]{1,0:T(8,128)S(1)} %shard_map.47.left.refs_0_), channel_id=1, source_target_pairs={{1,5},{3,7},{5,1},{8,12},{10,14},{12,8},{17,21},{19,23},{23,19},{2... | collective-permute-start | bytes 786440 | tf_op jit(solution)/shard_map/ppermute | solution.py:79
  51.1 32.6 %collective-permute-start.24 = (f32[1024,256]{1,0:T(8,128)S(1)}, f32[1024,256]{1,0:T(8,128)S(1)}, u32[]{:S(2)}, u32[]{:S(2)}) collective-permute-start(f32[1024,256]{1,0:T(8,128)S(1)} %get-tuple-element.24), channel_id=1, source_target_pairs={{24,0},{25,1},{26,2},{27,3},{28,4},{29,5},{30,6},{31,7},{0,8},{1,9... | collective-permute-start | bytes 3145736 | tf_op jit(solution)/shard_map/ppermute | solution.py:79
  51.1 12.8 %collective-permute-start.11 = (f32[256,256]{1,0:T(8,128)S(1)}, f32[256,256]{1,0:T(8,128)S(1)}, u32[]{:S(2)}, u32[]{:S(2)}) collective-permute-start(f32[256,256]{1,0:T(8,128)S(1)} %shard_map.47.left.refs_0_), channel_id=1, source_target_pairs={{1,0},{5,4},{8,9},{10,11},{12,13},{14,15},{19,18},{23,22},{24,25},... | collective-permute-start | bytes 786440 | tf_op jit(solution)/shard_map/ppermute | solution.py:79
  52.4 12.8 %collective-permute-start.22 = (f32[256,256]{1,0:T(8,128)S(1)}, f32[256,256]{1,0:T(8,128)S(1)}, u32[]{:S(2)}, u32[]{:S(2)}) collective-permute-start(f32[256,256]{1,0:T(8,128)S(1)} %shard_map.49.refs_0_), channel_id=1, source_target_pairs={{3,1},{5,3},{8,14},{12,10},{17,23},{21,19},{24,30},{26,24},{30,28}} | collective-permute-start | bytes 786440 | tf_op jit(solution)/shard_map/ppermute | solution.py:79
  57.5 11.7 %collective-permute-start.20 = (f32[256,256]{1,0:T(8,128)S(1)}, f32[256,256]{1,0:T(8,128)S(1)}, u32[]{:S(2)}, u32[]{:S(2)}) collective-permute-start(f32[256,256]{1,0:T(8,128)S(1)} %shard_map.49.refs_0_), channel_id=1, source_target_pairs={{3,7},{5,1},{8,12},{10,14},{12,8},{17,21},{21,17},{24,28},{26,30},... | collective-permute-start | bytes 786440 | tf_op jit(solution)/shard_map/ppermute | solution.py:79
  62.0 10.1 %collective-permute-start.18 = (f32[256,256]{1,0:T(8,128)S(1)}, f32[256,256]{1,0:T(8,128)S(1)}, u32[]{:S(2)}, u32[]{:S(2)}) collective-permute-start(f32[256,256]{1,0:T(8,128)S(1)} %shard_map.49.refs_0_), channel_id=1, source_target_pairs={{3,5},{5,7},{8,10},{10,12},{12,14},{17,19},{21,23},{24,26},{26,28}... | collective-permute-start | bytes 786440 | tf_op jit(solution)/shard_map/ppermute | solution.py:79
  63.9 9.5 %collective-permute-start.17 = (f32[256,256]{1,0:T(8,128)S(1)}, f32[256,256]{1,0:T(8,128)S(1)}, u32[]{:S(2)}, u32[]{:S(2)}) collective-permute-start(f32[256,256]{1,0:T(8,128)S(1)} %shard_map.49.refs_0_), channel_id=1, source_target_pairs={{3,2},{5,4},{8,9},{10,11},{12,13},{14,15},{17,16},{21,20},{24,25},... | collective-permute-start | bytes 786440 | tf_op jit(solution)/shard_map/ppermute | solution.py:79
  65.3 9.5 %collective-permute-start.16 = (f32[256,256]{1,0:T(8,128)S(1)}, f32[256,256]{1,0:T(8,128)S(1)}, u32[]{:S(2)}, u32[]{:S(2)}) collective-permute-start(f32[256,256]{1,0:T(8,128)S(1)} %collective-permute-done.15.refs_6_), channel_id=1, source_target_pairs={{7,6},{3,2},{14,15},{10,11},{23,22},{17,16},{21,20},{30,31},{24,25... | collective-permute-start | bytes 786440 | tf_op jit(solution)/shard_map/ppermute | solution.py:79
  69.2 6.8 %collective-permute-start.14 = (f32[256,256]{1,0:T(8,128)S(1)}, f32[256,256]{1,0:T(8,128)S(1)}, u32[]{:S(2)}, u32[]{:S(2)}) collective-permute-start(f32[256,256]{1,0:T(8,128)S(1)} %collective-permute-done.13.refs_4_), channel_id=1, source_target_pairs={{5,4},{7,6},{1,0},{12,13},{14,15},{8,9},{21,20},{23,22},{19,18},{2... | collective-permute-start | bytes 786440 | tf_op jit(solution)/shard_map/ppermute | solution.py:79
  72.1 11.5 %collective-permute-start.25 = (f32[512,256]{1,0:T(8,128)S(1)}, f32[512,256]{1,0:T(8,128)S(1)}, u32[]{:S(2)}, u32[]{:S(2)}) collective-permute-start(f32[512,256]{1,0:T(8,128)S(1)} %get-tuple-element.26), channel_id=1, source_target_pairs={{15,23},{22,30},{23,31}} | collective-permute-start | bytes 1572872 | tf_op jit(solution)/shard_map/ppermute | solution.py:79
  73.4 7.7 %collective-permute-start.23 = (f32[256,256]{1,0:T(8,128)S(1)}, f32[256,256]{1,0:T(8,128)S(1)}, u32[]{:S(2)}, u32[]{:S(2)}) collective-permute-start(f32[256,256]{1,0:T(8,128)S(1)} %collective-permute-done.22.refs_6_), channel_id=1, source_target_pairs={{1,0},{3,2},{14,15},{10,11},{23,22},{19,18},{30,31},{24,25},{28,29}} | collective-permute-start | bytes 786440 | tf_op jit(solution)/shard_map/ppermute | solution.py:79
  74.7 6.4 %collective-permute-start.21 = (f32[256,256]{1,0:T(8,128)S(1)}, f32[256,256]{1,0:T(8,128)S(1)}, u32[]{:S(2)}, u32[]{:S(2)}) collective-permute-start(f32[256,256]{1,0:T(8,128)S(1)} %collective-permute-done.20.refs_4_), channel_id=1, source_target_pairs={{7,6},{1,0},{12,13},{14,15},{8,9},{21,20},{17,16},{28,29},{30,31},... | collective-permute-start | bytes 786440 | tf_op jit(solution)/shard_map/ppermute | solution.py:79
  76.1 7.6 %collective-permute-start.19 = (f32[256,256]{1,0:T(8,128)S(1)}, f32[256,256]{1,0:T(8,128)S(1)}, u32[]{:S(2)}, u32[]{:S(2)}) collective-permute-start(f32[256,256]{1,0:T(8,128)S(1)} %collective-permute-done.18.refs_2_), channel_id=1, source_target_pairs={{5,4},{7,6},{10,11},{12,13},{14,15},{19,18},{23,22},{26,27},{28,29... | collective-permute-start | bytes 786440 | tf_op jit(solution)/shard_map/ppermute | solution.py:79

commit v4 on v3

v4 whole, which is shorter than its diff:
```python
import numpy as np
import jax
import jax.numpy as jnp
from jax import lax
from jax.experimental import pallas as pl
from jax.experimental.pallas import tpu as pltpu
from jax.sharding import PartitionSpec as P

AXES = ("row", "col")
LANES = 128
LIMIT = 40 * 1024 * 1024
LINE = 4
GATE_SPREAD = "none"
GATE_PANEL = "none"
GATE_FORWARD = "often"
GATE_SOLVE = "none"
PACK_SEEN = None
DIRECT = (True, False)
GATE_LOW = "none"


def product(first, second, dims=((1,), (0,))):
    return lax.dot_general(
        first,
        second,
        (dims, ((), ())),
        precision=lax.Precision.HIGHEST,
        preferred_element_type=jnp.float32,
    )


def solution(mesh):
    rows, cols = mesh.shape["row"], mesh.shape["col"]
    count = 4 * rows
    assert cols == 2 * rows and cols % LINE == 0
    stride = cols // LINE
    devices = [(r, c) for r in range(rows) for c in range(cols)]

    def holds(d, r, c):
        return c % rows == (d - r) % rows

    def local_row(d, c, q):
        return (d - q * cols - c) // rows

    def within(r):
        return r % (rows // 2) == 0

    def shift(c, by):
        return (c + by * stride) % cols

    def step(c, by):
        return c // stride * stride + (c + by) % stride

    first = [device for device in devices if holds(count - 1, *device)]
    second = [device for device in devices if holds(count, *device)]

    def send(value, moves):
        assert len({s for s, _ in moves}) == len(moves) == len({t for _, t in moves})
        return lax.ppermute(value, AXES, [(s[0] * cols + s[1], t[0] * cols + t[1]) for s, t in moves])

    def after(value, *others):
        return lax.optimization_barrier((value, *others))[0] if others else value

    mirror_first = [((rows - 1 - r, cols - 1 - c), (r, c)) for r, c in first]
    mirror_second = [((-r % rows, -c % cols), (r, c)) for r, c in second if r != 0]
    far = [((c % rows, c), (r, c)) for r, c in first]
    far += [((c % rows, step(c, 1)), (r, c)) for r, c in second if not within(r)]
    left = [((r, (c - 1) % cols), (r, c)) for r, c in second]
    above = [(((r - 1) % rows, c), (r, c)) for r, c in second]

    def middle(d, c):
        return (c == 0) & (d == count)

    def solved_row(d, c):
        return local_row(d, c, 0) - 2 * middle(d, c)

    def wants(k, d, c):
        return 0 <= d - k < count and cols + c >= d - k

    def needs(d, source):
        r, c = source
        k = solved_row(d, c) * rows + r
        at_all = range(cols)
        if d == count and within(r):
            return {(r, at) for at in at_all if wants(k, d, at) or wants(d - k, d, at)}
        return {(r, at) for at in at_all if wants(k, d, at)}

    def needs_turned(d, source):
        r, c = source
        if d == count and within(r):
            return set()
        k = d - (solved_row(d, c) * rows + r)
        return {(k % rows, at) for at in range(cols) if wants(k, d, at)}

    def spread_moves(d, sources, direct):
        own, turned = {}, {}
        for source in sources:
            own[source], turned[source] = needs(d, source), needs_turned(d, source)
            if not direct:
                own[source] = own[source] | {(source[0], at) for _, at in turned[source]}
                turned[source] = set()

        def line_moves(by, used, target_row):
            moves = []
            for r, c in sources:
                at = shift(c, by)
                if any((target_row(r), step(at, n)) in used[r, c] for n in range(stride)):
                    moves.append(((r, c), (target_row(r), at)))
            return moves

        def group_moves(half, n, used, target_row):
            moves = []
            for r, c in sources:
                for by in (2 * half, 2 * half + 1):
                    at = shift(c, by)
                    if (target_row(r), step(at, n)) in used[r, c]:
                        moves.append(((target_row(r), at), (target_row(r), step(at, n))))
            return moves

        same, other = (lambda r: r), (lambda r: (d - r) % rows)
        shifts = [line_moves(by, own, same) for by in range(LINE)]
        shifts_turned = [line_moves(by, turned, other) for by in range(LINE)]
        steps, steps_turned = {}, {}
        for half in range(2):
            for n in range(1, stride):
                steps[half, n] = group_moves(half, n, own, same)
                steps_turned[half, n] = group_moves(half, n, turned, other)
        return shifts, shifts_turned, steps, steps_turned

    def across_moves(d, sources):
        targets = set().union(*(needs_turned(d, source) for source in sources))
        return [(((d - t) % rows, c), (t, c)) for t, c in sorted(targets)]

    def reached(device, p, q):
        k = p * rows + device[0]
        return 0 < k and q * cols + device[1] > count - k

    slots = [(p, q) for p in range(4) for q in range(2)]
    common = [s for s in slots if reached((rows // 2, cols // 2), *s)]
    seldom = [s for s in slots if s not in common and any(reached(device, *s) for device in devices)]

    def panel_moves(chosen):
        return [
            (((r - 1) % rows, c), (r, c)) for r, c in devices if any(reached((r, c), *s) for s in chosen)
        ]

    def local(reversed_rows, state, basis, eigval):
        width = state.shape[2]
        halves = width // LANES
        stripe = 2 * halves
        slab = width * stripe
        running = state.reshape(4 * slab, LANES)
        panel = reversed_rows.reshape(4 * slab, LANES)
        own_basis = basis.reshape(4, width, width)
        own_values = eigval.reshape(4 * halves, LANES)
        vmem = pl.BlockSpec(memory_space=pltpu.VMEM)
        hbm = pl.BlockSpec(memory_space=pltpu.HBM)

        def blocks_shape(number, extra=0):
            return jax.ShapeDtypeStruct((number * width + extra, width), jnp.float32)

        def part(index):
            return slice(index * width, (index + 1) * width)

        def where_at(p, q, half):
            return pl.ds(p * slab + q * halves + half, width, stride=stripe)

        def joined(parts):
            return jnp.concatenate(parts, axis=1) if halves > 1 else parts[0]

        def read(ref, p, q):
            return joined([ref[where_at(p, q, half), :] for half in range(halves)])

        def write(ref, p, q, value):
            for half in range(halves):
                ref[where_at(p, q, half), :] = value[:, half * LANES : (half + 1) * LANES]

        def values_at(ref, p):
            return joined([ref[pl.ds(p * halves + half, 1), :] for half in range(halves)])

        def here():
            return lax.axis_index("row"), lax.axis_index("col")

        def near_row(d, c, q):
            return jnp.clip(local_row(d, c, q), 0, 3)

        def call(body, outputs, operands, specs=None, scratch=(), flops=0, seen=None):
            moved = sum(4 * int(np.prod(o.shape)) for o in (*operands, *outputs)) if seen is None else seen
            return pl.pallas_call(
                body,
                out_shape=outputs,
                in_specs=specs or [vmem] * len(operands),
                out_specs=[vmem] * len(outputs),
                scratch_shapes=scratch,
                compiler_params=pltpu.CompilerParams(vmem_limit_bytes=LIMIT),
                cost_estimate=pl.CostEstimate(flops=flops, bytes_accessed=moved, transcendentals=0),
            )(*operands)

        def slab_copy(ref, p, target, sem):
            return pltpu.make_async_copy(ref.at[pl.ds(pl.multiple_of(p * slab, slab), slab)], target, sem)

        def pack_first(state_ref, basis_ref, values_ref, own, upper, eigen, slabs, values, sems):
            r, c = here()
            column = jnp.where(c % rows == r, c, step(c, -1))
            index = column // rows
            copies = [
                slab_copy(state_ref, near_row(count - 1, c, q), slabs.at[q], sems.at[q]) for q in range(2)
            ]
            copies.append(pltpu.make_async_copy(basis_ref.at[index], eigen.at[pl.ds(0, width)], sems.at[2]))
            copies.append(pltpu.make_async_copy(values_ref, values, sems.at[3]))
            for copy in copies:
                copy.start()
            for target, q in ((own, 0), (upper, 1)):
                copies[q].wait()
                target[...] = read(slabs.at[q], 0, q)
            for copy in copies[2:]:
                copy.wait()
            eigen[width:, :] = jnp.broadcast_to(values_at(values, index), (8, width))

        def pack_second(state_ref, panel_ref, own, upper, often, rarely, slabs, panel_slabs, sems):
            r, c = here()
            places = [near_row(count, c, q) for q in range(2)]
            copies = [slab_copy(state_ref, places[q], slabs.at[q], sems.at[q]) for q in range(2)]
            copies.append(pltpu.make_async_copy(panel_ref, panel_slabs, sems.at[2]))
            for copy in copies:
                copy.start()
            for copy in copies:
                copy.wait()
            for target, q in ((own, 0), (upper, 1)):
                target[part(0), :] = read(slabs.at[q], 0, q)
                target[part(1), :] = read(panel_slabs, places[q], q)
            last = (r == rows - 1).astype(jnp.int32)
            for target, chosen in ((often, common), (rarely, seldom)):
                for index, (p, q) in enumerate(chosen):
                    target[part(index), :] = read(panel_slabs, jnp.maximum(p - last, 0), q)

        def column_of(values):
            return jnp.broadcast_to(values, (width, width)).T

        def solve(right_side, near, near_values, far_basis, far_values):
            inner = product(near.T, right_side)
            inner = product(inner, far_basis)
            inner = inner / (column_of(near_values) + far_values)
            return product(product(near, inner), far_basis, ((1,), (1,)))

        def solve_first(own, mirror, eigen, basis_ref, values_ref, out):
            r, c = here()
            mine = holds(count - 1, r, c)

            @pl.when(mine)
            def _():
                p = jnp.clip(solved_row(count - 1, c), 0, 3)
                right_side = own[...] + mirror[...].T
                near, values = basis_ref[p], values_at(values_ref, p)
                out[...] = solve(right_side, near, values, eigen[:width, :], eigen[width : width + 1, :])

            @pl.when(jnp.logical_not(mine))
            def _():
                out[...] = jnp.zeros_like(out)

        def solve_second(own, upper, mirror, eigen, left_ref, above_ref, basis_ref, values_ref, out):
            r, c = here()
            mine = holds(count, r, c)
            inside = within(r)
            lone = c == 0

            @pl.when(mine)
            def _():
                def own_part(index):
                    return jnp.where(lone, upper[part(index), :], own[part(index), :])

                def mirror_part(index):
                    return jnp.where(r == 0, upper[part(index), :], mirror[part(index), :])

                p = jnp.clip(solved_row(count, c), 0, 3)
                before = left_ref[...]
                turned = jnp.where(lone, before.T, above_ref[...])
                right_side = own_part(0) - product(before, own_part(1))
                right_side = right_side + (mirror_part(0).T - product(mirror_part(1).T, turned))
                index = (c + cols * lone) // rows
                far_basis = jnp.where(inside, basis_ref[index], eigen[:width, :])
                far_values = jnp.where(inside, values_at(values_ref, index), eigen[width : width + 1, :])
                out[...] = solve(right_side, basis_ref[p], values_at(values_ref, p), far_basis, far_values)

            @pl.when(jnp.logical_not(mine))
            def _():
                out[...] = jnp.zeros_like(out)

        def update(d, running, shares, sources, rows_of_a):
            arrays = []
            for share in shares:
                for array, _, _ in share:
                    if not any(array is other for other in arrays):
                        arrays.append(array)

            def body(running_ref, *refs):
                r, c = here()
                parts, given = refs[: len(arrays)], refs[len(arrays) : -2]
                out, blocks = refs[-2], refs[-1]
                for index, share in enumerate(shares):
                    total = None
                    residue = (d - r if index < 2 else r) % stride
                    for array, row, n in share:
                        ref = next(p for p, a in zip(parts, arrays) if a is array)
                        value = ref[part(row), :]
                        if n and d < count:
                            value = jnp.where((c - n) % stride == residue, value, 0.0)
                        total = value if total is None else total + value
                    blocks[index] = total
                for p in range(4):
                    k = p * rows + r
                    partner = d - k
                    source = jnp.minimum(k, partner) % cols
                    half = (c // stride - source // stride) % LINE // 2
                    turned = 2 * k < d
                    index = half + 2 * turned.astype(jnp.int32)
                    if d == count:
                        index = jnp.where(within(r), half, index)

                    def block():
                        found = blocks[index]
                        return jnp.where(turned, found.T, found) if p < 3 else found

                    for q in range(2):
                        at = q * cols + c
                        old = read(running_ref, p, q)
                        write(out, p, q, old)
                        a_block = rows_of_a(given, p, q)
                        if a_block is not None:

                            @pl.when((at > partner) & (partner < count))
                            def _():
                                write(out, p, q, old - product(block(), a_block()))

                        @pl.when(at == partner)
                        def _():
                            write(out, p, q, block())

            return call(
                body,
                [jax.ShapeDtypeStruct(running.shape, jnp.float32)],
                (running, *arrays, *sources),
                scratch=[pltpu.VMEM((4, width, width), jnp.float32)],
                flops=16 * width**3 * 6,
            )[0]

        def own_rows(given, p, q):
            return lambda: read(given[0], p, q)

        def next_rows(given, p, q):
            for ref, chosen in zip(given, (common, seldom)):
                if (p, q) in chosen:
                    index = chosen.index((p, q))
                    return lambda: ref[part(index), :]
            return None

        def spread(value, d, sources, direct, held=(), held_turned=()):
            shifts, shifts_turned, steps, steps_turned = spread_moves(d, sources, direct)
            moved = [value] + [send(value, moves) for moves in shifts[1:]]
            shares = [[(array, 0, 0) for array in moved[2 * half : 2 * half + 2]] for half in range(2)]
            if not direct:
                for half in range(2):
                    both = after(moved[2 * half] + moved[2 * half + 1], *held)
                    for n in range(1, stride):
                        shares[half].append((send(both, steps[half, n]), 0, n))
                pair = jnp.concatenate([sum(a for a, _, _ in share) for share in shares], axis=0)
                got = send(pair, across_moves(d, sources))
                return shares + [[(got, 0, 0)], [(got, 1, 0)]]
            low = after(value, *held_turned)
            low_moved = [send(low, moves) for moves in shifts_turned]
            shares += [[(array, 0, 0) for array in low_moved[2 * half : 2 * half + 2]] for half in range(2)]
            for half in range(2):
                both = after(moved[2 * half] + moved[2 * half + 1], *held)
                both_low = low_moved[2 * half] + low_moved[2 * half + 1]
                for n in range(1, stride):
                    if d < count:
                        got = send(both + both_low, steps[half, n] + steps_turned[half, n])
                        shares[half].append((got, 0, n))
                        shares[2 + half].append((got, 0, n))
                    else:
                        shares[half].append((send(both, steps[half, n]), 0, n))
                        shares[2 + half].append((send(both_low, steps_turned[half, n]), 0, n))
            return shares

        solve_flops = 4 * 2 * 6 * width**3

        own, upper, eigen = call(
            pack_first,
            [blocks_shape(1), blocks_shape(1), blocks_shape(1, 8)],
            (running, own_basis, own_values),
            specs=[hbm, hbm, hbm],
            scratch=[
                pltpu.VMEM((2, slab, LANES), jnp.float32),
                pltpu.VMEM((4 * halves, LANES), jnp.float32),
                pltpu.SemaphoreType.DMA((4,)),
            ],
            seen=PACK_SEEN,
        )
        mirror = send(upper, mirror_first)
        eigen = send(eigen, far)
        own_pair, upper_pair, often, rarely = call(
            pack_second,
            [blocks_shape(2), blocks_shape(2), blocks_shape(len(common)), blocks_shape(len(seldom))],
            (running, panel),
            specs=[hbm, hbm],
            scratch=[
                pltpu.VMEM((2, slab, LANES), jnp.float32),
                pltpu.VMEM((4 * slab, LANES), jnp.float32),
                pltpu.SemaphoreType.DMA((3,)),
            ],
            seen=PACK_SEEN,
        )
        pair_mirror = send(upper_pair, mirror_second)
        (solved,) = call(
            solve_first,
            [blocks_shape(1)],
            (own, mirror, eigen, own_basis, own_values),
            flops=solve_flops,
        )

        before = send(solved, left)
        above_it = send(solved, above)
        options = {"none": (), "solved": (solved,), "before": (before,), "direct": (before, above_it)}
        often = send(after(often, *options.get(GATE_PANEL, ())), panel_moves(common))
        rarely = send(after(rarely, *options.get(GATE_PANEL, ())), panel_moves(seldom))
        ready = {"none": (), "often": (often,), "both": (often, rarely)}[GATE_SOLVE]
        (solved_next,) = call(
            solve_second,
            [blocks_shape(1)],
            (after(own_pair, *ready), upper_pair, pair_mirror, eigen, before, above_it, own_basis, own_values),
            flops=3 * solve_flops // 2,
        )
        options["next"] = (solved_next,)
        options["often"], options["both"] = (often,), (often, rarely)
        shares = spread(
            after(solved, *options[GATE_SPREAD]),
            count - 1,
            first,
            DIRECT[0],
            options[GATE_FORWARD],
            options[GATE_LOW],
        )
        running = update(count - 1, running, shares, [panel], own_rows)

        shares = spread(solved_next, count, second, DIRECT[1])
        running = update(count, running, shares, [often, rarely], next_rows)
        return running.reshape(state.shape)

    placed = (
        P(None, "row", None, None, "col", None),
        P(None, "row", None, None, "col", None),
        P(None, "row", None, None),
        P(None, "row", None),
    )
    return jax.shard_map(
        local,
        mesh=mesh,
        in_specs=placed,
        out_specs=P(None, "row", None, None, "col", None),
        check_vma=False,
    )
```

time: 89.5 us -> 83.7 us (0.935)
  the two profiles are of different devices: /device:TPU:29 before, /device:TPU:27 now
where the time goes in v4:
time: 83.7 us; the launch traced here: 83.1 us
  waiting for transfers between devices  36 us (43%)
  starting transfers between devices  32.7 us (39%)
  Pallas kernels  10.2 us (12%)
  local copies, waits for them, and re-layouts  3.52 us (4%)
    ppermute x22, waiting for transfers between devices, send(): lax.ppermute(value, AXES, [(s[0] * cols + s[1], t[0] * cols + t[1]) for s...  36 us
    ppermute x22, starting transfers between devices, send(): lax.ppermute(value, AXES, [(s[0] * cols + s[1], t[0] * cols + t[1]) for s...  32.7 us
    pallas_call x6, Pallas kernels, call(): pl.pallas_call(body, out_shape=outputs, in_specs=specs or [vmem] * len(op...  10.2 us
    unnamed x14, local copies, waits for them, and re-layouts  3.52 us
  transfers between devices with their start and end apart: 22, of which 9 were waited for; matrix products, arithmetic and copies ran while one was open for 0% of the time, Pallas kernels for 8%

profile of v4, /device:TPU:27, one launch (start us, length us, event | category | flops | bytes accessed | tf_op | source)
XLA Modules:
  0.0 83.1 jit_solution(17679040433795782834)
XLA Ops:
  0.0 1.6 %copy-done = f32[4,1,256,2,1,256]{5,4,3,2,1,0:T(1,128)S(1)} copy-done((f32[4,1,256,2,1,256]{5,4,3,2,1,0:T(1,128)S(1)}, f32[4,1,256,2,1,256]{5,4,3,2,1,0:T(1,128)}, u32[]{:S(2)}) %copy-start) | copy-done | bytes 2097176
  1.6 1.2 %copy-done.3 = f32[4,1,256,256]{3,2,1,0:T(8,128)S(1)} copy-done((f32[4,1,256,256]{3,2,1,0:T(8,128)S(1)}, f32[4,1,256,256]{3,2,1,0:T(8,128)}, u32[]{:S(2)}) %copy-start.3) | copy-done | bytes 1048600
  2.8 0.7 copy-done.5
  3.5 0.2 shard_map.46
  3.7 1.4 %collective-permute-start.1 = (f32[264,256]{1,0:T(8,128)S(1)}, f32[264,256]{1,0:T(8,128)S(1)}, u32[]{:S(2)}, u32[]{:S(2)}) collective-permute-start(f32[264,256]{1,0:T(8,128)S(1)} %get-tuple-element.16), channel_id=1, source_target_pairs={{27,3},{31,7},{18,10},{22,14},{9,17},{13,21},{0,24},{4,28},{26,11}... | collective-permute-start | bytes 811016 | tf_op jit(solution)/shard_map/ppermute | solution.py:59
  5.1 0.7 collective-permute-start
  5.8 0.4 shard_map.48
  6.2 0.0 copy-start.4
  6.3 0.0 copy-start.6
  6.3 2.9 %collective-permute-start.12 = (f32[512,256]{1,0:T(8,128)S(1)}, f32[512,256]{1,0:T(8,128)S(1)}, u32[]{:S(2)}, u32[]{:S(2)}) collective-permute-start(f32[512,256]{1,0:T(8,128)S(1)} %get-tuple-element.21.upper), channel_id=1, source_target_pairs={{29,11},{25,15},{22,18},{18,22},{15,25},{11,29}} | collective-permute-start | bytes 1572872 | tf_op jit(solution)/shard_map/ppermute | solution.py:59
  9.2 0.1 collective-permute-start.3
  9.3 2.7 %collective-permute-done.1.eigen = f32[264,256]{1,0:T(8,128)S(1)} collective-permute-done((f32[264,256]{1,0:T(8,128)S(1)}, f32[264,256]{1,0:T(8,128)S(1)}, u32[]{:S(2)}, u32[]{:S(2)}) %collective-permute-start.1) | collective-permute-done | bytes 270368 | tf_op jit(solution)/shard_map/ppermute | solution.py:59
  12.0 1.3 %collective-permute-start.13 = (f32[256,256]{1,0:T(8,128)S(1)}, f32[256,256]{1,0:T(8,128)S(1)}, u32[]{:S(2)}, u32[]{:S(2)}) collective-permute-start(f32[256,256]{1,0:T(8,128)S(1)} %shard_map.47.refs_0_), channel_id=1, source_target_pairs={{7,0},{3,4},{10,11},{14,15},{17,18},{21,22},{24,25},{28,29}} | collective-permute-start | bytes 786440 | tf_op jit(solution)/shard_map/ppermute | solution.py:59
  13.3 1.3 %collective-permute-start.14 = (f32[256,256]{1,0:T(8,128)S(1)}, f32[256,256]{1,0:T(8,128)S(1)}, u32[]{:S(2)}, u32[]{:S(2)}) collective-permute-start(f32[256,256]{1,0:T(8,128)S(1)} %shard_map.47.refs_0_), channel_id=1, source_target_pairs={{24,0},{28,4},{3,11},{7,15},{10,18},{14,22},{17,25},{21,29}} | collective-permute-start | bytes 786440 | tf_op jit(solution)/shard_map/ppermute | solution.py:59
  14.6 0.7 collective-permute-start.2
  15.3 6.6 %collective-permute-done.12.mirror = f32[512,256]{1,0:T(8,128)S(1)} collective-permute-done((f32[512,256]{1,0:T(8,128)S(1)}, f32[512,256]{1,0:T(8,128)S(1)}, u32[]{:S(2)}, u32[]{:S(2)}) %collective-permute-start.12) | collective-permute-done | bytes 524320 | tf_op jit(solution)/shard_map/ppermute | solution.py:59
  21.9 0.7 collective-permute-start.7
  22.6 3.6 %collective-permute-done.13.left_ref = f32[256,256]{1,0:T(8,128)S(1)} collective-permute-done((f32[256,256]{1,0:T(8,128)S(1)}, f32[256,256]{1,0:T(8,128)S(1)}, u32[]{:S(2)}, u32[]{:S(2)}) %collective-permute-start.13) | collective-permute-done | bytes 262176 | tf_op jit(solution)/shard_map/ppermute | solution.py:59
  26.2 3.1 %collective-permute-done.14.above_ref = f32[256,256]{1,0:T(8,128)S(1)} collective-permute-done((f32[256,256]{1,0:T(8,128)S(1)}, f32[256,256]{1,0:T(8,128)S(1)}, u32[]{:S(2)}, u32[]{:S(2)}) %collective-permute-start.14) | collective-permute-done | bytes 262176 | tf_op jit(solution)/shard_map/ppermute | solution.py:59
  29.3 2.7 %shard_map.50.refs_0_ = f32[256,256]{1,0:T(8,128)S(1)} custom-call(f32[512,256]{1,0:T(8,128)S(1)} %get-tuple-element.20.own, f32[512,256]{1,0:T(8,128)S(1)} %get-tuple-element.21.upper, f32[512,256]{1,0:T(8,128)S(1)} %collective-permute-done.12.mirror, f32[264,256]{1,0:T(8,128)S(1)} %collective-permute-done.1.eigen, ...), custom_call_target="tpu_custom_call" | custom-call | flops 1207959552 | bytes 3682304 | tf_op jit(solution)/shard_map/pallas_call | solution.py:189
  32.0 2.0 %collective-permute-start.17 = (f32[256,256]{1,0:T(8,128)S(1)}, f32[256,256]{1,0:T(8,128)S(1)}, u32[]{:S(2)}, u32[]{:S(2)}) collective-permute-start(f32[256,256]{1,0:T(8,128)S(1)} %shard_map.50.refs_0_), channel_id=1, source_target_pairs={{0,4},{4,0},{11,15},{15,11},{18,22},{22,18},{25,29},{29,25}} | collective-permute-start | bytes 786440 | tf_op jit(solution)/shard_map/ppermute | solution.py:59
  34.0 1.3 %collective-permute-start.18 = (f32[256,256]{1,0:T(8,128)S(1)}, f32[256,256]{1,0:T(8,128)S(1)}, u32[]{:S(2)}, u32[]{:S(2)}) collective-permute-start(f32[256,256]{1,0:T(8,128)S(1)} %shard_map.50.refs_0_), channel_id=1, source_target_pairs={{0,6},{4,2},{11,9},{15,13},{18,16},{22,20},{25,31},{29,27}} | collective-permute-start | bytes 786440 | tf_op jit(solution)/shard_map/ppermute | solution.py:59
  35.3 1.3 %collective-permute-start.15 = (f32[256,256]{1,0:T(8,128)S(1)}, f32[256,256]{1,0:T(8,128)S(1)}, u32[]{:S(2)}, u32[]{:S(2)}) collective-permute-start(f32[256,256]{1,0:T(8,128)S(1)} %shard_map.50.refs_0_), channel_id=1, source_target_pairs={{0,2},{4,6},{11,13},{15,9},{18,20},{22,16},{25,27},{29,31}} | collective-permute-start | bytes 786440 | tf_op jit(solution)/shard_map/ppermute | solution.py:59
  36.6 0.0 collective-permute-done.7.refs_3_
  36.7 0.7 collective-permute-start.8
  37.3 3.6 %collective-permute-done.17.refs_3_ = f32[256,256]{1,0:T(8,128)S(1)} collective-permute-done((f32[256,256]{1,0:T(8,128)S(1)}, f32[256,256]{1,0:T(8,128)S(1)}, u32[]{:S(2)}, u32[]{:S(2)}) %collective-permute-start.17) | collective-permute-done | bytes 262176 | tf_op jit(solution)/shard_map/ppermute | solution.py:59
  40.9 0.7 collective-permute-start.4
  41.6 0.1 collective-permute-done.18.refs_4_
  41.7 1.3 %collective-permute-start.5 = (f32[256,256]{1,0:T(8,128)S(1)}, f32[256,256]{1,0:T(8,128)S(1)}, u32[]{:S(2)}, u32[]{:S(2)}) collective-permute-start(f32[256,256]{1,0:T(8,128)S(1)} %shard_map.47.refs_0_), channel_id=1, source_target_pairs={{3,29},{7,25},{10,20},{14,16},{21,15},{28,6}} | collective-permute-start | bytes 786440 | tf_op jit(solution)/shard_map/ppermute | solution.py:59
  43.0 4.3 %collective-permute-done.15.refs_1_ = f32[256,256]{1,0:T(8,128)S(1)} collective-permute-done((f32[256,256]{1,0:T(8,128)S(1)}, f32[256,256]{1,0:T(8,128)S(1)}, u32[]{:S(2)}, u32[]{:S(2)}) %collective-permute-start.15) | collective-permute-done | bytes 262176 | tf_op jit(solution)/shard_map/ppermute | solution.py:59
  47.4 4.7 %collective-permute-start.19 = (f32[256,256]{1,0:T(8,128)S(1)}, f32[256,256]{1,0:T(8,128)S(1)}, u32[]{:S(2)}, u32[]{:S(2)}) collective-permute-start(f32[256,256]{1,0:T(8,128)S(1)} %add.39), channel_id=1, source_target_pairs={{4,5},{6,7},{0,1},{2,3},{15,14},{9,8},{11,10},{13,12},{22,23},{16,... | collective-permute-start | bytes 786440 | tf_op jit(solution)/shard_map/ppermute | solution.py:59
  52.1 1.3 %collective-permute-start.16 = (f32[256,256]{1,0:T(8,128)S(1)}, f32[256,256]{1,0:T(8,128)S(1)}, u32[]{:S(2)}, u32[]{:S(2)}) collective-permute-start(f32[256,256]{1,0:T(8,128)S(1)} %add.38), channel_id=1, source_target_pairs={{0,1},{2,3},{4,5},{6,7},{11,10},{13,12},{15,14},{9,8},{18,19},{20,... | collective-permute-start | bytes 786440 | tf_op jit(solution)/shard_map/ppermute | solution.py:59
  53.5 0.0 collective-permute-done.3.refs_7_
  53.5 1.3 %collective-permute-start.21 = (f32[512,256]{1,0:T(8,128)S(1)}, f32[512,256]{1,0:T(8,128)S(1)}, u32[]{:S(2)}, u32[]{:S(2)}) collective-permute-start(f32[512,256]{1,0:T(8,128)S(1)} %get-tuple-element.22), channel_id=1, source_target_pairs={{15,23},{22,30},{23,31}} | collective-permute-start | bytes 1572872 | tf_op jit(solution)/shard_map/ppermute | solution.py:59
  54.9 0.7 collective-permute-start.9
  55.6 0.0 collective-permute-done.5.refs_7_
  55.6 1.3 %collective-permute-start.10 = (f32[256,256]{1,0:T(8,128)S(1)}, f32[256,256]{1,0:T(8,128)S(1)}, u32[]{:S(2)}, u32[]{:S(2)}) collective-permute-start(f32[256,256]{1,0:T(8,128)S(1)} %shard_map.47.refs_0_), channel_id=1, source_target_pairs={{7,29},{14,20},{17,15},{21,11},{24,6},{28,2}} | collective-permute-start | bytes 786440 | tf_op jit(solution)/shard_map/ppermute | solution.py:59
  56.9 0.1 add_add_fusion.1
  56.9 0.0 copy-start.1
  57.0 3.3 %collective-permute-start.6 = (f32[256,256]{1,0:T(8,128)S(1)}, f32[256,256]{1,0:T(8,128)S(1)}, u32[]{:S(2)}, u32[]{:S(2)}) collective-permute-start(f32[256,256]{1,0:T(8,128)S(1)} %add_add_fusion.1), channel_id=1, source_target_pairs={{3,2},{5,4},{7,6},{1,0},{10,11},{12,13},{14,15},{8,9},{17,16},{19,... | collective-permute-start | bytes 786440 | tf_op jit(solution)/shard_map/ppermute | solution.py:59
  60.3 0.0 collective-permute-done.16.refs_2_
  60.4 1.9 %collective-permute-start.20 = (f32[512,256]{1,0:T(8,128)S(1)}, f32[512,256]{1,0:T(8,128)S(1)}, u32[]{:S(2)}, u32[]{:S(2)}) collective-permute-start(f32[512,256]{1,0:T(8,128)S(1)} %pad_maximum_fusion), channel_id=1, source_target_pairs={{27,11},{28,12},{29,13},{30,14},{31,15},{9,25},{10,26},{11,27},{12... | collective-permute-start | bytes 1572872 | tf_op jit(solution)/shard_map/ppermute | solution.py:59
  62.4 3.7 %collective-permute-done.10.refs_9_ = f32[256,256]{1,0:T(8,128)S(1)} collective-permute-done((f32[256,256]{1,0:T(8,128)S(1)}, f32[256,256]{1,0:T(8,128)S(1)}, u32[]{:S(2)}, u32[]{:S(2)}) %collective-permute-start.10) | collective-permute-done | bytes 262176 | tf_op jit(solution)/shard_map/ppermute | solution.py:59
  66.1 0.1 add_add_fusion
  66.1 1.9 %collective-permute-start.11 = (f32[256,256]{1,0:T(8,128)S(1)}, f32[256,256]{1,0:T(8,128)S(1)}, u32[]{:S(2)}, u32[]{:S(2)}) collective-permute-start(f32[256,256]{1,0:T(8,128)S(1)} %add_add_fusion), channel_id=1, source_target_pairs={{7,6},{1,0},{3,2},{5,4},{14,15},{8,9},{10,11},{12,13},{21,20},{23,... | collective-permute-start | bytes 786440 | tf_op jit(solution)/shard_map/ppermute | solution.py:59
  68.1 8.2 %collective-permute-done.11.refs_5_ = f32[256,256]{1,0:T(8,128)S(1)} collective-permute-done((f32[256,256]{1,0:T(8,128)S(1)}, f32[256,256]{1,0:T(8,128)S(1)}, u32[]{:S(2)}, u32[]{:S(2)}) %collective-permute-start.11) | collective-permute-done | bytes 262176 | tf_op jit(solution)/shard_map/ppermute | solution.py:59
  76.2 3.1 %shard_map.49.running_ref = f32[4096,128]{1,0:T(8,128)S(1)} custom-call(f32[4096,128]{1,0:T(8,128)S(1)} %bitcast.7, f32[256,256]{1,0:T(8,128)S(1)} %shard_map.47.refs_0_, f32[256,256]{1,0:T(8,128)S(1)} %collective-permute-done.2.refs_1_, f32[256,256]{1,0:T(8,128)S(1)} %collective-permute-done.6.refs_2_, f32[256,256]{1,0:T(8,128)S(1)} %collective-permute-done.7.refs_3_, ...), custom_call_target="tpu_custom_call" | custom-call | flops 1610612736 | bytes 8912896 | tf_op jit(solution)/shard_map/pallas_call | solution.py:189
  79.4 3.7 %shard_map.51 = f32[4096,128]{1,0:T(8,128)} custom-call(f32[4096,128]{1,0:T(8,128)S(1)} %shard_map.49.running_ref, f32[256,256]{1,0:T(8,128)S(1)} %shard_map.50.refs_0_, f32[256,256]{1,0:T(8,128)S(1)} %collective-permute-done.15.refs_1_, f32[256,256]{1,0:T(8,128)S(1)} %collective-permute-done.16.refs_2_, f32[256,256]{1,0:T(8,128)S(1)} %collective-permute-done.17.refs_3_, ...), custom_call_target="tpu_custom_call" | custom-call | flops 1610612736 | bytes 7864320 | tf_op jit(solution)/shard_map/pallas_call | solution.py:189
  (25 shorter events, 0.3 us)
Async XLA Ops:
  0.0 1.6 %copy-start = (f32[4,1,256,2,1,256]{5,4,3,2,1,0:T(1,128)S(1)}, f32[4,1,256,2,1,256]{5,4,3,2,1,0:T(1,128)}, u32[]{:S(2)}) copy-start(f32[4,1,256,2,1,256]{5,4,3,2,1,0:T(1,128)} %param.5) | copy-start | bytes 6291460
  1.6 1.2 %copy-start.3 = (f32[4,1,256,256]{3,2,1,0:T(8,128)S(1)}, f32[4,1,256,256]{3,2,1,0:T(8,128)}, u32[]{:S(2)}) copy-start(f32[4,1,256,256]{3,2,1,0:T(8,128)} %param.6) | copy-start | bytes 3145732
  2.8 0.7 copy-start.5
  3.5 2.3 %copy-start.2 = (f32[4,1,256,2,1,256]{5,4,3,2,1,0:T(1,128)S(1)}, f32[4,1,256,2,1,256]{5,4,3,2,1,0:T(1,128)}, u32[]{:S(2)}) copy-start(f32[4,1,256,2,1,256]{5,4,3,2,1,0:T(1,128)} %param.4) | copy-start | bytes 6291460
  3.7 8.3 %collective-permute-start.1 = (f32[264,256]{1,0:T(8,128)S(1)}, f32[264,256]{1,0:T(8,128)S(1)}, u32[]{:S(2)}, u32[]{:S(2)}) collective-permute-start(f32[264,256]{1,0:T(8,128)S(1)} %get-tuple-element.16), channel_id=1, source_target_pairs={{27,3},{31,7},{18,10},{22,14},{9,17},{13,21},{0,24},{4,28},{26,11}... | collective-permute-start | bytes 811016 | tf_op jit(solution)/shard_map/ppermute | solution.py:59
  5.1 4.2 %collective-permute-start = (f32[256,256]{1,0:T(8,128)S(1)}, f32[256,256]{1,0:T(8,128)S(1)}, u32[]{:S(2)}, u32[]{:S(2)}) collective-permute-start(f32[256,256]{1,0:T(8,128)S(1)} %get-tuple-element.15), channel_id=1, source_target_pairs={{28,3},{24,7},{21,10},{17,14},{14,17},{10,21},{7,24},{3,28}} | collective-permute-start | bytes 786440 | tf_op jit(solution)/shard_map/ppermute | solution.py:59
  6.2 23.1 %copy-start.4 = (f32[4,1,256,256]{3,2,1,0:T(8,128)S(1)}, f32[4,1,256,256]{3,2,1,0:T(8,128)}, u32[]{:S(2)}) copy-start(f32[4,1,256,256]{3,2,1,0:T(8,128)} %param.6) | copy-start | bytes 3145732
  6.3 23.1 %copy-start.6 = (f32[4,1,256]{2,1,0:T(1,128)S(1)}, f32[4,1,256]{2,1,0:T(1,128)}, u32[]{:S(2)}) copy-start(f32[4,1,256]{2,1,0:T(1,128)} %param.7) | copy-start | bytes 12292
  6.3 15.7 %collective-permute-start.12 = (f32[512,256]{1,0:T(8,128)S(1)}, f32[512,256]{1,0:T(8,128)S(1)}, u32[]{:S(2)}, u32[]{:S(2)}) collective-permute-start(f32[512,256]{1,0:T(8,128)S(1)} %get-tuple-element.21.upper), channel_id=1, source_target_pairs={{29,11},{25,15},{22,18},{18,22},{15,25},{11,29}} | collective-permute-start | bytes 1572872 | tf_op jit(solution)/shard_map/ppermute | solution.py:59
  9.2 44.3 %collective-permute-start.3 = (f32[1024,256]{1,0:T(8,128)S(1)}, f32[1024,256]{1,0:T(8,128)S(1)}, u32[]{:S(2)}, u32[]{:S(2)}) collective-permute-start(f32[1024,256]{1,0:T(8,128)S(1)} %get-tuple-element.17), channel_id=1, source_target_pairs={{24,0},{25,1},{26,2},{27,3},{28,4},{29,5},{30,6},{31,7},{0,8},{1,9... | collective-permute-start | bytes 3145736 | tf_op jit(solution)/shard_map/ppermute | solution.py:59
  12.0 14.2 %collective-permute-start.13 = (f32[256,256]{1,0:T(8,128)S(1)}, f32[256,256]{1,0:T(8,128)S(1)}, u32[]{:S(2)}, u32[]{:S(2)}) collective-permute-start(f32[256,256]{1,0:T(8,128)S(1)} %shard_map.47.refs_0_), channel_id=1, source_target_pairs={{7,0},{3,4},{10,11},{14,15},{17,18},{21,22},{24,25},{28,29}} | collective-permute-start | bytes 786440 | tf_op jit(solution)/shard_map/ppermute | solution.py:59
  13.3 16.0 %collective-permute-start.14 = (f32[256,256]{1,0:T(8,128)S(1)}, f32[256,256]{1,0:T(8,128)S(1)}, u32[]{:S(2)}, u32[]{:S(2)}) collective-permute-start(f32[256,256]{1,0:T(8,128)S(1)} %shard_map.47.refs_0_), channel_id=1, source_target_pairs={{24,0},{28,4},{3,11},{7,15},{10,18},{14,22},{17,25},{21,29}} | collective-permute-start | bytes 786440 | tf_op jit(solution)/shard_map/ppermute | solution.py:59
  14.6 20.7 %collective-permute-start.2 = (f32[256,256]{1,0:T(8,128)S(1)}, f32[256,256]{1,0:T(8,128)S(1)}, u32[]{:S(2)}, u32[]{:S(2)}) collective-permute-start(f32[256,256]{1,0:T(8,128)S(1)} %shard_map.47.refs_0_), channel_id=1, source_target_pairs={{3,5},{7,1},{10,12},{14,8},{17,19},{21,23},{24,26},{28,30}} | collective-permute-start | bytes 786440 | tf_op jit(solution)/shard_map/ppermute | solution.py:59
  21.9 14.7 %collective-permute-start.7 = (f32[256,256]{1,0:T(8,128)S(1)}, f32[256,256]{1,0:T(8,128)S(1)}, u32[]{:S(2)}, u32[]{:S(2)}) collective-permute-start(f32[256,256]{1,0:T(8,128)S(1)} %shard_map.47.refs_0_), channel_id=1, source_target_pairs={{3,7},{7,3},{10,14},{14,10},{17,21},{21,17},{24,28},{28,24}} | collective-permute-start | bytes 786440 | tf_op jit(solution)/shard_map/ppermute | solution.py:59
  32.0 8.9 %collective-permute-start.17 = (f32[256,256]{1,0:T(8,128)S(1)}, f32[256,256]{1,0:T(8,128)S(1)}, u32[]{:S(2)}, u32[]{:S(2)}) collective-permute-start(f32[256,256]{1,0:T(8,128)S(1)} %shard_map.50.refs_0_), channel_id=1, source_target_pairs={{0,4},{4,0},{11,15},{15,11},{18,22},{22,18},{25,29},{29,25}} | collective-permute-start | bytes 786440 | tf_op jit(solution)/shard_map/ppermute | solution.py:59
  34.0 7.7 %collective-permute-start.18 = (f32[256,256]{1,0:T(8,128)S(1)}, f32[256,256]{1,0:T(8,128)S(1)}, u32[]{:S(2)}, u32[]{:S(2)}) collective-permute-start(f32[256,256]{1,0:T(8,128)S(1)} %shard_map.50.refs_0_), channel_id=1, source_target_pairs={{0,6},{4,2},{11,9},{15,13},{18,16},{22,20},{25,31},{29,27}} | collective-permute-start | bytes 786440 | tf_op jit(solution)/shard_map/ppermute | solution.py:59
  35.3 12.1 %collective-permute-start.15 = (f32[256,256]{1,0:T(8,128)S(1)}, f32[256,256]{1,0:T(8,128)S(1)}, u32[]{:S(2)}, u32[]{:S(2)}) collective-permute-start(f32[256,256]{1,0:T(8,128)S(1)} %shard_map.50.refs_0_), channel_id=1, source_target_pairs={{0,2},{4,6},{11,13},{15,9},{18,20},{22,16},{25,27},{29,31}} | collective-permute-start | bytes 786440 | tf_op jit(solution)/shard_map/ppermute | solution.py:59
  36.7 15.5 %collective-permute-start.8 = (f32[256,256]{1,0:T(8,128)S(1)}, f32[256,256]{1,0:T(8,128)S(1)}, u32[]{:S(2)}, u32[]{:S(2)}) collective-permute-start(f32[256,256]{1,0:T(8,128)S(1)} %shard_map.47.refs_0_), channel_id=1, source_target_pairs={{3,1},{7,5},{10,8},{14,12},{17,23},{21,19},{24,30},{28,26}} | collective-permute-start | bytes 786440 | tf_op jit(solution)/shard_map/ppermute | solution.py:59
  40.9 13.9 %collective-permute-start.4 = (f32[256,256]{1,0:T(8,128)S(1)}, f32[256,256]{1,0:T(8,128)S(1)}, u32[]{:S(2)}, u32[]{:S(2)}) collective-permute-start(f32[256,256]{1,0:T(8,128)S(1)} %shard_map.47.refs_0_), channel_id=1, source_target_pairs={{7,31},{14,22},{21,13},{28,4}} | collective-permute-start | bytes 786440 | tf_op jit(solution)/shard_map/ppermute | solution.py:59
  41.7 13.9 %collective-permute-start.5 = (f32[256,256]{1,0:T(8,128)S(1)}, f32[256,256]{1,0:T(8,128)S(1)}, u32[]{:S(2)}, u32[]{:S(2)}) collective-permute-start(f32[256,256]{1,0:T(8,128)S(1)} %shard_map.47.refs_0_), channel_id=1, source_target_pairs={{3,29},{7,25},{10,20},{14,16},{21,15},{28,6}} | collective-permute-start | bytes 786440 | tf_op jit(solution)/shard_map/ppermute | solution.py:59
  47.4 9.6 %collective-permute-start.19 = (f32[256,256]{1,0:T(8,128)S(1)}, f32[256,256]{1,0:T(8,128)S(1)}, u32[]{:S(2)}, u32[]{:S(2)}) collective-permute-start(f32[256,256]{1,0:T(8,128)S(1)} %add.39), channel_id=1, source_target_pairs={{4,5},{6,7},{0,1},{2,3},{15,14},{9,8},{11,10},{13,12},{22,23},{16,... | collective-permute-start | bytes 786440 | tf_op jit(solution)/shard_map/ppermute | solution.py:59
  52.1 8.2 %collective-permute-start.16 = (f32[256,256]{1,0:T(8,128)S(1)}, f32[256,256]{1,0:T(8,128)S(1)}, u32[]{:S(2)}, u32[]{:S(2)}) collective-permute-start(f32[256,256]{1,0:T(8,128)S(1)} %add.38), channel_id=1, source_target_pairs={{0,1},{2,3},{4,5},{6,7},{11,10},{13,12},{15,14},{9,8},{18,19},{20,... | collective-permute-start | bytes 786440 | tf_op jit(solution)/shard_map/ppermute | solution.py:59
  53.5 25.8 %collective-permute-start.21 = (f32[512,256]{1,0:T(8,128)S(1)}, f32[512,256]{1,0:T(8,128)S(1)}, u32[]{:S(2)}, u32[]{:S(2)}) collective-permute-start(f32[512,256]{1,0:T(8,128)S(1)} %get-tuple-element.22), channel_id=1, source_target_pairs={{15,23},{22,30},{23,31}} | collective-permute-start | bytes 1572872 | tf_op jit(solution)/shard_map/ppermute | solution.py:59
  54.9 7.5 %collective-permute-start.9 = (f32[256,256]{1,0:T(8,128)S(1)}, f32[256,256]{1,0:T(8,128)S(1)}, u32[]{:S(2)}, u32[]{:S(2)}) collective-permute-start(f32[256,256]{1,0:T(8,128)S(1)} %shard_map.47.refs_0_), channel_id=1, source_target_pairs={{3,31},{7,27},{10,22},{14,18}} | collective-permute-start | bytes 786440 | tf_op jit(solution)/shard_map/ppermute | solution.py:59
  55.6 10.5 %collective-permute-start.10 = (f32[256,256]{1,0:T(8,128)S(1)}, f32[256,256]{1,0:T(8,128)S(1)}, u32[]{:S(2)}, u32[]{:S(2)}) collective-permute-start(f32[256,256]{1,0:T(8,128)S(1)} %shard_map.47.refs_0_), channel_id=1, source_target_pairs={{7,29},{14,20},{17,15},{21,11},{24,6},{28,2}} | collective-permute-start | bytes 786440 | tf_op jit(solution)/shard_map/ppermute | solution.py:59
  56.9 19.3 %copy-start.1 = (f32[4,1,256,2,1,256]{5,4,3,2,1,0:T(1,128)S(1)}, f32[4,1,256,2,1,256]{5,4,3,2,1,0:T(1,128)}, u32[]{:S(2)}) copy-start(f32[4,1,256,2,1,256]{5,4,3,2,1,0:T(1,128)} %param.5) | copy-start | bytes 6291460
  57.0 11.1 %collective-permute-start.6 = (f32[256,256]{1,0:T(8,128)S(1)}, f32[256,256]{1,0:T(8,128)S(1)}, u32[]{:S(2)}, u32[]{:S(2)}) collective-permute-start(f32[256,256]{1,0:T(8,128)S(1)} %add_add_fusion.1), channel_id=1, source_target_pairs={{3,2},{5,4},{7,6},{1,0},{10,11},{12,13},{14,15},{8,9},{17,16},{19,... | collective-permute-start | bytes 786440 | tf_op jit(solution)/shard_map/ppermute | solution.py:59
  60.4 18.9 %collective-permute-start.20 = (f32[512,256]{1,0:T(8,128)S(1)}, f32[512,256]{1,0:T(8,128)S(1)}, u32[]{:S(2)}, u32[]{:S(2)}) collective-permute-start(f32[512,256]{1,0:T(8,128)S(1)} %pad_maximum_fusion), channel_id=1, source_target_pairs={{27,11},{28,12},{29,13},{30,14},{31,15},{9,25},{10,26},{11,27},{12... | collective-permute-start | bytes 1572872 | tf_op jit(solution)/shard_map/ppermute | solution.py:59
  66.1 10.1 %collective-permute-start.11 = (f32[256,256]{1,0:T(8,128)S(1)}, f32[256,256]{1,0:T(8,128)S(1)}, u32[]{:S(2)}, u32[]{:S(2)}) collective-permute-start(f32[256,256]{1,0:T(8,128)S(1)} %add_add_fusion), channel_id=1, source_target_pairs={{7,6},{1,0},{3,2},{5,4},{14,15},{8,9},{10,11},{12,13},{21,20},{23,... | collective-permute-start | bytes 786440 | tf_op jit(solution)/shard_map/ppermute | solution.py:59

commit v5 on v4

--- a/solution.py
+++ b/solution.py
@@ -11,12 +11,11 @@
 LIMIT = 40 * 1024 * 1024
 LINE = 4
 GATE_SPREAD = "none"
-GATE_PANEL = "none"
-GATE_FORWARD = "often"
+GATE_PANEL = "solved"
+GATE_FORWARD = "none"
 GATE_SOLVE = "none"
-PACK_SEEN = None
-DIRECT = (True, False)
 GATE_LOW = "none"
+GATE_SECOND = ("own","often")
 
 
 def product(first, second, dims=((1,), (0,))):
@@ -92,44 +91,38 @@
         k = d - (solved_row(d, c) * rows + r)
         return {(k % rows, at) for at in range(cols) if wants(k, d, at)}
 
-    def spread_moves(d, sources, direct):
+    def spread_moves(d, sources):
         own, turned = {}, {}
         for source in sources:
             own[source], turned[source] = needs(d, source), needs_turned(d, source)
-            if not direct:
+            if d == count:
                 own[source] = own[source] | {(source[0], at) for _, at in turned[source]}
-                turned[source] = set()
-
-        def line_moves(by, used, target_row):
+
+        def in_group(used, r, at):
+            return any((r, step(at, n)) in used for n in range(stride))
+
+        shifts, across = [], set()
+        steps, steps_turned = ({n: set() for n in range(1, stride)} for _ in range(2))
+        for by in range(LINE):
             moves = []
             for r, c in sources:
-                at = shift(c, by)
-                if any((target_row(r), step(at, n)) in used[r, c] for n in range(stride)):
-                    moves.append(((r, c), (target_row(r), at)))
-            return moves
-
-        def group_moves(half, n, used, target_row):
-            moves = []
-            for r, c in sources:
-                for by in (2 * half, 2 * half + 1):
-                    at = shift(c, by)
-                    if (target_row(r), step(at, n)) in used[r, c]:
-                        moves.append(((target_row(r), at), (target_row(r), step(at, n))))
-            return moves
-
-        same, other = (lambda r: r), (lambda r: (d - r) % rows)
-        shifts = [line_moves(by, own, same) for by in range(LINE)]
-        shifts_turned = [line_moves(by, turned, other) for by in range(LINE)]
-        steps, steps_turned = {}, {}
-        for half in range(2):
-            for n in range(1, stride):
-                steps[half, n] = group_moves(half, n, own, same)
-                steps_turned[half, n] = group_moves(half, n, turned, other)
-        return shifts, shifts_turned, steps, steps_turned
-
-    def across_moves(d, sources):
-        targets = set().union(*(needs_turned(d, source) for source in sources))
-        return [(((d - t) % rows, c), (t, c)) for t, c in sorted(targets)]
+                at, other = shift(c, by), (d - r) % rows
+                here, there = in_group(own[r, c], r, at), in_group(turned[r, c], other, at)
+                if here or (d < count and there):
+                    moves.append(((r, c), (r, at)))
+                if d < count and there:
+                    across.add(((r, at), (other, at)))
+                for n in range(1, stride):
+                    near = step(at, n)
+                    if (r, near) in own[r, c]:
+                        steps[n].add(((r, at), (r, near)))
+                    if d < count and (other, near) in turned[r, c]:
+                        steps_turned[n].add(((other, at), (other, near)))
+            shifts.append(moves)
+        if d == count:
+            targets = set().union(*turned.values())
+            across = {(((d - t) % rows, c), (t, c)) for t, c in targets}
+        return shifts[1:], steps, steps_turned, sorted(across)
 
     def reached(device, p, q):
         k = p * rows + device[0]
@@ -184,8 +177,8 @@
         def near_row(d, c, q):
             return jnp.clip(local_row(d, c, q), 0, 3)
 
-        def call(body, outputs, operands, specs=None, scratch=(), flops=0, seen=None):
-            moved = sum(4 * int(np.prod(o.shape)) for o in (*operands, *outputs)) if seen is None else seen
+        def call(body, outputs, operands, specs=None, scratch=(), flops=0):
+            moved = sum(4 * int(np.prod(o.shape)) for o in (*operands, *outputs))
             return pl.pallas_call(
                 body,
                 out_shape=outputs,
@@ -286,66 +279,141 @@
             def _():
                 out[...] = jnp.zeros_like(out)
 
-        def update(d, running, shares, sources, rows_of_a):
-            arrays = []
-            for share in shares:
-                for array, _, _ in share:
-                    if not any(array is other for other in arrays):
-                        arrays.append(array)
-
-            def body(running_ref, *refs):
+        def block_sum(refs, half):
+            total = refs[0][part(half), :]
+            for ref in refs[1:]:
+                total = total + ref[part(half), :]
+            return total
+
+        def half_of(r, c, d, k):
+            source = jnp.minimum(k, d - k) % cols
+            return (c // stride - source // stride) % LINE // 2
+
+        def update(running, panel, spread_first, spread_second, sources):
+            own_first, low_first, steps_first, steps_low = spread_first
+            own_second, steps_second = spread_second
+            operands = (
+                running, panel, own_first, *steps_first, low_first, *steps_low, own_second, *steps_second,
+                *sources,
+            )
+
+            def body(running_ref, panel_ref, *refs):
                 r, c = here()
-                parts, given = refs[: len(arrays)], refs[len(arrays) : -2]
-                out, blocks = refs[-2], refs[-1]
-                for index, share in enumerate(shares):
-                    total = None
-                    residue = (d - r if index < 2 else r) % stride
-                    for array, row, n in share:
-                        ref = next(p for p, a in zip(parts, arrays) if a is array)
-                        value = ref[part(row), :]
-                        if n and d < count:
-                            value = jnp.where((c - n) % stride == residue, value, 0.0)
-                        total = value if total is None else total + value
-                    blocks[index] = total
+                first_refs, low_refs = refs[:stride], refs[stride : 2 * stride]
+                second_refs, refs = refs[2 * stride : 3 * stride], refs[3 * stride :]
+                given, out, blocks = refs[: len(sources)], refs[len(sources)], refs[len(sources) + 1]
+                for half in range(2):
+                    blocks[half] = block_sum(first_refs, half)
+                    blocks[2 + half] = block_sum(low_refs, half)
+                    blocks[4 + half] = block_sum(second_refs, half)
+                inside = within(r)
                 for p in range(4):
                     k = p * rows + r
-                    partner = d - k
-                    source = jnp.minimum(k, partner) % cols
-                    half = (c // stride - source // stride) % LINE // 2
-                    turned = 2 * k < d
-                    index = half + 2 * turned.astype(jnp.int32)
-                    if d == count:
-                        index = jnp.where(within(r), half, index)
-
-                    def block():
-                        found = blocks[index]
-                        return jnp.where(turned, found.T, found) if p < 3 else found
+                    partner = count - 1 - k
+
+                    def block_first():
+                        found = blocks[half_of(r, c, count - 1, k) + (2 if p < 2 else 0)]
+                        return found.T if p < 2 else found
+
+                    def block_second():
+                        found = blocks[4 + half_of(r, c, count, k)]
+                        return found.T if p < 2 else found
 
                     for q in range(2):
                         at = q * cols + c
                         old = read(running_ref, p, q)
                         write(out, p, q, old)
-                        a_block = rows_of_a(given, p, q)
-                        if a_block is not None:
-
-                            @pl.when((at > partner) & (partner < count))
-                            def _():
-                                write(out, p, q, old - product(block(), a_block()))
+                        if p < 2 and q == 0:
+                            continue
+                        a_second = next_rows(given, p, q)
 
                         @pl.when(at == partner)
                         def _():
-                            write(out, p, q, block())
+                            write(out, p, q, block_first())
+
+                        known = inside if p < 2 else at == at
+
+                        @pl.when((at == partner + 1) & known)
+                        def _():
+                            write(out, p, q, block_second())
+
+                        if a_second is None:
+                            continue
+
+                        @pl.when((at > partner + 1) & known)
+                        def _():
+                            change = product(block_first(), read(panel_ref, p, q))
+                            change = change + product(block_second(), a_second())
+                            write(out, p, q, old - change)
+
+                        if p < 2:
+
+                            @pl.when((at > partner + 1) & jnp.logical_not(known))
+                            def _():
+                                write(out, p, q, old - product(block_first(), read(panel_ref, p, q)))
 
             return call(
                 body,
                 [jax.ShapeDtypeStruct(running.shape, jnp.float32)],
-                (running, *arrays, *sources),
-                scratch=[pltpu.VMEM((4, width, width), jnp.float32)],
+                operands,
+                scratch=[pltpu.VMEM((6, width, width), jnp.float32)],
                 flops=16 * width**3 * 6,
             )[0]
 
-        def own_rows(given, p, q):
-            return lambda: read(given[0], p, q)
+        def finish(running, low, sources):
+            def body(running_ref, low_ref, *refs):
+                given, out, slabs, sems = refs[: len(sources)], refs[-3], refs[-2], refs[-1]
+                r, c = here()
+                at = cols + c
+                del running_ref
+
+                def touched(p):
+                    return jnp.logical_not(within(r)) & (at >= count - (p * rows + r))
+
+                for p in range(2):
+
+                    @pl.when(touched(p))
+                    def _():
+                        pltpu.make_async_copy(out.at[pl.ds(p * slab, slab)], slabs.at[p], sems.at[p]).start()
+
+                for p in range(2):
+                    k = p * rows + r
+
+                    @pl.when(touched(p))
+                    def _():
+                        pltpu.make_async_copy(out.at[pl.ds(p * slab, slab)], slabs.at[p], sems.at[p]).wait()
+                        start = pl.multiple_of(half_of(r, c, count, k) * width, width)
+                        block = low_ref[pl.ds(start, width), :].T
+                        a_block = next_rows(given, p, 1)
+
+                        @pl.when(at == count - k)
+                        def _():
+                            write(slabs.at[p], 0, 1, block)
+
+                        @pl.when(at > count - k)
+                        def _():
+                            write(slabs.at[p], 0, 1, read(slabs.at[p], 0, 1) - product(block, a_block()))
+
+                        pltpu.make_async_copy(slabs.at[p], out.at[pl.ds(p * slab, slab)], sems.at[p]).start()
+
+                for p in range(2):
+
+                    @pl.when(touched(p))
+                    def _():
+                        pltpu.make_async_copy(slabs.at[p], out.at[pl.ds(p * slab, slab)], sems.at[p]).wait()
+
+            return pl.pallas_call(
+                body,
+                out_shape=jax.ShapeDtypeStruct(running.shape, jnp.float32),
+                in_specs=[hbm] + [vmem] * (1 + len(sources)),
+                out_specs=hbm,
+                scratch_shapes=[pltpu.VMEM((2, slab, LANES), jnp.float32), pltpu.SemaphoreType.DMA((2,))],
+                input_output_aliases={0: 0},
+                compiler_params=pltpu.CompilerParams(vmem_limit_bytes=LIMIT),
+                cost_estimate=pl.CostEstimate(
+                    flops=2 * width**3 * 12, bytes_accessed=4 * slab * LANES * 4, transcendentals=0
+                ),
+            )(running, low, *sources)
 
         def next_rows(given, p, q):
             for ref, chosen in zip(given, (common, seldom)):
@@ -354,61 +422,45 @@
                     return lambda: ref[part(index), :]
             return None
 
-        def spread(value, d, sources, direct, held=(), held_turned=()):
-            shifts, shifts_turned, steps, steps_turned = spread_moves(d, sources, direct)
-            moved = [value] + [send(value, moves) for moves in shifts[1:]]
-            shares = [[(array, 0, 0) for array in moved[2 * half : 2 * half + 2]] for half in range(2)]
-            if not direct:
-                for half in range(2):
-                    both = after(moved[2 * half] + moved[2 * half + 1], *held)
-                    for n in range(1, stride):
-                        shares[half].append((send(both, steps[half, n]), 0, n))
-                pair = jnp.concatenate([sum(a for a, _, _ in share) for share in shares], axis=0)
-                got = send(pair, across_moves(d, sources))
-                return shares + [[(got, 0, 0)], [(got, 1, 0)]]
-            low = after(value, *held_turned)
-            low_moved = [send(low, moves) for moves in shifts_turned]
-            shares += [[(array, 0, 0) for array in low_moved[2 * half : 2 * half + 2]] for half in range(2)]
-            for half in range(2):
-                both = after(moved[2 * half] + moved[2 * half + 1], *held)
-                both_low = low_moved[2 * half] + low_moved[2 * half + 1]
-                for n in range(1, stride):
-                    if d < count:
-                        got = send(both + both_low, steps[half, n] + steps_turned[half, n])
-                        shares[half].append((got, 0, n))
-                        shares[2 + half].append((got, 0, n))
-                    else:
-                        shares[half].append((send(both, steps[half, n]), 0, n))
-                        shares[2 + half].append((send(both_low, steps_turned[half, n]), 0, n))
-            return shares
+        def spread(value, d, sources, held=(), held_low=()):
+            shifts, steps, steps_turned, across = spread_moves(d, sources)
+            moved = [value] + [send(value, moves) for moves in shifts]
+            pair = jnp.concatenate([moved[0] + moved[1], moved[2] + moved[3]], axis=0)
+            pair = after(pair, *held)
+            got = [send(pair, sorted(steps[n])) for n in range(1, stride)]
+            if d < count:
+                low = send(after(pair, *held_low), across)
+                return pair, low, got, [send(low, sorted(steps_turned[n])) for n in range(1, stride)]
+            return pair, got, send(sum(got, pair), across)
+
+        def in_hbm(*arrays):
+            return tuple(pltpu.with_memory_space_constraint(array, pltpu.HBM) for array in arrays)
 
         solve_flops = 4 * 2 * 6 * width**3
 
         own, upper, eigen = call(
             pack_first,
             [blocks_shape(1), blocks_shape(1), blocks_shape(1, 8)],
-            (running, own_basis, own_values),
+            in_hbm(running, own_basis, own_values),
             specs=[hbm, hbm, hbm],
             scratch=[
                 pltpu.VMEM((2, slab, LANES), jnp.float32),
                 pltpu.VMEM((4 * halves, LANES), jnp.float32),
                 pltpu.SemaphoreType.DMA((4,)),
             ],
-            seen=PACK_SEEN,
         )
         mirror = send(upper, mirror_first)
         eigen = send(eigen, far)
         own_pair, upper_pair, often, rarely = call(
             pack_second,
             [blocks_shape(2), blocks_shape(2), blocks_shape(len(common)), blocks_shape(len(seldom))],
-            (running, panel),
+            in_hbm(after(running, own), panel),
             specs=[hbm, hbm],
             scratch=[
                 pltpu.VMEM((2, slab, LANES), jnp.float32),
                 pltpu.VMEM((4 * slab, LANES), jnp.float32),
                 pltpu.SemaphoreType.DMA((3,)),
             ],
-            seen=PACK_SEEN,
         )
         pair_mirror = send(upper_pair, mirror_second)
         (solved,) = call(
@@ -432,18 +484,14 @@
         )
         options["next"] = (solved_next,)
         options["often"], options["both"] = (often,), (often, rarely)
-        shares = spread(
-            after(solved, *options[GATE_SPREAD]),
-            count - 1,
-            first,
-            DIRECT[0],
-            options[GATE_FORWARD],
-            options[GATE_LOW],
+        spread_first = spread(
+            after(solved, *options[GATE_SPREAD]), count - 1, first, options[GATE_FORWARD], options[GATE_LOW]
         )
-        running = update(count - 1, running, shares, [panel], own_rows)
-
-        shares = spread(solved_next, count, second, DIRECT[1])
-        running = update(count, running, shares, [often, rarely], next_rows)
+        pair, low, got, got_low = spread_first
+        earlier = {"often": often, "rarely": rarely, "own": got[0], "low": low, "turned": got_low[0]}
+        *spread_second, low = spread(solved_next, count, second, [earlier[name] for name in GATE_SECOND])
+        running = update(running, panel, spread_first, spread_second, [often, rarely])
+        running = finish(running, low, [often, rarely])
         return running.reshape(state.shape)
 
     placed = (

time: 83.7 us -> 71.3 us (0.85)
  the two profiles are of different devices: /device:TPU:27 before, /device:TPU:29 now
where the time goes in v5:
time: 71.3 us; the launch traced here: 70 us
  starting transfers between devices  35 us (49%)
  waiting for transfers between devices  22.4 us (31%)
  Pallas kernels  11.9 us (17%)
    ppermute x18, starting transfers between devices, send(): lax.ppermute(value, AXES, [(s[0] * cols + s[1], t[0] * cols + t[1]) for s...  35 us
    ppermute x18, waiting for transfers between devices, send(): lax.ppermute(value, AXES, [(s[0] * cols + s[1], t[0] * cols + t[1]) for s...  22.4 us
    pallas_call x5, Pallas kernels, call(): pl.pallas_call(body, out_shape=outputs, in_specs=specs or [vmem] * len(op...  9 us
    pallas_call x1, Pallas kernels, finish(): pl.pallas_call(body, out_shape=jax.ShapeDtypeStruct(running.shape, jnp.fl...  2.9 us
  transfers between devices with their start and end apart: 18, of which 6 were waited for; matrix products, arithmetic and copies ran while one was open for 0% of the time, Pallas kernels for 11%

profile of v5, /device:TPU:29, one launch (start us, length us, event | category | flops | bytes accessed | tf_op | source)
XLA Modules:
  0.0 70.0 jit_solution(13337443605843387984)
XLA Ops:
  0.0 1.3 %shard_map.46 = (f32[256,256]{1,0:T(8,128)S(1)}, f32[256,256]{1,0:T(8,128)S(1)}, f32[264,256]{1,0:T(8,128)S(1)}) custom-call(f32[4096,128]{1,0:T(8,128)} %bitcast.5, f32[4,256,256]{2,1,0:T(8,128)} %bitcast.10, f32[8,128]{1,0:T(8,128)} %bitcast.13), custom_call_target="tpu_custom_call" | custom-call | bytes 3944448 | tf_op jit(solution)/shard_map/pallas_call | solution.py:182
  1.3 3.1 %collective-permute-start.1 = (f32[264,256]{1,0:T(8,128)S(1)}, f32[264,256]{1,0:T(8,128)S(1)}, u32[]{:S(2)}, u32[]{:S(2)}) collective-permute-start(f32[264,256]{1,0:T(8,128)S(1)} %get-tuple-element.18), channel_id=1, source_target_pairs={{27,3},{31,7},{18,10},{22,14},{9,17},{13,21},{0,24},{4,28},{26,11}... | collective-permute-start | bytes 811016 | tf_op jit(solution)/shard_map/ppermute | solution.py:58
  4.4 0.7 collective-permute-start
  5.1 0.0 copy-start.2
  5.1 0.0 copy-start.3
  5.1 2.2 %shard_map.48 = (f32[512,256]{1,0:T(8,128)S(1)}, f32[512,256]{1,0:T(8,128)S(1)}, f32[1024,256]{1,0:T(8,128)S(1)}, f32[512,256]{1,0:T(8,128)S(1)}) custom-call(f32[4096,128]{1,0:T(8,128)} %bitcast.6, f32[4096,128]{1,0:T(8,128)} %bitcast.8), custom_call_target="tpu_custom_call" | custom-call | bytes 6815744 | tf_op jit(solution)/shard_map/pallas_call | solution.py:182
  7.3 0.0 collective-permute-done.mirror
  7.3 0.5 collective-permute-done.1.eigen
  7.8 0.0 copy-done.2
  7.8 0.0 copy-done.3
  7.8 1.3 %collective-permute-start.4 = (f32[256,256]{1,0:T(8,128)S(1)}, f32[256,256]{1,0:T(8,128)S(1)}, u32[]{:S(2)}, u32[]{:S(2)}) collective-permute-start(f32[256,256]{1,0:T(8,128)S(1)} %shard_map.47), channel_id=1, source_target_pairs={{3,1},{7,5},{10,8},{14,12},{17,23},{21,19},{24,30},{28,26}} | collective-permute-start | bytes 786440 | tf_op jit(solution)/shard_map/ppermute | solution.py:58
  9.1 0.7 collective-permute-start.8
  9.8 1.3 %collective-permute-start.2 = (f32[256,256]{1,0:T(8,128)S(1)}, f32[256,256]{1,0:T(8,128)S(1)}, u32[]{:S(2)}, u32[]{:S(2)}) collective-permute-start(f32[256,256]{1,0:T(8,128)S(1)} %shard_map.47), channel_id=1, source_target_pairs={{3,5},{7,1},{10,12},{14,8},{17,19},{21,23},{24,26},{28,30}} | collective-permute-start | bytes 786440 | tf_op jit(solution)/shard_map/ppermute | solution.py:58
  11.1 0.1 collective-permute-start.14
  11.2 0.7 collective-permute-start.3
  11.9 9.4 %collective-permute-done.4 = f32[256,256]{1,0:T(8,128)S(1)} collective-permute-done((f32[256,256]{1,0:T(8,128)S(1)}, f32[256,256]{1,0:T(8,128)S(1)}, u32[]{:S(2)}, u32[]{:S(2)}) %collective-permute-start.4) | collective-permute-done | bytes 262176 | tf_op jit(solution)/shard_map/ppermute | solution.py:58
  21.3 0.7 collective-permute-start.10
  21.9 3.8 %collective-permute-done.2 = f32[256,256]{1,0:T(8,128)S(1)} collective-permute-done((f32[256,256]{1,0:T(8,128)S(1)}, f32[256,256]{1,0:T(8,128)S(1)}, u32[]{:S(2)}, u32[]{:S(2)}) %collective-permute-start.2) | collective-permute-done | bytes 262176 | tf_op jit(solution)/shard_map/ppermute | solution.py:58
  25.7 0.7 collective-permute-start.9
  26.4 0.0 collective-permute-done.3
  26.5 1.3 %collective-permute-start.5 = (f32[512,256]{1,0:T(8,128)S(1)}, f32[512,256]{1,0:T(8,128)S(1)}, u32[]{:S(2)}, u32[]{:S(2)}) collective-permute-start(f32[512,256]{1,0:T(8,128)S(1)} %pad_maximum_fusion.refs_0_), channel_id=1, source_target_pairs={{1,0},{3,2},{5,4},{7,6},{8,9},{10,11},{12,13},{14,15},{17,16},{19,... | collective-permute-start | bytes 1572872 | tf_op jit(solution)/shard_map/ppermute | solution.py:58
  27.9 0.0 collective-permute-done.8.mirror
  27.9 0.0 collective-permute-done.10.above_ref
  27.9 0.0 collective-permute-done.9.left_ref
  27.9 0.0 copy-start
  28.0 0.0 copy-start.1
  28.0 0.8 %collective-permute-start.11 = (f32[256,256]{1,0:T(8,128)S(1)}, f32[256,256]{1,0:T(8,128)S(1)}, u32[]{:S(2)}, u32[]{:S(2)}) collective-permute-start(f32[256,256]{1,0:T(8,128)S(1)} %shard_map.49), channel_id=1, source_target_pairs={{0,2},{4,6},{11,13},{15,9},{18,20},{22,16},{25,27},{29,31}} | collective-permute-start | bytes 786440 | tf_op jit(solution)/shard_map/ppermute | solution.py:58
  28.8 0.8 %collective-permute-start.13 = (f32[256,256]{1,0:T(8,128)S(1)}, f32[256,256]{1,0:T(8,128)S(1)}, u32[]{:S(2)}, u32[]{:S(2)}) collective-permute-start(f32[256,256]{1,0:T(8,128)S(1)} %shard_map.49), channel_id=1, source_target_pairs={{0,6},{4,2},{11,9},{15,13},{18,16},{22,20},{25,31},{29,27}} | collective-permute-start | bytes 786440 | tf_op jit(solution)/shard_map/ppermute | solution.py:58
  29.6 0.7 collective-permute-start.12
  30.3 0.0 collective-permute-done.11
  30.3 15.4 %collective-permute-start.6 = (f32[512,256]{1,0:T(8,128)S(1)}, f32[512,256]{1,0:T(8,128)S(1)}, u32[]{:S(2)}, u32[]{:S(2)}) collective-permute-start(f32[512,256]{1,0:T(8,128)S(1)} %pad_maximum_fusion.refs_0_), channel_id=1, source_target_pairs={{1,25},{3,27},{5,29},{7,31},{8,16},{10,18},{12,20},{14,22},{19,11}... | collective-permute-start | bytes 1572872 | tf_op jit(solution)/shard_map/ppermute | solution.py:58
  45.7 0.0 collective-permute-done.13
  45.7 0.0 collective-permute-done.12
  45.8 0.0 collective-permute-done.5.refs_1_
  45.8 0.0 collective-permute-done.14.refs_6_.refs_0_
  45.8 1.3 %collective-permute-start.15 = (f32[512,256]{1,0:T(8,128)S(1)}, f32[512,256]{1,0:T(8,128)S(1)}, u32[]{:S(2)}, u32[]{:S(2)}) collective-permute-start(f32[512,256]{1,0:T(8,128)S(1)} %pad_maximum_fusion.1.refs_4_), channel_id=1, source_target_pairs={{0,1},{2,3},{4,5},{6,7},{9,8},{11,10},{13,12},{15,14},{16,17},{18,... | collective-permute-start | bytes 1572872 | tf_op jit(solution)/shard_map/ppermute | solution.py:58
  47.1 1.3 %collective-permute-start.16 = (f32[512,256]{1,0:T(8,128)S(1)}, f32[512,256]{1,0:T(8,128)S(1)}, u32[]{:S(2)}, u32[]{:S(2)}) collective-permute-start(f32[512,256]{1,0:T(8,128)S(1)} %get-tuple-element.26), channel_id=1, source_target_pairs={{15,23},{22,30},{23,31}} | collective-permute-start | bytes 1572872 | tf_op jit(solution)/shard_map/ppermute | solution.py:58
  48.4 3.3 %collective-permute-done.6.refs_2_ = f32[512,256]{1,0:T(8,128)S(1)} collective-permute-done((f32[512,256]{1,0:T(8,128)S(1)}, f32[512,256]{1,0:T(8,128)S(1)}, u32[]{:S(2)}, u32[]{:S(2)}) %collective-permute-start.6) | collective-permute-done | bytes 524320 | tf_op jit(solution)/shard_map/ppermute | solution.py:58
  51.7 1.3 %collective-permute-start.7 = (f32[512,256]{1,0:T(8,128)S(1)}, f32[512,256]{1,0:T(8,128)S(1)}, u32[]{:S(2)}, u32[]{:S(2)}) collective-permute-start(f32[512,256]{1,0:T(8,128)S(1)} %collective-permute-done.6.refs_2_), channel_id=1, source_target_pairs={{2,3},{4,5},{6,7},{11,10},{13,12},{15,14},{16,17},{18,19},{20,21},... | collective-permute-start | bytes 1572872 | tf_op jit(solution)/shard_map/ppermute | solution.py:58
  53.0 2.7 %collective-permute-done.15.refs_5_ = f32[512,256]{1,0:T(8,128)S(1)} collective-permute-done((f32[512,256]{1,0:T(8,128)S(1)}, f32[512,256]{1,0:T(8,128)S(1)}, u32[]{:S(2)}, u32[]{:S(2)}) %collective-permute-start.15) | collective-permute-done | bytes 524320 | tf_op jit(solution)/shard_map/ppermute | solution.py:58
  55.8 0.1 add.19
  55.8 3.1 %collective-permute-start.17 = (f32[512,256]{1,0:T(8,128)S(1)}, f32[512,256]{1,0:T(8,128)S(1)}, u32[]{:S(2)}, u32[]{:S(2)}) collective-permute-start(f32[512,256]{1,0:T(8,128)S(1)} %add.19), channel_id=1, source_target_pairs={{9,25},{10,26},{11,27},{12,28},{13,29},{14,30},{15,31},{27,11},{28... | collective-permute-start | bytes 1572872 | tf_op jit(solution)/shard_map/ppermute | solution.py:58
  58.9 0.0 collective-permute-done.16.refs_7_.refs_1_
  58.9 2.7 %collective-permute-done.7.refs_3_ = f32[512,256]{1,0:T(8,128)S(1)} collective-permute-done((f32[512,256]{1,0:T(8,128)S(1)}, f32[512,256]{1,0:T(8,128)S(1)}, u32[]{:S(2)}, u32[]{:S(2)}) %collective-permute-start.7) | collective-permute-done | bytes 524320 | tf_op jit(solution)/shard_map/ppermute | solution.py:58
  61.6 0.0 copy-done
  61.6 5.4 %shard_map.50.running_ref = f32[4096,128]{1,0:T(8,128)} custom-call(f32[4096,128]{1,0:T(8,128)S(1)} %bitcast.7, f32[4096,128]{1,0:T(8,128)S(1)} %bitcast.9, f32[512,256]{1,0:T(8,128)S(1)} %pad_maximum_fusion.refs_0_, f32[512,256]{1,0:T(8,128)S(1)} %collective-permute-done.5.refs_1_, f32[512,256]{1,0:T(8,128)S(1)} %collective-permute-done.6.refs_2_, ...), custom_call_target="tpu_custom_call" | custom-call | flops 1610612736 | bytes 11010048 | tf_op jit(solution)/shard_map/pallas_call | solution.py:182
  67.1 0.0 collective-permute-done.17.low_ref
  67.1 2.9 %shard_map.51 = f32[4096,128]{1,0:T(8,128)} custom-call(f32[4096,128]{1,0:T(8,128)} %shard_map.50.running_ref, f32[512,256]{1,0:T(8,128)S(1)} %collective-permute-done.17.low_ref, f32[1024,256]{1,0:T(8,128)S(1)} %collective-permute-done.14.refs_6_.refs_0_, f32[512,256]{1,0:T(8,128)S(1)} %collective-permute-done.16.refs_7_.refs_1_), custom_call_target="tpu_custom_call", output_to_operand_aliasing={{}: (0, {})} | custom-call | flops 402653184 | bytes 2097152 | tf_op jit(solution)/shard_map/pallas_call | solution.py:405
  (9 shorter events, 0.3 us)
Async XLA Ops:
  1.3 6.5 %collective-permute-start.1 = (f32[264,256]{1,0:T(8,128)S(1)}, f32[264,256]{1,0:T(8,128)S(1)}, u32[]{:S(2)}, u32[]{:S(2)}) collective-permute-start(f32[264,256]{1,0:T(8,128)S(1)} %get-tuple-element.18), channel_id=1, source_target_pairs={{27,3},{31,7},{18,10},{22,14},{9,17},{13,21},{0,24},{4,28},{26,11}... | collective-permute-start | bytes 811016 | tf_op jit(solution)/shard_map/ppermute | solution.py:58
  4.4 2.9 %collective-permute-start = (f32[256,256]{1,0:T(8,128)S(1)}, f32[256,256]{1,0:T(8,128)S(1)}, u32[]{:S(2)}, u32[]{:S(2)}) collective-permute-start(f32[256,256]{1,0:T(8,128)S(1)} %get-tuple-element.17), channel_id=1, source_target_pairs={{28,3},{24,7},{21,10},{17,14},{14,17},{10,21},{7,24},{3,28}} | collective-permute-start | bytes 786440 | tf_op jit(solution)/shard_map/ppermute | solution.py:58
  5.1 2.7 %copy-start.2 = (f32[4,1,256,256]{3,2,1,0:T(8,128)S(1)}, f32[4,1,256,256]{3,2,1,0:T(8,128)}, u32[]{:S(2)}) copy-start(f32[4,1,256,256]{3,2,1,0:T(8,128)} %param.6) | copy-start | bytes 3145732
  5.1 2.7 %copy-start.3 = (f32[4,1,256]{2,1,0:T(1,128)S(1)}, f32[4,1,256]{2,1,0:T(1,128)}, u32[]{:S(2)}) copy-start(f32[4,1,256]{2,1,0:T(1,128)} %param.7) | copy-start | bytes 12292
  7.8 13.4 %collective-permute-start.4 = (f32[256,256]{1,0:T(8,128)S(1)}, f32[256,256]{1,0:T(8,128)S(1)}, u32[]{:S(2)}, u32[]{:S(2)}) collective-permute-start(f32[256,256]{1,0:T(8,128)S(1)} %shard_map.47), channel_id=1, source_target_pairs={{3,1},{7,5},{10,8},{14,12},{17,23},{21,19},{24,30},{28,26}} | collective-permute-start | bytes 786440 | tf_op jit(solution)/shard_map/ppermute | solution.py:58
  9.1 18.7 %collective-permute-start.8 = (f32[512,256]{1,0:T(8,128)S(1)}, f32[512,256]{1,0:T(8,128)S(1)}, u32[]{:S(2)}, u32[]{:S(2)}) collective-permute-start(f32[512,256]{1,0:T(8,128)S(1)} %get-tuple-element.21.upper), channel_id=1, source_target_pairs={{29,11},{25,15},{22,18},{18,22},{15,25},{11,29}} | collective-permute-start | bytes 1572872 | tf_op jit(solution)/shard_map/ppermute | solution.py:58
  9.8 15.9 %collective-permute-start.2 = (f32[256,256]{1,0:T(8,128)S(1)}, f32[256,256]{1,0:T(8,128)S(1)}, u32[]{:S(2)}, u32[]{:S(2)}) collective-permute-start(f32[256,256]{1,0:T(8,128)S(1)} %shard_map.47), channel_id=1, source_target_pairs={{3,5},{7,1},{10,12},{14,8},{17,19},{21,23},{24,26},{28,30}} | collective-permute-start | bytes 786440 | tf_op jit(solution)/shard_map/ppermute | solution.py:58
  11.1 34.7 %collective-permute-start.14 = (f32[1024,256]{1,0:T(8,128)S(1)}, f32[1024,256]{1,0:T(8,128)S(1)}, u32[]{:S(2)}, u32[]{:S(2)}) collective-permute-start(f32[1024,256]{1,0:T(8,128)S(1)} %get-tuple-element.23), channel_id=1, source_target_pairs={{24,0},{25,1},{26,2},{27,3},{28,4},{29,5},{30,6},{31,7},{0,8},{1,9... | collective-permute-start | bytes 3145736 | tf_op jit(solution)/shard_map/ppermute | solution.py:58
  11.2 15.2 %collective-permute-start.3 = (f32[256,256]{1,0:T(8,128)S(1)}, f32[256,256]{1,0:T(8,128)S(1)}, u32[]{:S(2)}, u32[]{:S(2)}) collective-permute-start(f32[256,256]{1,0:T(8,128)S(1)} %shard_map.47), channel_id=1, source_target_pairs={{3,7},{7,3},{10,14},{14,10},{17,21},{21,17},{24,28},{28,24}} | collective-permute-start | bytes 786440 | tf_op jit(solution)/shard_map/ppermute | solution.py:58
  21.3 6.6 %collective-permute-start.10 = (f32[256,256]{1,0:T(8,128)S(1)}, f32[256,256]{1,0:T(8,128)S(1)}, u32[]{:S(2)}, u32[]{:S(2)}) collective-permute-start(f32[256,256]{1,0:T(8,128)S(1)} %shard_map.47), channel_id=1, source_target_pairs={{24,0},{28,4},{3,11},{7,15},{10,18},{14,22},{17,25},{21,29}} | collective-permute-start | bytes 786440 | tf_op jit(solution)/shard_map/ppermute | solution.py:58
  25.7 2.2 %collective-permute-start.9 = (f32[256,256]{1,0:T(8,128)S(1)}, f32[256,256]{1,0:T(8,128)S(1)}, u32[]{:S(2)}, u32[]{:S(2)}) collective-permute-start(f32[256,256]{1,0:T(8,128)S(1)} %shard_map.47), channel_id=1, source_target_pairs={{7,0},{3,4},{10,11},{14,15},{17,18},{21,22},{24,25},{28,29}} | collective-permute-start | bytes 786440 | tf_op jit(solution)/shard_map/ppermute | solution.py:58
  26.5 19.3 %collective-permute-start.5 = (f32[512,256]{1,0:T(8,128)S(1)}, f32[512,256]{1,0:T(8,128)S(1)}, u32[]{:S(2)}, u32[]{:S(2)}) collective-permute-start(f32[512,256]{1,0:T(8,128)S(1)} %pad_maximum_fusion.refs_0_), channel_id=1, source_target_pairs={{1,0},{3,2},{5,4},{7,6},{8,9},{10,11},{12,13},{14,15},{17,16},{19,... | collective-permute-start | bytes 1572872 | tf_op jit(solution)/shard_map/ppermute | solution.py:58
  27.9 33.7 %copy-start = (f32[4,1,256,2,1,256]{5,4,3,2,1,0:T(1,128)S(1)}, f32[4,1,256,2,1,256]{5,4,3,2,1,0:T(1,128)}, u32[]{:S(2)}) copy-start(f32[4,1,256,2,1,256]{5,4,3,2,1,0:T(1,128)} %param.5) | copy-start | bytes 6291460
  28.0 33.7 %copy-start.1 = (f32[4,1,256,2,1,256]{5,4,3,2,1,0:T(1,128)S(1)}, f32[4,1,256,2,1,256]{5,4,3,2,1,0:T(1,128)}, u32[]{:S(2)}) copy-start(f32[4,1,256,2,1,256]{5,4,3,2,1,0:T(1,128)} %param.4) | copy-start | bytes 6291460
  28.0 2.3 %collective-permute-start.11 = (f32[256,256]{1,0:T(8,128)S(1)}, f32[256,256]{1,0:T(8,128)S(1)}, u32[]{:S(2)}, u32[]{:S(2)}) collective-permute-start(f32[256,256]{1,0:T(8,128)S(1)} %shard_map.49), channel_id=1, source_target_pairs={{0,2},{4,6},{11,13},{15,9},{18,20},{22,16},{25,27},{29,31}} | collective-permute-start | bytes 786440 | tf_op jit(solution)/shard_map/ppermute | solution.py:58
  28.8 16.9 %collective-permute-start.13 = (f32[256,256]{1,0:T(8,128)S(1)}, f32[256,256]{1,0:T(8,128)S(1)}, u32[]{:S(2)}, u32[]{:S(2)}) collective-permute-start(f32[256,256]{1,0:T(8,128)S(1)} %shard_map.49), channel_id=1, source_target_pairs={{0,6},{4,2},{11,9},{15,13},{18,16},{22,20},{25,31},{29,27}} | collective-permute-start | bytes 786440 | tf_op jit(solution)/shard_map/ppermute | solution.py:58
  29.6 16.1 %collective-permute-start.12 = (f32[256,256]{1,0:T(8,128)S(1)}, f32[256,256]{1,0:T(8,128)S(1)}, u32[]{:S(2)}, u32[]{:S(2)}) collective-permute-start(f32[256,256]{1,0:T(8,128)S(1)} %shard_map.49), channel_id=1, source_target_pairs={{0,4},{4,0},{11,15},{15,11},{18,22},{22,18},{25,29},{29,25}} | collective-permute-start | bytes 786440 | tf_op jit(solution)/shard_map/ppermute | solution.py:58
  30.3 21.4 %collective-permute-start.6 = (f32[512,256]{1,0:T(8,128)S(1)}, f32[512,256]{1,0:T(8,128)S(1)}, u32[]{:S(2)}, u32[]{:S(2)}) collective-permute-start(f32[512,256]{1,0:T(8,128)S(1)} %pad_maximum_fusion.refs_0_), channel_id=1, source_target_pairs={{1,25},{3,27},{5,29},{7,31},{8,16},{10,18},{12,20},{14,22},{19,11}... | collective-permute-start | bytes 1572872 | tf_op jit(solution)/shard_map/ppermute | solution.py:58
  45.8 9.9 %collective-permute-start.15 = (f32[512,256]{1,0:T(8,128)S(1)}, f32[512,256]{1,0:T(8,128)S(1)}, u32[]{:S(2)}, u32[]{:S(2)}) collective-permute-start(f32[512,256]{1,0:T(8,128)S(1)} %pad_maximum_fusion.1.refs_4_), channel_id=1, source_target_pairs={{0,1},{2,3},{4,5},{6,7},{9,8},{11,10},{13,12},{15,14},{16,17},{18,... | collective-permute-start | bytes 1572872 | tf_op jit(solution)/shard_map/ppermute | solution.py:58
  47.1 11.8 %collective-permute-start.16 = (f32[512,256]{1,0:T(8,128)S(1)}, f32[512,256]{1,0:T(8,128)S(1)}, u32[]{:S(2)}, u32[]{:S(2)}) collective-permute-start(f32[512,256]{1,0:T(8,128)S(1)} %get-tuple-element.26), channel_id=1, source_target_pairs={{15,23},{22,30},{23,31}} | collective-permute-start | bytes 1572872 | tf_op jit(solution)/shard_map/ppermute | solution.py:58
  51.7 9.9 %collective-permute-start.7 = (f32[512,256]{1,0:T(8,128)S(1)}, f32[512,256]{1,0:T(8,128)S(1)}, u32[]{:S(2)}, u32[]{:S(2)}) collective-permute-start(f32[512,256]{1,0:T(8,128)S(1)} %collective-permute-done.6.refs_2_), channel_id=1, source_target_pairs={{2,3},{4,5},{6,7},{11,10},{13,12},{15,14},{16,17},{18,19},{20,21},... | collective-permute-start | bytes 1572872 | tf_op jit(solution)/shard_map/ppermute | solution.py:58
  55.8 11.3 %collective-permute-start.17 = (f32[512,256]{1,0:T(8,128)S(1)}, f32[512,256]{1,0:T(8,128)S(1)}, u32[]{:S(2)}, u32[]{:S(2)}) collective-permute-start(f32[512,256]{1,0:T(8,128)S(1)} %add.19), channel_id=1, source_target_pairs={{9,25},{10,26},{11,27},{12,28},{13,29},{14,30},{15,31},{27,11},{28... | collective-permute-start | bytes 1572872 | tf_op jit(solution)/shard_map/ppermute | solution.py:58

commit v6 on v5

--- a/solution.py
+++ b/solution.py
@@ -15,7 +15,9 @@
 GATE_FORWARD = "none"
 GATE_SOLVE = "none"
 GATE_LOW = "none"
-GATE_SECOND = ("own","often")
+GATE_SECOND = ("own", "often")
+PACK_EARLY = True
+ONE_PANEL = False
 
 
 def product(first, second, dims=((1,), (0,))):
@@ -26,6 +28,19 @@
         precision=lax.Precision.HIGHEST,
         preferred_element_type=jnp.float32,
     )
+
+
+def quick_product(first, second):
+    parts = []
+    for value in (first, second):
+        high = value.astype(jnp.bfloat16)
+        parts.append((high, (value - high.astype(jnp.float32)).astype(jnp.bfloat16)))
+    (high, low), (other_high, other_low) = parts
+
+    def one_pass(a, b):
+        return jnp.dot(a, b, preferred_element_type=jnp.float32)
+
+    return one_pass(high, other_high) + (one_pass(high, other_low) + one_pass(low, other_high))
 
 
 def solution(mesh):
@@ -130,7 +145,11 @@
 
     slots = [(p, q) for p in range(4) for q in range(2)]
     common = [s for s in slots if reached((rows // 2, cols // 2), *s)]
+    if ONE_PANEL:
+        common = [s for s in slots if any(reached(device, *s) for device in devices)]
     seldom = [s for s in slots if s not in common and any(reached(device, *s) for device in devices)]
+
+    messages = [chosen for chosen in (common, seldom) if chosen]
 
     def panel_moves(chosen):
         return [
@@ -210,7 +229,8 @@
                 copy.wait()
             eigen[width:, :] = jnp.broadcast_to(values_at(values, index), (8, width))
 
-        def pack_second(state_ref, panel_ref, own, upper, often, rarely, slabs, panel_slabs, sems):
+        def pack_second(state_ref, panel_ref, own, upper, *refs):
+            targets, (slabs, panel_slabs, sems) = refs[:-3], refs[-3:]
             r, c = here()
             places = [near_row(count, c, q) for q in range(2)]
             copies = [slab_copy(state_ref, places[q], slabs.at[q], sems.at[q]) for q in range(2)]
@@ -223,7 +243,7 @@
                 target[part(0), :] = read(slabs.at[q], 0, q)
                 target[part(1), :] = read(panel_slabs, places[q], q)
             last = (r == rows - 1).astype(jnp.int32)
-            for target, chosen in ((often, common), (rarely, seldom)):
+            for target, chosen in zip(targets, messages):
                 for index, (p, q) in enumerate(chosen):
                     target[part(index), :] = read(panel_slabs, jnp.maximum(p - last, 0), q)
 
@@ -279,133 +299,119 @@
             def _():
                 out[...] = jnp.zeros_like(out)
 
-        def block_sum(refs, half):
-            total = refs[0][part(half), :]
-            for ref in refs[1:]:
-                total = total + ref[part(half), :]
-            return total
-
         def half_of(r, c, d, k):
             source = jnp.minimum(k, d - k) % cols
             return (c // stride - source // stride) % LINE // 2
 
-        def update(running, panel, spread_first, spread_second, sources):
-            own_first, low_first, steps_first, steps_low = spread_first
-            own_second, steps_second = spread_second
-            operands = (
-                running, panel, own_first, *steps_first, low_first, *steps_low, own_second, *steps_second,
-                *sources,
-            )
-
+        def block_at(refs, half):
+            where = pl.ds(pl.multiple_of(half * width, width), width)
+            return sum((ref[where, :] for ref in refs[1:]), refs[0][where, :])
+
+        def settle(p, q, old, first_block, second_block, a_first, a_second, store):
+            r, c = here()
+            at, partner = q * cols + c, count - 1 - (p * rows + r)
+
+            @pl.when(at == partner)
+            def _():
+                store(first_block())
+
+            @pl.when(at == partner + 1)
+            def _():
+                store(second_block())
+
+            if a_second is not None:
+
+                @pl.when(at > partner + 1)
+                def _():
+                    change = quick_product(first_block(), a_first())
+                    store(old() - (change + quick_product(second_block(), a_second())))
+
+        def update(running, panel, own_first, own_second, sources):
             def body(running_ref, panel_ref, *refs):
                 r, c = here()
-                first_refs, low_refs = refs[:stride], refs[stride : 2 * stride]
-                second_refs, refs = refs[2 * stride : 3 * stride], refs[3 * stride :]
-                given, out, blocks = refs[: len(sources)], refs[len(sources)], refs[len(sources) + 1]
-                for half in range(2):
-                    blocks[half] = block_sum(first_refs, half)
-                    blocks[2 + half] = block_sum(low_refs, half)
-                    blocks[4 + half] = block_sum(second_refs, half)
-                inside = within(r)
-                for p in range(4):
+                first_refs, second_refs, given = refs[:stride], refs[stride : 2 * stride], refs[2 * stride : -1]
+                out = refs[-1]
+                out[: 2 * slab, :] = running_ref[: 2 * slab, :]
+                for p in (2, 3):
                     k = p * rows + r
-                    partner = count - 1 - k
-
-                    def block_first():
-                        found = blocks[half_of(r, c, count - 1, k) + (2 if p < 2 else 0)]
-                        return found.T if p < 2 else found
-
-                    def block_second():
-                        found = blocks[4 + half_of(r, c, count, k)]
-                        return found.T if p < 2 else found
-
                     for q in range(2):
-                        at = q * cols + c
-                        old = read(running_ref, p, q)
-                        write(out, p, q, old)
-                        if p < 2 and q == 0:
-                            continue
-                        a_second = next_rows(given, p, q)
-
-                        @pl.when(at == partner)
-                        def _():
-                            write(out, p, q, block_first())
-
-                        known = inside if p < 2 else at == at
-
-                        @pl.when((at == partner + 1) & known)
-                        def _():
-                            write(out, p, q, block_second())
-
-                        if a_second is None:
-                            continue
-
-                        @pl.when((at > partner + 1) & known)
-                        def _():
-                            change = product(block_first(), read(panel_ref, p, q))
-                            change = change + product(block_second(), a_second())
-                            write(out, p, q, old - change)
-
-                        if p < 2:
-
-                            @pl.when((at > partner + 1) & jnp.logical_not(known))
-                            def _():
-                                write(out, p, q, old - product(block_first(), read(panel_ref, p, q)))
+                        write(out, p, q, read(running_ref, p, q))
+                        settle(
+                            p,
+                            q,
+                            lambda: read(running_ref, p, q),
+                            lambda: block_at(first_refs, half_of(r, c, count - 1, k)),
+                            lambda: block_at(second_refs, half_of(r, c, count, k)),
+                            lambda: read(panel_ref, p, q),
+                            next_rows(given, p, q),
+                            lambda value: write(out, p, q, value),
+                        )
 
             return call(
                 body,
                 [jax.ShapeDtypeStruct(running.shape, jnp.float32)],
-                operands,
-                scratch=[pltpu.VMEM((6, width, width), jnp.float32)],
+                (running, panel, *own_first, *own_second, *sources),
                 flops=16 * width**3 * 6,
             )[0]
 
-        def finish(running, low, sources):
-            def body(running_ref, low_ref, *refs):
-                given, out, slabs, sems = refs[: len(sources)], refs[-3], refs[-2], refs[-1]
+        def finish(running, panel, low_first, own_second, low_second, sources):
+            def body(running_ref, panel_ref, *refs):
+                del running_ref
                 r, c = here()
+                first_refs, second_refs = refs[:stride], refs[stride : 2 * stride]
+                turned_ref, given = refs[2 * stride], refs[2 * stride + 1 : -3]
+                out, slabs, sems = refs[-3:]
                 at = cols + c
-                del running_ref
 
                 def touched(p):
-                    return jnp.logical_not(within(r)) & (at >= count - (p * rows + r))
+                    return at >= count - 1 - (p * rows + r)
+
+                def slab_in(p):
+                    return pltpu.make_async_copy(out.at[pl.ds(p * slab, slab)], slabs.at[p], sems.at[p])
+
+                def slab_out(p):
+                    return pltpu.make_async_copy(slabs.at[p], out.at[pl.ds(p * slab, slab)], sems.at[p])
 
                 for p in range(2):
 
                     @pl.when(touched(p))
                     def _():
-                        pltpu.make_async_copy(out.at[pl.ds(p * slab, slab)], slabs.at[p], sems.at[p]).start()
+                        slab_in(p).start()
 
                 for p in range(2):
                     k = p * rows + r
 
+                    def second_block():
+                        half = half_of(r, c, count, k)
+                        own = block_at(second_refs, half)
+                        return jnp.where(within(r), own, block_at((turned_ref,), half)).T
+
                     @pl.when(touched(p))
                     def _():
-                        pltpu.make_async_copy(out.at[pl.ds(p * slab, slab)], slabs.at[p], sems.at[p]).wait()
-                        start = pl.multiple_of(half_of(r, c, count, k) * width, width)
-                        block = low_ref[pl.ds(start, width), :].T
-                        a_block = next_rows(given, p, 1)
-
-                        @pl.when(at == count - k)
-                        def _():
-                            write(slabs.at[p], 0, 1, block)
-
-                        @pl.when(at > count - k)
-                        def _():
-                            write(slabs.at[p], 0, 1, read(slabs.at[p], 0, 1) - product(block, a_block()))
-
-                        pltpu.make_async_copy(slabs.at[p], out.at[pl.ds(p * slab, slab)], sems.at[p]).start()
+                        slab_in(p).wait()
+                        settle(
+                            p,
+                            1,
+                            lambda: read(slabs.at[p], 0, 1),
+                            lambda: block_at(first_refs, half_of(r, c, count - 1, k)).T,
+                            second_block,
+                            lambda: read(panel_ref, p, 1),
+                            next_rows(given, p, 1),
+                            lambda value: write(slabs.at[p], 0, 1, value),
+                        )
+                        slab_out(p).start()
 
                 for p in range(2):
 
                     @pl.when(touched(p))
                     def _():
-                        pltpu.make_async_copy(slabs.at[p], out.at[pl.ds(p * slab, slab)], sems.at[p]).wait()
-
+                        slab_out(p).wait()
+
+            operands = (running, panel, *low_first, *own_second, low_second, *sources)
             return pl.pallas_call(
                 body,
                 out_shape=jax.ShapeDtypeStruct(running.shape, jnp.float32),
-                in_specs=[hbm] + [vmem] * (1 + len(sources)),
+                in_specs=[hbm] + [vmem] * (len(operands) - 1),
                 out_specs=hbm,
                 scratch_shapes=[pltpu.VMEM((2, slab, LANES), jnp.float32), pltpu.SemaphoreType.DMA((2,))],
                 input_output_aliases={0: 0},
@@ -413,10 +419,10 @@
                 cost_estimate=pl.CostEstimate(
                     flops=2 * width**3 * 12, bytes_accessed=4 * slab * LANES * 4, transcendentals=0
                 ),
-            )(running, low, *sources)
+            )(*operands)
 
         def next_rows(given, p, q):
-            for ref, chosen in zip(given, (common, seldom)):
+            for ref, chosen in zip(given, messages):
                 if (p, q) in chosen:
                     index = chosen.index((p, q))
                     return lambda: ref[part(index), :]
@@ -451,9 +457,9 @@
         )
         mirror = send(upper, mirror_first)
         eigen = send(eigen, far)
-        own_pair, upper_pair, often, rarely = call(
+        own_pair, upper_pair, *panels = call(
             pack_second,
-            [blocks_shape(2), blocks_shape(2), blocks_shape(len(common)), blocks_shape(len(seldom))],
+            [blocks_shape(2), blocks_shape(2), *(blocks_shape(len(chosen)) for chosen in messages)],
             in_hbm(after(running, own), panel),
             specs=[hbm, hbm],
             scratch=[
@@ -466,15 +472,18 @@
         (solved,) = call(
             solve_first,
             [blocks_shape(1)],
-            (own, mirror, eigen, own_basis, own_values),
+            (after(own, *((own_pair,) if PACK_EARLY else ())), mirror, eigen, own_basis, own_values),
             flops=solve_flops,
         )
 
         before = send(solved, left)
         above_it = send(solved, above)
         options = {"none": (), "solved": (solved,), "before": (before,), "direct": (before, above_it)}
-        often = send(after(often, *options.get(GATE_PANEL, ())), panel_moves(common))
-        rarely = send(after(rarely, *options.get(GATE_PANEL, ())), panel_moves(seldom))
+        panels = [
+            send(after(panel_blocks, *options.get(GATE_PANEL, ())), panel_moves(chosen))
+            for panel_blocks, chosen in zip(panels, messages)
+        ]
+        often, rarely = panels[0], panels[-1]
         ready = {"none": (), "often": (often,), "both": (often, rarely)}[GATE_SOLVE]
         (solved_next,) = call(
             solve_second,
@@ -483,15 +492,20 @@
             flops=3 * solve_flops // 2,
         )
         options["next"] = (solved_next,)
-        options["often"], options["both"] = (often,), (often, rarely)
+        options["often"], options["both"], options["above"] = (often,), (often, rarely), (above_it,)
+        options["mirror"] = (pair_mirror,)
+        options["mirror_above"] = (pair_mirror, above_it)
+        options["all"] = (pair_mirror, above_it, before)
         spread_first = spread(
             after(solved, *options[GATE_SPREAD]), count - 1, first, options[GATE_FORWARD], options[GATE_LOW]
         )
-        pair, low, got, got_low = spread_first
-        earlier = {"often": often, "rarely": rarely, "own": got[0], "low": low, "turned": got_low[0]}
+        pair, low_before, got, got_low = spread_first
+        earlier = {"often": often, "rarely": rarely, "own": got[0], "low": low_before, "turned": got_low[0]}
         *spread_second, low = spread(solved_next, count, second, [earlier[name] for name in GATE_SECOND])
-        running = update(running, panel, spread_first, spread_second, [often, rarely])
-        running = finish(running, low, [often, rarely])
+        pair_next, got_next = spread_second
+        own_second = (pair_next, *got_next)
+        running = update(running, panel, (pair, *got), own_second, panels)
+        running = finish(running, panel, (low_before, *got_low), own_second, low, panels)
         return running.reshape(state.shape)
 
     placed = (

time: 71.3 us -> 70.3 us (0.986)
  the two profiles are of different devices: /device:TPU:29 before, /device:TPU:13 now
where the time goes in v6:
time: 70.3 us; the launch traced here: 69.9 us
  starting transfers between devices  35.6 us (51%)
  waiting for transfers between devices  25 us (36%)
  Pallas kernels  8.64 us (12%)
    ppermute x18, starting transfers between devices, send(): lax.ppermute(value, AXES, [(s[0] * cols + s[1], t[0] * cols + t[1]) for s...  35.6 us
    ppermute x18, waiting for transfers between devices, send(): lax.ppermute(value, AXES, [(s[0] * cols + s[1], t[0] * cols + t[1]) for s...  25 us
    pallas_call x5, Pallas kernels, call(): pl.pallas_call(body, out_shape=outputs, in_specs=specs or [vmem] * len(op...  6.29 us
    pallas_call x1, Pallas kernels, finish(): pl.pallas_call(body, out_shape=jax.ShapeDtypeStruct(running.shape, jnp.fl...  2.35 us
  transfers between devices with their start and end apart: 18, of which 7 were waited for; matrix products, arithmetic and copies ran while one was open for 0% of the time, Pallas kernels for 7%

profile of v6, /device:TPU:13, one launch (start us, length us, event | category | flops | bytes accessed | tf_op | source)
XLA Modules:
  0.0 69.9 jit_solution(2944890289361432632)
XLA Ops:
  0.0 1.3 %shard_map.46 = (f32[256,256]{1,0:T(8,128)S(1)}, f32[256,256]{1,0:T(8,128)S(1)}, f32[264,256]{1,0:T(8,128)S(1)}) custom-call(f32[4096,128]{1,0:T(8,128)} %bitcast.8, f32[4,256,256]{2,1,0:T(8,128)} %bitcast.11, f32[8,128]{1,0:T(8,128)} %bitcast.14), custom_call_target="tpu_custom_call" | custom-call | bytes 3944448 | tf_op jit(solution)/shard_map/pallas_call | solution.py:201
  1.3 3.1 %collective-permute-start.1 = (f32[264,256]{1,0:T(8,128)S(1)}, f32[264,256]{1,0:T(8,128)S(1)}, u32[]{:S(2)}, u32[]{:S(2)}) collective-permute-start(f32[264,256]{1,0:T(8,128)S(1)} %get-tuple-element.22), channel_id=1, source_target_pairs={{27,3},{31,7},{18,10},{22,14},{9,17},{13,21},{0,24},{4,28},{26,11}... | collective-permute-start | bytes 811016 | tf_op jit(solution)/shard_map/ppermute | solution.py:73
  4.4 0.7 collective-permute-start
  5.1 0.0 copy-start.2
  5.1 0.0 copy-start.3
  5.1 2.2 %shard_map.47 = (f32[512,256]{1,0:T(8,128)S(1)}, f32[512,256]{1,0:T(8,128)S(1)}, f32[1024,256]{1,0:T(8,128)S(1)}, f32[512,256]{1,0:T(8,128)S(1)}) custom-call(f32[4096,128]{1,0:T(8,128)} %bitcast.9, f32[4096,128]{1,0:T(8,128)} %bitcast.5), custom_call_target="tpu_custom_call" | custom-call | bytes 6815744 | tf_op jit(solution)/shard_map/pallas_call | solution.py:201
  7.3 0.0 collective-permute-done.mirror
  7.3 0.5 collective-permute-done.1.eigen
  7.8 0.0 copy-done.2
  7.8 0.0 copy-done.3
  7.8 0.1 collective-permute-start.12
  7.9 1.3 %collective-permute-start.4 = (f32[256,256]{1,0:T(8,128)S(1)}, f32[256,256]{1,0:T(8,128)S(1)}, u32[]{:S(2)}, u32[]{:S(2)}) collective-permute-start(f32[256,256]{1,0:T(8,128)S(1)} %shard_map.48), channel_id=1, source_target_pairs={{3,1},{7,5},{10,8},{14,12},{17,23},{21,19},{24,30},{28,26}} | collective-permute-start | bytes 786440 | tf_op jit(solution)/shard_map/ppermute | solution.py:73
  9.2 0.7 collective-permute-start.6
  9.9 1.3 %collective-permute-start.2 = (f32[256,256]{1,0:T(8,128)S(1)}, f32[256,256]{1,0:T(8,128)S(1)}, u32[]{:S(2)}, u32[]{:S(2)}) collective-permute-start(f32[256,256]{1,0:T(8,128)S(1)} %shard_map.48), channel_id=1, source_target_pairs={{3,5},{7,1},{10,12},{14,8},{17,19},{21,23},{24,26},{28,30}} | collective-permute-start | bytes 786440 | tf_op jit(solution)/shard_map/ppermute | solution.py:73
  11.2 0.7 collective-permute-start.3
  11.9 11.6 %collective-permute-done.4 = f32[256,256]{1,0:T(8,128)S(1)} collective-permute-done((f32[256,256]{1,0:T(8,128)S(1)}, f32[256,256]{1,0:T(8,128)S(1)}, u32[]{:S(2)}, u32[]{:S(2)}) %collective-permute-start.4) | collective-permute-done | bytes 262176 | tf_op jit(solution)/shard_map/ppermute | solution.py:73
  23.5 0.7 collective-permute-start.8
  24.1 0.4 collective-permute-done.2
  24.6 0.7 collective-permute-start.7
  25.3 0.0 collective-permute-done.3
  25.4 1.3 %collective-permute-start.5 = (f32[512,256]{1,0:T(8,128)S(1)}, f32[512,256]{1,0:T(8,128)S(1)}, u32[]{:S(2)}, u32[]{:S(2)}) collective-permute-start(f32[512,256]{1,0:T(8,128)S(1)} %pad_maximum_fusion.refs_0_), channel_id=1, source_target_pairs={{1,0},{3,2},{5,4},{7,6},{8,9},{10,11},{12,13},{14,15},{17,16},{19,... | collective-permute-start | bytes 1572872 | tf_op jit(solution)/shard_map/ppermute | solution.py:73
  26.7 0.0 collective-permute-done.6.mirror
  26.7 0.0 collective-permute-done.8.above_ref
  26.7 0.0 collective-permute-done.7.left_ref
  26.8 0.0 copy-start
  26.8 0.0 copy-start.1
  26.8 0.8 %collective-permute-start.9 = (f32[256,256]{1,0:T(8,128)S(1)}, f32[256,256]{1,0:T(8,128)S(1)}, u32[]{:S(2)}, u32[]{:S(2)}) collective-permute-start(f32[256,256]{1,0:T(8,128)S(1)} %shard_map.49), channel_id=1, source_target_pairs={{0,2},{4,6},{11,13},{15,9},{18,20},{22,16},{25,27},{29,31}} | collective-permute-start | bytes 786440 | tf_op jit(solution)/shard_map/ppermute | solution.py:73
  27.6 0.8 %collective-permute-start.11 = (f32[256,256]{1,0:T(8,128)S(1)}, f32[256,256]{1,0:T(8,128)S(1)}, u32[]{:S(2)}, u32[]{:S(2)}) collective-permute-start(f32[256,256]{1,0:T(8,128)S(1)} %shard_map.49), channel_id=1, source_target_pairs={{0,6},{4,2},{11,9},{15,13},{18,16},{22,20},{25,31},{29,27}} | collective-permute-start | bytes 786440 | tf_op jit(solution)/shard_map/ppermute | solution.py:73
  28.4 0.7 collective-permute-start.10
  29.1 0.0 collective-permute-done.9
  29.1 18.3 %collective-permute-start.15 = (f32[512,256]{1,0:T(8,128)S(1)}, f32[512,256]{1,0:T(8,128)S(1)}, u32[]{:S(2)}, u32[]{:S(2)}) collective-permute-start(f32[512,256]{1,0:T(8,128)S(1)} %pad_maximum_fusion.refs_0_), channel_id=1, source_target_pairs={{1,25},{3,27},{5,29},{7,31},{8,16},{10,18},{12,20},{14,22},{19,11}... | collective-permute-start | bytes 1572872 | tf_op jit(solution)/shard_map/ppermute | solution.py:73
  47.5 0.0 collective-permute-done.11
  47.5 0.0 collective-permute-done.10
  47.6 0.0 collective-permute-done.5.refs_1_
  47.6 0.0 collective-permute-done.12.refs_4_.refs_5_
  47.6 1.3 %collective-permute-start.13 = (f32[512,256]{1,0:T(8,128)S(1)}, f32[512,256]{1,0:T(8,128)S(1)}, u32[]{:S(2)}, u32[]{:S(2)}) collective-permute-start(f32[512,256]{1,0:T(8,128)S(1)} %pad_maximum_fusion.1.refs_2_), channel_id=1, source_target_pairs={{0,1},{2,3},{4,5},{6,7},{9,8},{11,10},{13,12},{15,14},{16,17},{18,... | collective-permute-start | bytes 1572872 | tf_op jit(solution)/shard_map/ppermute | solution.py:73
  48.9 0.7 collective-permute-start.14
  49.6 3.9 %collective-permute-done.15.refs_0_ = f32[512,256]{1,0:T(8,128)S(1)} collective-permute-done((f32[512,256]{1,0:T(8,128)S(1)}, f32[512,256]{1,0:T(8,128)S(1)}, u32[]{:S(2)}, u32[]{:S(2)}) %collective-permute-start.15) | collective-permute-done | bytes 524320 | tf_op jit(solution)/shard_map/ppermute | solution.py:73
  53.5 1.3 %collective-permute-start.16 = (f32[512,256]{1,0:T(8,128)S(1)}, f32[512,256]{1,0:T(8,128)S(1)}, u32[]{:S(2)}, u32[]{:S(2)}) collective-permute-start(f32[512,256]{1,0:T(8,128)S(1)} %collective-permute-done.15.refs_0_), channel_id=1, source_target_pairs={{2,3},{4,5},{6,7},{11,10},{13,12},{15,14},{16,17},{18,19},{20,21},... | collective-permute-start | bytes 1572872 | tf_op jit(solution)/shard_map/ppermute | solution.py:73
  54.8 2.7 %collective-permute-done.13.refs_3_ = f32[512,256]{1,0:T(8,128)S(1)} collective-permute-done((f32[512,256]{1,0:T(8,128)S(1)}, f32[512,256]{1,0:T(8,128)S(1)}, u32[]{:S(2)}, u32[]{:S(2)}) %collective-permute-start.13) | collective-permute-done | bytes 524320 | tf_op jit(solution)/shard_map/ppermute | solution.py:73
  57.5 0.1 add.19
  57.6 1.3 %collective-permute-start.17 = (f32[512,256]{1,0:T(8,128)S(1)}, f32[512,256]{1,0:T(8,128)S(1)}, u32[]{:S(2)}, u32[]{:S(2)}) collective-permute-start(f32[512,256]{1,0:T(8,128)S(1)} %add.19), channel_id=1, source_target_pairs={{9,25},{10,26},{11,27},{12,28},{13,29},{14,30},{15,31},{27,11},{28... | collective-permute-start | bytes 1572872 | tf_op jit(solution)/shard_map/ppermute | solution.py:73
  58.9 0.0 collective-permute-done.14.refs_5_.refs_6_
  58.9 0.0 copy-done
  58.9 2.7 %shard_map.50.running_ref = f32[4096,128]{1,0:T(8,128)} custom-call(f32[4096,128]{1,0:T(8,128)S(1)} %bitcast.10, f32[4096,128]{1,0:T(8,128)S(1)} %bitcast.6, f32[512,256]{1,0:T(8,128)S(1)} %pad_maximum_fusion.refs_0_, f32[512,256]{1,0:T(8,128)S(1)} %collective-permute-done.5.refs_1_, f32[512,256]{1,0:T(8,128)S(1)} %pad_maximum_fusion.1.refs_2_, ...), custom_call_target="tpu_custom_call" | custom-call | flops 1610612736 | bytes 9961472 | tf_op jit(solution)/shard_map/pallas_call | solution.py:201
  61.7 1.8 %collective-permute-done.16.refs_1_ = f32[512,256]{1,0:T(8,128)S(1)} collective-permute-done((f32[512,256]{1,0:T(8,128)S(1)}, f32[512,256]{1,0:T(8,128)S(1)}, u32[]{:S(2)}, u32[]{:S(2)}) %collective-permute-start.16) | collective-permute-done | bytes 524320 | tf_op jit(solution)/shard_map/ppermute | solution.py:73
  63.4 4.1 %collective-permute-done.17.refs_4_ = f32[512,256]{1,0:T(8,128)S(1)} collective-permute-done((f32[512,256]{1,0:T(8,128)S(1)}, f32[512,256]{1,0:T(8,128)S(1)}, u32[]{:S(2)}, u32[]{:S(2)}) %collective-permute-start.17) | collective-permute-done | bytes 524320 | tf_op jit(solution)/shard_map/ppermute | solution.py:73
  67.5 2.4 %shard_map.51 = f32[4096,128]{1,0:T(8,128)} custom-call(f32[4096,128]{1,0:T(8,128)} %shard_map.50.running_ref, f32[4096,128]{1,0:T(8,128)S(1)} %bitcast.7, f32[512,256]{1,0:T(8,128)S(1)} %collective-permute-done.15.refs_0_, f32[512,256]{1,0:T(8,128)S(1)} %collective-permute-done.16.refs_1_, ...), custom_call_target="tpu_custom_call", output_to_operand_aliasing={{}: (0, {})} | custom-call | flops 402653184 | bytes 2097152 | tf_op jit(solution)/shard_map/pallas_call | solution.py:411
  (9 shorter events, 0.3 us)
Async XLA Ops:
  1.3 6.5 %collective-permute-start.1 = (f32[264,256]{1,0:T(8,128)S(1)}, f32[264,256]{1,0:T(8,128)S(1)}, u32[]{:S(2)}, u32[]{:S(2)}) collective-permute-start(f32[264,256]{1,0:T(8,128)S(1)} %get-tuple-element.22), channel_id=1, source_target_pairs={{27,3},{31,7},{18,10},{22,14},{9,17},{13,21},{0,24},{4,28},{26,11}... | collective-permute-start | bytes 811016 | tf_op jit(solution)/shard_map/ppermute | solution.py:73
  4.4 2.9 %collective-permute-start = (f32[256,256]{1,0:T(8,128)S(1)}, f32[256,256]{1,0:T(8,128)S(1)}, u32[]{:S(2)}, u32[]{:S(2)}) collective-permute-start(f32[256,256]{1,0:T(8,128)S(1)} %get-tuple-element.21), channel_id=1, source_target_pairs={{28,3},{24,7},{21,10},{17,14},{14,17},{10,21},{7,24},{3,28}} | collective-permute-start | bytes 786440 | tf_op jit(solution)/shard_map/ppermute | solution.py:73
  5.1 2.7 %copy-start.2 = (f32[4,1,256,256]{3,2,1,0:T(8,128)S(1)}, f32[4,1,256,256]{3,2,1,0:T(8,128)}, u32[]{:S(2)}) copy-start(f32[4,1,256,256]{3,2,1,0:T(8,128)} %param.6) | copy-start | bytes 3145732
  5.1 2.7 %copy-start.3 = (f32[4,1,256]{2,1,0:T(1,128)S(1)}, f32[4,1,256]{2,1,0:T(1,128)}, u32[]{:S(2)}) copy-start(f32[4,1,256]{2,1,0:T(1,128)} %param.7) | copy-start | bytes 12292
  7.8 39.8 %collective-permute-start.12 = (f32[1024,256]{1,0:T(8,128)S(1)}, f32[1024,256]{1,0:T(8,128)S(1)}, u32[]{:S(2)}, u32[]{:S(2)}) collective-permute-start(f32[1024,256]{1,0:T(8,128)S(1)} %get-tuple-element.25), channel_id=1, source_target_pairs={{24,0},{25,1},{26,2},{27,3},{28,4},{29,5},{30,6},{31,7},{0,8},{1,9... | collective-permute-start | bytes 3145736 | tf_op jit(solution)/shard_map/ppermute | solution.py:73
  7.9 15.6 %collective-permute-start.4 = (f32[256,256]{1,0:T(8,128)S(1)}, f32[256,256]{1,0:T(8,128)S(1)}, u32[]{:S(2)}, u32[]{:S(2)}) collective-permute-start(f32[256,256]{1,0:T(8,128)S(1)} %shard_map.48), channel_id=1, source_target_pairs={{3,1},{7,5},{10,8},{14,12},{17,23},{21,19},{24,30},{28,26}} | collective-permute-start | bytes 786440 | tf_op jit(solution)/shard_map/ppermute | solution.py:73
  9.2 17.5 %collective-permute-start.6 = (f32[512,256]{1,0:T(8,128)S(1)}, f32[512,256]{1,0:T(8,128)S(1)}, u32[]{:S(2)}, u32[]{:S(2)}) collective-permute-start(f32[512,256]{1,0:T(8,128)S(1)} %get-tuple-element.23.upper), channel_id=1, source_target_pairs={{29,11},{25,15},{22,18},{18,22},{15,25},{11,29}} | collective-permute-start | bytes 1572872 | tf_op jit(solution)/shard_map/ppermute | solution.py:73
  9.9 14.7 %collective-permute-start.2 = (f32[256,256]{1,0:T(8,128)S(1)}, f32[256,256]{1,0:T(8,128)S(1)}, u32[]{:S(2)}, u32[]{:S(2)}) collective-permute-start(f32[256,256]{1,0:T(8,128)S(1)} %shard_map.48), channel_id=1, source_target_pairs={{3,5},{7,1},{10,12},{14,8},{17,19},{21,23},{24,26},{28,30}} | collective-permute-start | bytes 786440 | tf_op jit(solution)/shard_map/ppermute | solution.py:73
  11.2 14.1 %collective-permute-start.3 = (f32[256,256]{1,0:T(8,128)S(1)}, f32[256,256]{1,0:T(8,128)S(1)}, u32[]{:S(2)}, u32[]{:S(2)}) collective-permute-start(f32[256,256]{1,0:T(8,128)S(1)} %shard_map.48), channel_id=1, source_target_pairs={{3,7},{7,3},{10,14},{14,10},{17,21},{21,17},{24,28},{28,24}} | collective-permute-start | bytes 786440 | tf_op jit(solution)/shard_map/ppermute | solution.py:73
  23.5 3.3 %collective-permute-start.8 = (f32[256,256]{1,0:T(8,128)S(1)}, f32[256,256]{1,0:T(8,128)S(1)}, u32[]{:S(2)}, u32[]{:S(2)}) collective-permute-start(f32[256,256]{1,0:T(8,128)S(1)} %shard_map.48), channel_id=1, source_target_pairs={{24,0},{28,4},{3,11},{7,15},{10,18},{14,22},{17,25},{21,29}} | collective-permute-start | bytes 786440 | tf_op jit(solution)/shard_map/ppermute | solution.py:73
  24.6 2.2 %collective-permute-start.7 = (f32[256,256]{1,0:T(8,128)S(1)}, f32[256,256]{1,0:T(8,128)S(1)}, u32[]{:S(2)}, u32[]{:S(2)}) collective-permute-start(f32[256,256]{1,0:T(8,128)S(1)} %shard_map.48), channel_id=1, source_target_pairs={{7,0},{3,4},{10,11},{14,15},{17,18},{21,22},{24,25},{28,29}} | collective-permute-start | bytes 786440 | tf_op jit(solution)/shard_map/ppermute | solution.py:73
  25.4 22.2 %collective-permute-start.5 = (f32[512,256]{1,0:T(8,128)S(1)}, f32[512,256]{1,0:T(8,128)S(1)}, u32[]{:S(2)}, u32[]{:S(2)}) collective-permute-start(f32[512,256]{1,0:T(8,128)S(1)} %pad_maximum_fusion.refs_0_), channel_id=1, source_target_pairs={{1,0},{3,2},{5,4},{7,6},{8,9},{10,11},{12,13},{14,15},{17,16},{19,... | collective-permute-start | bytes 1572872 | tf_op jit(solution)/shard_map/ppermute | solution.py:73
  26.8 32.1 %copy-start = (f32[4,1,256,2,1,256]{5,4,3,2,1,0:T(1,128)S(1)}, f32[4,1,256,2,1,256]{5,4,3,2,1,0:T(1,128)}, u32[]{:S(2)}) copy-start(f32[4,1,256,2,1,256]{5,4,3,2,1,0:T(1,128)} %param.4) | copy-start | bytes 6291460
  26.8 32.1 %copy-start.1 = (f32[4,1,256,2,1,256]{5,4,3,2,1,0:T(1,128)S(1)}, f32[4,1,256,2,1,256]{5,4,3,2,1,0:T(1,128)}, u32[]{:S(2)}) copy-start(f32[4,1,256,2,1,256]{5,4,3,2,1,0:T(1,128)} %param.5) | copy-start | bytes 6291460
  26.8 2.3 %collective-permute-start.9 = (f32[256,256]{1,0:T(8,128)S(1)}, f32[256,256]{1,0:T(8,128)S(1)}, u32[]{:S(2)}, u32[]{:S(2)}) collective-permute-start(f32[256,256]{1,0:T(8,128)S(1)} %shard_map.49), channel_id=1, source_target_pairs={{0,2},{4,6},{11,13},{15,9},{18,20},{22,16},{25,27},{29,31}} | collective-permute-start | bytes 786440 | tf_op jit(solution)/shard_map/ppermute | solution.py:73
  27.6 19.9 %collective-permute-start.11 = (f32[256,256]{1,0:T(8,128)S(1)}, f32[256,256]{1,0:T(8,128)S(1)}, u32[]{:S(2)}, u32[]{:S(2)}) collective-permute-start(f32[256,256]{1,0:T(8,128)S(1)} %shard_map.49), channel_id=1, source_target_pairs={{0,6},{4,2},{11,9},{15,13},{18,16},{22,20},{25,31},{29,27}} | collective-permute-start | bytes 786440 | tf_op jit(solution)/shard_map/ppermute | solution.py:73
  28.4 19.1 %collective-permute-start.10 = (f32[256,256]{1,0:T(8,128)S(1)}, f32[256,256]{1,0:T(8,128)S(1)}, u32[]{:S(2)}, u32[]{:S(2)}) collective-permute-start(f32[256,256]{1,0:T(8,128)S(1)} %shard_map.49), channel_id=1, source_target_pairs={{0,4},{4,0},{11,15},{15,11},{18,22},{22,18},{25,29},{29,25}} | collective-permute-start | bytes 786440 | tf_op jit(solution)/shard_map/ppermute | solution.py:73
  29.1 24.4 %collective-permute-start.15 = (f32[512,256]{1,0:T(8,128)S(1)}, f32[512,256]{1,0:T(8,128)S(1)}, u32[]{:S(2)}, u32[]{:S(2)}) collective-permute-start(f32[512,256]{1,0:T(8,128)S(1)} %pad_maximum_fusion.refs_0_), channel_id=1, source_target_pairs={{1,25},{3,27},{5,29},{7,31},{8,16},{10,18},{12,20},{14,22},{19,11}... | collective-permute-start | bytes 1572872 | tf_op jit(solution)/shard_map/ppermute | solution.py:73
  47.6 9.9 %collective-permute-start.13 = (f32[512,256]{1,0:T(8,128)S(1)}, f32[512,256]{1,0:T(8,128)S(1)}, u32[]{:S(2)}, u32[]{:S(2)}) collective-permute-start(f32[512,256]{1,0:T(8,128)S(1)} %pad_maximum_fusion.1.refs_2_), channel_id=1, source_target_pairs={{0,1},{2,3},{4,5},{6,7},{9,8},{11,10},{13,12},{15,14},{16,17},{18,... | collective-permute-start | bytes 1572872 | tf_op jit(solution)/shard_map/ppermute | solution.py:73
  48.9 10.0 %collective-permute-start.14 = (f32[512,256]{1,0:T(8,128)S(1)}, f32[512,256]{1,0:T(8,128)S(1)}, u32[]{:S(2)}, u32[]{:S(2)}) collective-permute-start(f32[512,256]{1,0:T(8,128)S(1)} %get-tuple-element.28), channel_id=1, source_target_pairs={{15,23},{22,30},{23,31}} | collective-permute-start | bytes 1572872 | tf_op jit(solution)/shard_map/ppermute | solution.py:73
  53.5 9.9 %collective-permute-start.16 = (f32[512,256]{1,0:T(8,128)S(1)}, f32[512,256]{1,0:T(8,128)S(1)}, u32[]{:S(2)}, u32[]{:S(2)}) collective-permute-start(f32[512,256]{1,0:T(8,128)S(1)} %collective-permute-done.15.refs_0_), channel_id=1, source_target_pairs={{2,3},{4,5},{6,7},{11,10},{13,12},{15,14},{16,17},{18,19},{20,21},... | collective-permute-start | bytes 1572872 | tf_op jit(solution)/shard_map/ppermute | solution.py:73
  57.6 9.9 %collective-permute-start.17 = (f32[512,256]{1,0:T(8,128)S(1)}, f32[512,256]{1,0:T(8,128)S(1)}, u32[]{:S(2)}, u32[]{:S(2)}) collective-permute-start(f32[512,256]{1,0:T(8,128)S(1)} %add.19), channel_id=1, source_target_pairs={{9,25},{10,26},{11,27},{12,28},{13,29},{14,30},{15,31},{27,11},{28... | collective-permute-start | bytes 1572872 | tf_op jit(solution)/shard_map/ppermute | solution.py:73
